TPU v7x, 32 devices: a whole 2x2x4 slice. The times are simulated.
32 devices in a mesh: rows: 8 (over y, x, core), cols: 4 (over z).
Axes of the slice: x: 2, y: 2, z: 4, core: 2. Of those that a mesh axis runs over, the one named last changes fastest.
Arguments:
- unary: float32 [21, 128, 512], P(None, 'rows', 'cols'), may hold values from -8 to 300
- features: bfloat16 [64, 128, 512], P(None, 'rows', 'cols'), may hold values from -9 to 9
- compat: float32 [21, 21], replicated, may hold values from -6 to 6
- grad_output: float32 [21, 128, 512], P(None, 'rows', 'cols'), may hold values from -6 to 6
Outputs:
- unary_grad: float32 [21, 128, 512], P(None, 'rows', 'cols')
- feature_grad: float32 [64, 128, 512], P(None, 'rows', 'cols')
- compat_grad: float32 [21, 21], replicated
All inputs are finite; a program needn't handle non-finite values.
Results may differ from a plain program's by a relative error of at most 0.0003.
Values may be sent and summed in bfloat16 or wider, within the bound.
No kernel may reach another device: no remote copies, remote signals or barrier semaphores. Data moves between devices by JAX's collectives and lax.ppermute only.
A program may use at most 128 MiB of HBM per device.

v0:
```python
import math

import jax
import jax.numpy as jnp
from jax import lax
from jax.sharding import PartitionSpec as P

ITERS = 2


THETA_PIXELS = 3.0
WINDOW_OFFSETS = [
    (row_step, col_step)
    for row_step in range(-3, 4)
    for col_step in range(-3, 4)
    if row_step != 0 or col_step != 0
]


def with_halo(block, sides, width):
    for axis, dim in sides:
        count = lax.axis_size(axis)
        forward = [(i, i + 1) for i in range(count - 1)]
        backward = [(target, source) for source, target in forward]
        low = lax.ppermute(
            lax.slice_in_dim(block, block.shape[dim] - width, None, axis=dim), axis, forward
        )
        high = lax.ppermute(lax.slice_in_dim(block, 0, width, axis=dim), axis, backward)
        block = jnp.concatenate([low, block, high], axis=dim)
    return block


def spatial_weight(row_step, col_step):
    return math.exp(
        -(row_step * row_step + col_step * col_step) / (2.0 * THETA_PIXELS * THETA_PIXELS)
    )


def shifted_view(padded, row_step, col_step, height, width_cells):
    return padded[
        :, 3 + row_step : 3 + row_step + height, 3 + col_step : 3 + col_step + width_cells
    ]


def affinity(padded_features):
    height = padded_features.shape[1] - 6
    width_cells = padded_features.shape[2] - 6
    center = shifted_view(padded_features, 0, 0, height, width_cells).astype(jnp.float32)
    factor = 1.0 / (2.0 * padded_features.shape[0])
    layers = []
    for row_step, col_step in WINDOW_OFFSETS:
        shifted = shifted_view(padded_features, row_step, col_step, height, width_cells).astype(
            jnp.float32
        )
        distance = jnp.sum((shifted - center) * (shifted - center), axis=0)
        layers.append(spatial_weight(row_step, col_step) * jnp.exp(-distance * factor))
    return jnp.stack(layers)


def message(kernel, padded):
    height = kernel.shape[1]
    width_cells = kernel.shape[2]
    total = jnp.zeros((padded.shape[0], height, width_cells), jnp.float32)
    for number, (row_step, col_step) in enumerate(WINDOW_OFFSETS):
        total = total + kernel[number][None] * shifted_view(
            padded, row_step, col_step, height, width_cells
        )
    return total


def pair_terms(grad_padded, prob_padded):
    height = grad_padded.shape[1] - 6
    width_cells = grad_padded.shape[2] - 6
    grad_center = shifted_view(grad_padded, 0, 0, height, width_cells)
    prob_center = shifted_view(prob_padded, 0, 0, height, width_cells)
    layers = []
    for row_step, col_step in WINDOW_OFFSETS:
        prob_shift = shifted_view(prob_padded, row_step, col_step, height, width_cells)
        grad_shift = shifted_view(grad_padded, row_step, col_step, height, width_cells)
        layers.append(jnp.sum(grad_center * prob_shift + grad_shift * prob_center, axis=0))
    return jnp.stack(layers)


def feature_term(coefs, kernel, padded_features):
    height = kernel.shape[1]
    width_cells = kernel.shape[2]
    center = shifted_view(padded_features, 0, 0, height, width_cells).astype(jnp.float32)
    factor = 1.0 / padded_features.shape[0]
    total = jnp.zeros(center.shape, jnp.float32)
    for number, (row_step, col_step) in enumerate(WINDOW_OFFSETS):
        shifted = shifted_view(padded_features, row_step, col_step, height, width_cells).astype(
            jnp.float32
        )
        weight_map = coefs[number] * kernel[number] * factor
        total = total + weight_map[None] * (shifted - center)
    return total


def mix(compat, values):
    return jnp.einsum("cd,dhw->chw", compat, values, precision=lax.Precision.HIGHEST)


def mix_back(compat, values):
    return jnp.einsum("cd,chw->dhw", compat, values, precision=lax.Precision.HIGHEST)


def outer_sum(left, right):
    return jnp.einsum("chw,dhw->cd", left, right, precision=lax.Precision.HIGHEST)


def softmax_grad(prob, cotangent):
    return prob * (cotangent - jnp.sum(cotangent * prob, axis=0, keepdims=True))


def on_device(unary, features, compat, grad_output):
    height = unary.shape[1]
    width_cells = unary.shape[2]
    total_pixels = height * lax.axis_size("rows") * width_cells * lax.axis_size("cols")
    reach = 0
    feat_wide = with_halo(features, (("rows", 1), ("cols", 2)), 3)
    cotangent = grad_output
    start_prob = jax.nn.softmax(unary, axis=0)
    kern_store = affinity(feat_wide)

    def kernel_at():
        return kern_store

    prob_list = [start_prob]
    pad_list = [reach]
    wide_list = []
    message_list = []
    for step in range(ITERS):
        current = prob_list[-1]
        prob_wide = with_halo(current, (("rows", 1), ("cols", 2)), 3)
        wide_pad = 3
        wide_list.append((prob_wide, wide_pad))
        out_pad = wide_pad - 3
        message_out = message(kernel_at(), prob_wide)
        message_list.append(message_out)
        logits = unary - mix(compat, message_out)
        next_prob = jax.nn.softmax(logits, axis=0)
        prob_list.append(next_prob)
        pad_list.append(out_pad)
    unary_sum = jnp.zeros(unary.shape, jnp.float32)
    compat_sum = jnp.zeros(compat.shape, jnp.float32)
    coefs = jnp.zeros((len(WINDOW_OFFSETS), height, width_cells), jnp.float32)
    for step in reversed(range(ITERS)):
        later_prob = prob_list[step + 1]
        logit_grad = softmax_grad(later_prob, cotangent)
        unary_sum = unary_sum + logit_grad
        compat_sum = compat_sum - outer_sum(logit_grad, message_list[step])
        msg_grad = -mix_back(compat, logit_grad)
        grad_wide = with_halo(msg_grad, (("rows", 1), ("cols", 2)), 3)
        cotangent = message(kernel_at(), grad_wide)
        prob_wide, wide_pad = wide_list[step]
        coefs = coefs + pair_terms(grad_wide, prob_wide)
    unary_grad = unary_sum + softmax_grad(prob_list[0], cotangent)
    feature_grad = feature_term(coefs, kernel_at(), feat_wide)
    compat_grad = lax.psum(compat_sum, ("rows", "cols")) / math.sqrt(total_pixels)
    return (unary_grad, feature_grad, compat_grad)


def solution(mesh):
    placed = (P(None, "rows", "cols"), P(None, "rows", "cols"), P(), P(None, "rows", "cols"))
    return jax.shard_map(
        on_device,
        mesh=mesh,
        in_specs=placed,
        out_specs=(P(None, "rows", "cols"), P(None, "rows", "cols"), P()),
        check_vma=False,
    )
```

profile of v0, /device:TPU:4, one launch (start us, length us, event | category | flops | bytes accessed | tf_op | source)
XLA Modules:
  0.0 244.2 jit_solution(10473670717247180716)
XLA Ops:
  1.6 1.0 fusion.39
  2.7 1.0 fusion.38
  3.7 1.9 collective-permute-start.3
  5.6 4.5 %collective-permute-start.4 = (f32[21,3,128]{2,0,1:T(8,128)S(1)}, f32[21,3,128]{2,0,1:T(8,128)S(1)}, u32[]{:S(2)}, u32[]{:S(2)}) collective-permute-start(f32[21,3,128]{2,0,1:T(8,128)S(1)} %get-tuple-element.239), channel_id=1, source_target_pairs={{4,0},{8,4},{12,8},{16,12},{20,16},{24,20},{28,24},{5,1},{9,5},{13... | collective-permute-start | bytes 96776 | tf_op jit(solution)/shard_map/ppermute | solution.py:28
  10.2 1.9 collective-permute-start
  12.2 4.5 %collective-permute-start.1 = (bf16[64,3,128]{2,1,0:T(4,128)(2,1)S(1)}, bf16[64,3,128]{2,1,0:T(4,128)(2,1)S(1)}, u32[]{:S(2)}, u32[]{:S(2)}) collective-permute-start(bf16[64,3,128]{2,1,0:T(4,128)(2,1)S(1)} %get-tuple-element.230), channel_id=1, source_target_pairs={{4,0},{8,4},{12,8},{16,12},{20,16},{24,20},{28,24},{5,1},{9,5},{13... | collective-permute-start | bytes 147464 | tf_op jit(solution)/shard_map/ppermute | solution.py:28
  16.9 3.5 %collective-permute-start.5 = (f32[21,22,3]{2,0,1:T(8,128)S(1)}, f32[21,22,3]{2,0,1:T(8,128)S(1)}, u32[]{:S(2)}, u32[]{:S(2)}) collective-permute-start(f32[21,22,3]{2,0,1:T(8,128)S(1)} %get-tuple-element.227), channel_id=1, source_target_pairs={{0,1},{1,2},{2,3},{4,5},{5,6},{6,7},{8,9},{9,10},{10,11},{12,13},{... | collective-permute-start | bytes 16640 | tf_op jit(solution)/shard_map/ppermute | solution.py:25
  20.4 1.3 collective-permute-start.7
  21.7 2.6 %collective-permute-done.5 = f32[21,22,3]{2,0,1:T(8,128)S(1)} collective-permute-done((f32[21,22,3]{2,0,1:T(8,128)S(1)}, f32[21,22,3]{2,0,1:T(8,128)S(1)}, u32[]{:S(2)}, u32[]{:S(2)}) %collective-permute-start.5) | collective-permute-done | bytes 5576 | tf_op jit(solution)/shard_map/ppermute | solution.py:25
  24.4 4.4 %collective-permute-done.7 = f32[21,22,3]{2,0,1:T(8,128)S(1)} collective-permute-done((f32[21,22,3]{2,0,1:T(8,128)S(1)}, f32[21,22,3]{2,0,1:T(8,128)S(1)}, u32[]{:S(2)}, u32[]{:S(2)}) %collective-permute-start.7) | collective-permute-done | bytes 5576 | tf_op jit(solution)/shard_map/ppermute | solution.py:28
  29.4 1.3 collective-permute-start.6
  30.7 4.6 %collective-permute-start.2 = (bf16[64,22,3]{2,1,0:T(8,128)(2,1)S(1)}, bf16[64,22,3]{2,1,0:T(8,128)(2,1)S(1)}, u32[]{:S(2)}, u32[]{:S(2)}) collective-permute-start(bf16[64,22,3]{2,1,0:T(8,128)(2,1)S(1)} %get-tuple-element.212), channel_id=1, source_target_pairs={{0,1},{1,2},{2,3},{4,5},{5,6},{6,7},{8,9},{9,10},{10,11},{12,13},{... | collective-permute-start | bytes 25352 | tf_op jit(solution)/shard_map/ppermute | solution.py:25
  35.3 3.7 %collective-permute-done.6 = bf16[64,22,3]{2,1,0:T(8,128)(2,1)S(1)} collective-permute-done((bf16[64,22,3]{2,1,0:T(8,128)(2,1)S(1)}, bf16[64,22,3]{2,1,0:T(8,128)(2,1)S(1)}, u32[]{:S(2)}, u32[]{:S(2)}) %collective-permute-start.6) | collective-permute-done | bytes 8480 | tf_op jit(solution)/shard_map/ppermute | solution.py:28
  39.1 1.5 collective-permute-done.2
  40.5 1.1 pad_maximum_fusion
  41.7 2.4 multiply_reduce_fusion.43
  44.2 2.9 %multiply_reduce_fusion.47 = (f32[16,128]{1,0:T(8,128)S(1)}, f32[16,128]{1,0:T(8,128)}, f32[16,128]{1,0:T(8,128)}, f32[16,128]{1,0:T(8,128)}, f32[16,128]{1,0:T(...) fusion(bf16[64,16,128]{2,1,0:T(8,128)(2,1)S(1)} %copy-done.5, ...), kind=kLoop, calls=%fused_computation.128 | loop fusion | flops 9531392 | bytes 5128192 | tf_op jit(solution)/shard_map/reduce_sum | solution.py:55
  47.1 2.6 %multiply_reduce_fusion.46 = (f32[16,128]{1,0:T(8,128)}, f32[16,128]{1,0:T(8,128)}, f32[16,128]{1,0:T(8,128)}, f32[16,128]{1,0:T(8,128)}, f32[16,128]{1,0:T(8,12...) fusion(bf16[64,16,128]{2,1,0:T(8,128)(2,1)S(1)} %copy-done.5, ...), kind=kLoop, calls=%fused_computation.127 | loop fusion | flops 7577600 | bytes 2768896 | tf_op jit(solution)/shard_map/reduce_sum | solution.py:55
  57.7 1.3 exponential_multiply_fusion.25
  59.0 1.3 exponential_multiply_fusion.20
  60.3 1.3 exponential_multiply_fusion.18
  61.7 1.3 exponential_multiply_fusion.12
  63.0 1.3 exponential_multiply_fusion.6
  64.3 2.7 %multiply_add_fusion.4 = f32[21,16,128]{2,0,1:T(8,128)S(1)} fusion(f32[21,22,131]{2,0,1:T(8,128)S(1)} %get-tuple-element.226, f32[21,22,131]{2,0,1:T(8,128)S(1)} %get-tuple-element.225, f32[21,16,128]{2,0,1:T(8,128)S(1)} %fusion.38, f32[21,3,128]{2,0,1:T(8,128)S(1)} %collective-permute-done.3, f32[21,3,128]{2,0,1:T(8,128)S(1)} %collective-permute-done.4, ...), kind=kLoop, calls=%fused_computation.402 | loop fusion | flops 4343808 | bytes 8027136 | tf_op jit(solution)/shard_map/add | solution.py:65
  68.1 1.9 collective-permute-start.8
  70.0 4.7 %collective-permute-start.9 = (f32[21,3,128]{2,0,1:T(8,128)S(1)}, f32[21,3,128]{2,0,1:T(8,128)S(1)}, u32[]{:S(2)}, u32[]{:S(2)}) collective-permute-start(f32[21,3,128]{2,0,1:T(8,128)S(1)} %get-tuple-element.237), channel_id=1, source_target_pairs={{4,0},{8,4},{12,8},{16,12},{20,16},{24,20},{28,24},{5,1},{9,5},{13... | collective-permute-start | bytes 96776 | tf_op jit(solution)/shard_map/ppermute | solution.py:28
  74.8 1.6 collective-permute-done.9
  76.6 4.4 %collective-permute-start.10 = (f32[21,22,3]{2,0,1:T(8,128)S(1)}, f32[21,22,3]{2,0,1:T(8,128)S(1)}, u32[]{:S(2)}, u32[]{:S(2)}) collective-permute-start(f32[21,22,3]{2,0,1:T(8,128)S(1)} %get-tuple-element.223), channel_id=1, source_target_pairs={{0,1},{1,2},{2,3},{4,5},{5,6},{6,7},{8,9},{9,10},{10,11},{12,13},{... | collective-permute-start | bytes 16640 | tf_op jit(solution)/shard_map/ppermute | solution.py:25
  81.0 1.5 collective-permute-start.11
  82.4 4.0 %collective-permute-done.10 = f32[21,22,3]{2,0,1:T(8,128)S(1)} collective-permute-done((f32[21,22,3]{2,0,1:T(8,128)S(1)}, f32[21,22,3]{2,0,1:T(8,128)S(1)}, u32[]{:S(2)}, u32[]{:S(2)}) %collective-permute-start.10) | collective-permute-done | bytes 5576 | tf_op jit(solution)/shard_map/ppermute | solution.py:25
  86.5 4.1 %collective-permute-done.11 = f32[21,22,3]{2,0,1:T(8,128)S(1)} collective-permute-done((f32[21,22,3]{2,0,1:T(8,128)S(1)}, f32[21,22,3]{2,0,1:T(8,128)S(1)}, u32[]{:S(2)}, u32[]{:S(2)}) %collective-permute-start.11) | collective-permute-done | bytes 5576 | tf_op jit(solution)/shard_map/ppermute | solution.py:28
  90.8 2.8 %multiply_add_fusion.3 = f32[21,16,128]{2,0,1:T(8,128)S(1)} fusion(f32[21,22,131]{2,0,1:T(8,128)S(1)} %get-tuple-element.222, f32[21,22,131]{2,0,1:T(8,128)S(1)} %get-tuple-element.221, f32[21,16,128]{2,0,1:T(8,128)S(1)} %broadcast_divide_fusion.1, f32[21,3,128]{2,0,1:T(8,128)S(1)} %collective-permute-done.8, f32[21,3,128]{2,0,1:T(8,128)S(1)} %collective-permute-done.9, ...), kind=kLoop, calls=%fused_computation.401 | loop fusion | flops 4343808 | bytes 8027136 | tf_op jit(solution)/shard_map/add | solution.py:65
  94.0 1.2 fusion.154
  95.2 1.4 fusion.19
  96.6 1.1 fusion.11
  97.7 1.9 collective-permute-start.12
  99.6 4.5 %collective-permute-start.13 = (f32[21,3,128]{2,0,1:T(8,128)S(1)}, f32[21,3,128]{2,0,1:T(8,128)S(1)}, u32[]{:S(2)}, u32[]{:S(2)}) collective-permute-start(f32[21,3,128]{2,0,1:T(8,128)S(1)} %get-tuple-element.235), channel_id=1, source_target_pairs={{4,0},{8,4},{12,8},{16,12},{20,16},{24,20},{28,24},{5,1},{9,5},{13... | collective-permute-start | bytes 96776 | tf_op jit(solution)/shard_map/ppermute | solution.py:28
  104.2 1.6 collective-permute-done.13
  106.0 3.5 %collective-permute-start.14 = (f32[21,22,3]{2,0,1:T(8,128)S(1)}, f32[21,22,3]{2,0,1:T(8,128)S(1)}, u32[]{:S(2)}, u32[]{:S(2)}) collective-permute-start(f32[21,22,3]{2,0,1:T(8,128)S(1)} %get-tuple-element.219), channel_id=1, source_target_pairs={{0,1},{1,2},{2,3},{4,5},{5,6},{6,7},{8,9},{9,10},{10,11},{12,13},{... | collective-permute-start | bytes 16640 | tf_op jit(solution)/shard_map/ppermute | solution.py:25
  109.4 1.3 collective-permute-start.15
  111.5 1.9 collective-permute-done.14
  113.4 4.4 %collective-permute-done.15 = f32[21,22,3]{2,0,1:T(8,128)S(1)} collective-permute-done((f32[21,22,3]{2,0,1:T(8,128)S(1)}, f32[21,22,3]{2,0,1:T(8,128)S(1)}, u32[]{:S(2)}, u32[]{:S(2)}) %collective-permute-start.15) | collective-permute-done | bytes 5576 | tf_op jit(solution)/shard_map/ppermute | solution.py:28
  118.0 1.2 add_reduce_fusion.83
  119.2 1.5 add_reduce_fusion.64
  120.7 1.0 add_reduce_fusion.87
  121.8 1.3 add_reduce_fusion.52
  123.1 1.2 add_reduce_fusion.68
  124.7 4.4 %add_reduce_fusion.48 = (f32[16,128]{1,0:T(8,128)}, f32[16,128]{1,0:T(8,128)}, f32[16,128]{1,0:T(8,128)}, f32[16,128]{1,0:T(8,128)}, f32[16,128]{1,0:T(8,128)}, ...) fusion(f32[21,16,128]{2,0,1:T(8,128)S(1)} %fusion.11, ...), kind=kLoop, calls=%fused_computation.349 | loop fusion | flops 5830656 | bytes 9657344 | tf_op jit(solution)/shard_map/reduce_sum | solution.py:80
  131.2 1.1 fusion.15
  132.3 43.0 %psum.7 = f32[21,21]{1,0:T(8,128)S(1)} all-reduce(f32[21,21]{1,0:T(8,128)S(1)} %fusion.15), channel_id=1, replica_groups=mesh['rows'=8,'cols'=4] {'rows','cols'}, use_global_device_ids=true, to_apply=%region_153.0 | all-reduce | flops 441 | bytes 3528 | tf_op jit(solution)/shard_map/psum | solution.py:159
  176.0 1.9 collective-permute-start.16
  177.9 4.5 %collective-permute-start.17 = (f32[21,3,128]{2,0,1:T(8,128)S(1)}, f32[21,3,128]{2,0,1:T(8,128)S(1)}, u32[]{:S(2)}, u32[]{:S(2)}) collective-permute-start(f32[21,3,128]{2,0,1:T(8,128)S(1)} %get-tuple-element.233), channel_id=1, source_target_pairs={{4,0},{8,4},{12,8},{16,12},{20,16},{24,20},{28,24},{5,1},{9,5},{13... | collective-permute-start | bytes 96776 | tf_op jit(solution)/shard_map/ppermute | solution.py:28
  194.4 2.3 collective-permute-start.18
  196.7 1.5 collective-permute-start.19
  198.6 3.5 %collective-permute-done.18 = f32[21,22,3]{2,0,1:T(8,128)S(1)} collective-permute-done((f32[21,22,3]{2,0,1:T(8,128)S(1)}, f32[21,22,3]{2,0,1:T(8,128)S(1)}, u32[]{:S(2)}, u32[]{:S(2)}) %collective-permute-start.18) | collective-permute-done | bytes 5576 | tf_op jit(solution)/shard_map/ppermute | solution.py:25
  202.1 4.1 %collective-permute-done.19 = f32[21,22,3]{2,0,1:T(8,128)S(1)} collective-permute-done((f32[21,22,3]{2,0,1:T(8,128)S(1)}, f32[21,22,3]{2,0,1:T(8,128)S(1)}, u32[]{:S(2)}, u32[]{:S(2)}) %collective-permute-start.19) | collective-permute-done | bytes 5576 | tf_op jit(solution)/shard_map/ppermute | solution.py:28
  211.8 1.4 fusion.129
  213.3 1.4 fusion.131
  214.7 1.4 fusion.133
  216.2 1.4 fusion.135
  217.7 1.4 fusion.137
  219.1 1.5 fusion.139
  220.9 13.9 %fusion.7 = f32[21,16,128]{2,0,1:T(8,128)S(1)} fusion(f32[21,16,128]{2,0,1:T(8,128)S(1)} %copy-done.10, f32[16,128]{1,0:T(8,128)} %fusion.19, f32[21,16,128]{2,1,0:T(8,128)} %param.7, f32[21,16,128]{2,0,1:T(8,128)} %copy-done.11, f32[16,128]{1,0:T(8,128)} %get-tuple-element.242, f32[16,128]{1,0:T(8,128)S(1)} %copy-done.13, f32[16,128]{1,0:T(8,128)S(1)} %reduce_max.27, ...), kind=kOutput, calls=%fused_computation.55 | output fusion | flops 9205780 | bytes 18972672 | tf_op jit(solution)/shard_map/sub | solution.py:112
  235.9 8.3 %multiply_add_fusion = f32[64,16,128]{2,1,0:T(8,128)} fusion(bf16[64,16,128]{2,1,0:T(8,128)(2,1)S(1)} %copy-done.6, bf16[64,3,128]{2,1,0:T(4,128)(2,1)S(1)} %collective-permute-done, f32[16,128]{1,0:T(8,128)} %get-tuple-element.162, f32[16,128]{1,0:T(8,128)} %get-tuple-element.163, f32[16,128]{1,0:T(8,128)} %get-tuple-element.164, ...), kind=kLoop, calls=%fused_computation.80 | loop fusion | flops 26345472 | bytes 13025280 | tf_op jit(solution)/shard_map/add | solution.py:95
  (476 shorter events, 32.4 us)
Async XLA Ops:
  0.6 66.4 %copy-start = (f32[21,21]{1,0:T(8,128)S(1)}, f32[21,21]{1,0:T(8,128)}, u32[]{:S(2)}) copy-start(f32[21,21]{1,0:T(8,128)} %param.6) | copy-start | bytes 5296
  3.7 13.0 %collective-permute-start.3 = (f32[21,3,128]{2,0,1:T(8,128)S(1)}, f32[21,3,128]{2,0,1:T(8,128)S(1)}, u32[]{:S(2)}, u32[]{:S(2)}) collective-permute-start(f32[21,3,128]{2,0,1:T(8,128)S(1)} %get-tuple-element.238), channel_id=1, source_target_pairs={{0,4},{4,8},{8,12},{12,16},{16,20},{20,24},{24,28},{1,5},{5,9},{9,... | collective-permute-start | bytes 96776 | tf_op jit(solution)/shard_map/ppermute | solution.py:25
  5.6 11.1 %collective-permute-start.4 = (f32[21,3,128]{2,0,1:T(8,128)S(1)}, f32[21,3,128]{2,0,1:T(8,128)S(1)}, u32[]{:S(2)}, u32[]{:S(2)}) collective-permute-start(f32[21,3,128]{2,0,1:T(8,128)S(1)} %get-tuple-element.239), channel_id=1, source_target_pairs={{4,0},{8,4},{12,8},{16,12},{20,16},{24,20},{28,24},{5,1},{9,5},{13... | collective-permute-start | bytes 96776 | tf_op jit(solution)/shard_map/ppermute | solution.py:28
  10.2 18.8 %collective-permute-start = (bf16[64,3,128]{2,1,0:T(4,128)(2,1)S(1)}, bf16[64,3,128]{2,1,0:T(4,128)(2,1)S(1)}, u32[]{:S(2)}, u32[]{:S(2)}) collective-permute-start(bf16[64,3,128]{2,1,0:T(4,128)(2,1)S(1)} %get-tuple-element.229), channel_id=1, source_target_pairs={{0,4},{4,8},{8,12},{12,16},{16,20},{20,24},{24,28},{1,5},{5,9},{9,... | collective-permute-start | bytes 147464 | tf_op jit(solution)/shard_map/ppermute | solution.py:25
  12.2 16.8 %collective-permute-start.1 = (bf16[64,3,128]{2,1,0:T(4,128)(2,1)S(1)}, bf16[64,3,128]{2,1,0:T(4,128)(2,1)S(1)}, u32[]{:S(2)}, u32[]{:S(2)}) collective-permute-start(bf16[64,3,128]{2,1,0:T(4,128)(2,1)S(1)} %get-tuple-element.230), channel_id=1, source_target_pairs={{4,0},{8,4},{12,8},{16,12},{20,16},{24,20},{28,24},{5,1},{9,5},{13... | collective-permute-start | bytes 147464 | tf_op jit(solution)/shard_map/ppermute | solution.py:28
  16.9 7.5 %collective-permute-start.5 = (f32[21,22,3]{2,0,1:T(8,128)S(1)}, f32[21,22,3]{2,0,1:T(8,128)S(1)}, u32[]{:S(2)}, u32[]{:S(2)}) collective-permute-start(f32[21,22,3]{2,0,1:T(8,128)S(1)} %get-tuple-element.227), channel_id=1, source_target_pairs={{0,1},{1,2},{2,3},{4,5},{5,6},{6,7},{8,9},{9,10},{10,11},{12,13},{... | collective-permute-start | bytes 16640 | tf_op jit(solution)/shard_map/ppermute | solution.py:25
  20.4 8.4 %collective-permute-start.7 = (f32[21,22,3]{2,0,1:T(8,128)S(1)}, f32[21,22,3]{2,0,1:T(8,128)S(1)}, u32[]{:S(2)}, u32[]{:S(2)}) collective-permute-start(f32[21,22,3]{2,0,1:T(8,128)S(1)} %get-tuple-element.228), channel_id=1, source_target_pairs={{1,0},{2,1},{3,2},{5,4},{6,5},{7,6},{9,8},{10,9},{11,10},{13,12},{... | collective-permute-start | bytes 16640 | tf_op jit(solution)/shard_map/ppermute | solution.py:28
  29.4 9.7 %collective-permute-start.6 = (bf16[64,22,3]{2,1,0:T(8,128)(2,1)S(1)}, bf16[64,22,3]{2,1,0:T(8,128)(2,1)S(1)}, u32[]{:S(2)}, u32[]{:S(2)}) collective-permute-start(bf16[64,22,3]{2,1,0:T(8,128)(2,1)S(1)} %get-tuple-element.211), channel_id=1, source_target_pairs={{1,0},{2,1},{3,2},{5,4},{6,5},{7,6},{9,8},{10,9},{11,10},{13,12},{... | collective-permute-start | bytes 25352 | tf_op jit(solution)/shard_map/ppermute | solution.py:28
  30.7 9.8 %collective-permute-start.2 = (bf16[64,22,3]{2,1,0:T(8,128)(2,1)S(1)}, bf16[64,22,3]{2,1,0:T(8,128)(2,1)S(1)}, u32[]{:S(2)}, u32[]{:S(2)}) collective-permute-start(bf16[64,22,3]{2,1,0:T(8,128)(2,1)S(1)} %get-tuple-element.212), channel_id=1, source_target_pairs={{0,1},{1,2},{2,3},{4,5},{5,6},{6,7},{8,9},{9,10},{10,11},{12,13},{... | collective-permute-start | bytes 25352 | tf_op jit(solution)/shard_map/ppermute | solution.py:25
  50.4 73.9 %copy-start.19 = (f32[16,128]{1,0:T(8,128)}, f32[16,128]{1,0:T(8,128)S(1)}, u32[]{:S(2)}) copy-start(f32[16,128]{1,0:T(8,128)S(1)} %get-tuple-element.254) | copy-start | bytes 24580
  50.4 73.9 %copy-start.21 = (f32[16,128]{1,0:T(8,128)}, f32[16,128]{1,0:T(8,128)S(1)}, u32[]{:S(2)}) copy-start(f32[16,128]{1,0:T(8,128)S(1)} %get-tuple-element.255) | copy-start | bytes 24580
  51.2 73.1 %copy-start.23 = (f32[16,128]{1,0:T(8,128)}, f32[16,128]{1,0:T(8,128)S(1)}, u32[]{:S(2)}) copy-start(f32[16,128]{1,0:T(8,128)S(1)} %get-tuple-element.248) | copy-start | bytes 24580
  51.2 73.1 %copy-start.25 = (f32[16,128]{1,0:T(8,128)}, f32[16,128]{1,0:T(8,128)S(1)}, u32[]{:S(2)}) copy-start(f32[16,128]{1,0:T(8,128)S(1)} %get-tuple-element.249) | copy-start | bytes 24580
  51.9 72.4 %copy-start.27 = (f32[16,128]{1,0:T(8,128)}, f32[16,128]{1,0:T(8,128)S(1)}, u32[]{:S(2)}) copy-start(f32[16,128]{1,0:T(8,128)S(1)} %get-tuple-element.252) | copy-start | bytes 24580
  51.9 72.4 %copy-start.29 = (f32[16,128]{1,0:T(8,128)}, f32[16,128]{1,0:T(8,128)S(1)}, u32[]{:S(2)}) copy-start(f32[16,128]{1,0:T(8,128)S(1)} %get-tuple-element.253) | copy-start | bytes 24580
  52.7 71.7 %copy-start.31 = (f32[16,128]{1,0:T(8,128)}, f32[16,128]{1,0:T(8,128)S(1)}, u32[]{:S(2)}) copy-start(f32[16,128]{1,0:T(8,128)S(1)} %get-tuple-element.246) | copy-start | bytes 24580
  52.7 71.7 %copy-start.32 = (f32[16,128]{1,0:T(8,128)}, f32[16,128]{1,0:T(8,128)S(1)}, u32[]{:S(2)}) copy-start(f32[16,128]{1,0:T(8,128)S(1)} %get-tuple-element.247) | copy-start | bytes 24580
  53.4 71.0 %copy-start.33 = (f32[16,128]{1,0:T(8,128)}, f32[16,128]{1,0:T(8,128)S(1)}, u32[]{:S(2)}) copy-start(f32[16,128]{1,0:T(8,128)S(1)} %get-tuple-element.250) | copy-start | bytes 24580
  53.4 71.0 %copy-start.34 = (f32[16,128]{1,0:T(8,128)}, f32[16,128]{1,0:T(8,128)S(1)}, u32[]{:S(2)}) copy-start(f32[16,128]{1,0:T(8,128)S(1)} %get-tuple-element.251) | copy-start | bytes 24580
  54.2 70.2 %copy-start.35 = (f32[16,128]{1,0:T(8,128)}, f32[16,128]{1,0:T(8,128)S(1)}, u32[]{:S(2)}) copy-start(f32[16,128]{1,0:T(8,128)S(1)} %get-tuple-element.244) | copy-start | bytes 24580
  54.2 70.2 %copy-start.36 = (f32[16,128]{1,0:T(8,128)}, f32[16,128]{1,0:T(8,128)S(1)}, u32[]{:S(2)}) copy-start(f32[16,128]{1,0:T(8,128)S(1)} %get-tuple-element.245) | copy-start | bytes 24580
  54.2 70.2 %copy-start.37 = (f32[16,128]{1,0:T(8,128)}, f32[16,128]{1,0:T(8,128)S(1)}, u32[]{:S(2)}) copy-start(f32[16,128]{1,0:T(8,128)S(1)} %get-tuple-element.290) | copy-start | bytes 24580
  54.2 70.2 %copy-start.38 = (f32[16,128]{1,0:T(8,128)}, f32[16,128]{1,0:T(8,128)S(1)}, u32[]{:S(2)}) copy-start(f32[16,128]{1,0:T(8,128)S(1)} %get-tuple-element.291) | copy-start | bytes 24580
  54.3 70.1 %copy-start.39 = (f32[16,128]{1,0:T(8,128)}, f32[16,128]{1,0:T(8,128)S(1)}, u32[]{:S(2)}) copy-start(f32[16,128]{1,0:T(8,128)S(1)} %get-tuple-element.288) | copy-start | bytes 24580
  54.3 70.1 %copy-start.40 = (f32[16,128]{1,0:T(8,128)}, f32[16,128]{1,0:T(8,128)S(1)}, u32[]{:S(2)}) copy-start(f32[16,128]{1,0:T(8,128)S(1)} %get-tuple-element.289) | copy-start | bytes 24580
  54.3 70.1 %copy-start.41 = (f32[16,128]{1,0:T(8,128)}, f32[16,128]{1,0:T(8,128)S(1)}, u32[]{:S(2)}) copy-start(f32[16,128]{1,0:T(8,128)S(1)} %get-tuple-element.286) | copy-start | bytes 24580
  54.3 70.1 %copy-start.42 = (f32[16,128]{1,0:T(8,128)}, f32[16,128]{1,0:T(8,128)S(1)}, u32[]{:S(2)}) copy-start(f32[16,128]{1,0:T(8,128)S(1)} %get-tuple-element.287) | copy-start | bytes 24580
  54.4 70.1 %copy-start.43 = (f32[16,128]{1,0:T(8,128)}, f32[16,128]{1,0:T(8,128)S(1)}, u32[]{:S(2)}) copy-start(f32[16,128]{1,0:T(8,128)S(1)} %get-tuple-element.284) | copy-start | bytes 24580
  54.4 70.1 %copy-start.44 = (f32[16,128]{1,0:T(8,128)}, f32[16,128]{1,0:T(8,128)S(1)}, u32[]{:S(2)}) copy-start(f32[16,128]{1,0:T(8,128)S(1)} %get-tuple-element.285) | copy-start | bytes 24580
  54.5 70.0 %copy-start.45 = (f32[16,128]{1,0:T(8,128)}, f32[16,128]{1,0:T(8,128)S(1)}, u32[]{:S(2)}) copy-start(f32[16,128]{1,0:T(8,128)S(1)} %get-tuple-element.282) | copy-start | bytes 24580
  54.5 70.0 %copy-start.46 = (f32[16,128]{1,0:T(8,128)}, f32[16,128]{1,0:T(8,128)S(1)}, u32[]{:S(2)}) copy-start(f32[16,128]{1,0:T(8,128)S(1)} %get-tuple-element.283) | copy-start | bytes 24580
  54.5 70.0 %copy-start.47 = (f32[16,128]{1,0:T(8,128)}, f32[16,128]{1,0:T(8,128)S(1)}, u32[]{:S(2)}) copy-start(f32[16,128]{1,0:T(8,128)S(1)} %get-tuple-element.280) | copy-start | bytes 24580
  54.5 70.0 %copy-start.48 = (f32[16,128]{1,0:T(8,128)}, f32[16,128]{1,0:T(8,128)S(1)}, u32[]{:S(2)}) copy-start(f32[16,128]{1,0:T(8,128)S(1)} %get-tuple-element.281) | copy-start | bytes 24580
  54.6 70.0 %copy-start.49 = (f32[16,128]{1,0:T(8,128)}, f32[16,128]{1,0:T(8,128)S(1)}, u32[]{:S(2)}) copy-start(f32[16,128]{1,0:T(8,128)S(1)} %get-tuple-element.278) | copy-start | bytes 24580
  54.6 70.0 %copy-start.50 = (f32[16,128]{1,0:T(8,128)}, f32[16,128]{1,0:T(8,128)S(1)}, u32[]{:S(2)}) copy-start(f32[16,128]{1,0:T(8,128)S(1)} %get-tuple-element.279) | copy-start | bytes 24580
  54.6 69.9 %copy-start.51 = (f32[16,128]{1,0:T(8,128)}, f32[16,128]{1,0:T(8,128)S(1)}, u32[]{:S(2)}) copy-start(f32[16,128]{1,0:T(8,128)S(1)} %get-tuple-element.276) | copy-start | bytes 24580
  54.6 69.9 %copy-start.52 = (f32[16,128]{1,0:T(8,128)}, f32[16,128]{1,0:T(8,128)S(1)}, u32[]{:S(2)}) copy-start(f32[16,128]{1,0:T(8,128)S(1)} %get-tuple-element.277) | copy-start | bytes 24580
  54.7 69.9 %copy-start.53 = (f32[16,128]{1,0:T(8,128)}, f32[16,128]{1,0:T(8,128)S(1)}, u32[]{:S(2)}) copy-start(f32[16,128]{1,0:T(8,128)S(1)} %get-tuple-element.274) | copy-start | bytes 24580
  54.7 69.9 %copy-start.54 = (f32[16,128]{1,0:T(8,128)}, f32[16,128]{1,0:T(8,128)S(1)}, u32[]{:S(2)}) copy-start(f32[16,128]{1,0:T(8,128)S(1)} %get-tuple-element.275) | copy-start | bytes 24580
  55.4 69.2 %copy-start.55 = (f32[16,128]{1,0:T(8,128)}, f32[16,128]{1,0:T(8,128)S(1)}, u32[]{:S(2)}) copy-start(f32[16,128]{1,0:T(8,128)S(1)} %get-tuple-element.272) | copy-start | bytes 24580
  55.4 69.2 %copy-start.56 = (f32[16,128]{1,0:T(8,128)}, f32[16,128]{1,0:T(8,128)S(1)}, u32[]{:S(2)}) copy-start(f32[16,128]{1,0:T(8,128)S(1)} %get-tuple-element.273) | copy-start | bytes 24580
  56.2 68.4 %copy-start.57 = (f32[16,128]{1,0:T(8,128)}, f32[16,128]{1,0:T(8,128)S(1)}, u32[]{:S(2)}) copy-start(f32[16,128]{1,0:T(8,128)S(1)} %get-tuple-element.270) | copy-start | bytes 24580
  56.2 68.4 %copy-start.58 = (f32[16,128]{1,0:T(8,128)}, f32[16,128]{1,0:T(8,128)S(1)}, u32[]{:S(2)}) copy-start(f32[16,128]{1,0:T(8,128)S(1)} %get-tuple-element.271) | copy-start | bytes 24580
  56.9 67.7 %copy-start.59 = (f32[16,128]{1,0:T(8,128)}, f32[16,128]{1,0:T(8,128)S(1)}, u32[]{:S(2)}) copy-start(f32[16,128]{1,0:T(8,128)S(1)} %get-tuple-element.268) | copy-start | bytes 24580
  56.9 67.7 %copy-start.60 = (f32[16,128]{1,0:T(8,128)}, f32[16,128]{1,0:T(8,128)S(1)}, u32[]{:S(2)}) copy-start(f32[16,128]{1,0:T(8,128)S(1)} %get-tuple-element.269) | copy-start | bytes 24580
  57.7 67.0 %copy-start.61 = (f32[16,128]{1,0:T(8,128)}, f32[16,128]{1,0:T(8,128)S(1)}, u32[]{:S(2)}) copy-start(f32[16,128]{1,0:T(8,128)S(1)} %get-tuple-element.266) | copy-start | bytes 24580
  57.7 67.0 %copy-start.62 = (f32[16,128]{1,0:T(8,128)}, f32[16,128]{1,0:T(8,128)S(1)}, u32[]{:S(2)}) copy-start(f32[16,128]{1,0:T(8,128)S(1)} %get-tuple-element.267) | copy-start | bytes 24580
  68.1 6.7 %collective-permute-start.8 = (f32[21,3,128]{2,0,1:T(8,128)S(1)}, f32[21,3,128]{2,0,1:T(8,128)S(1)}, u32[]{:S(2)}, u32[]{:S(2)}) collective-permute-start(f32[21,3,128]{2,0,1:T(8,128)S(1)} %get-tuple-element.236), channel_id=1, source_target_pairs={{0,4},{4,8},{8,12},{12,16},{16,20},{20,24},{24,28},{1,5},{5,9},{9,... | collective-permute-start | bytes 96776 | tf_op jit(solution)/shard_map/ppermute | solution.py:25
  70.0 6.4 %collective-permute-start.9 = (f32[21,3,128]{2,0,1:T(8,128)S(1)}, f32[21,3,128]{2,0,1:T(8,128)S(1)}, u32[]{:S(2)}, u32[]{:S(2)}) collective-permute-start(f32[21,3,128]{2,0,1:T(8,128)S(1)} %get-tuple-element.237), channel_id=1, source_target_pairs={{4,0},{8,4},{12,8},{16,12},{20,16},{24,20},{28,24},{5,1},{9,5},{13... | collective-permute-start | bytes 96776 | tf_op jit(solution)/shard_map/ppermute | solution.py:28
  76.6 9.9 %collective-permute-start.10 = (f32[21,22,3]{2,0,1:T(8,128)S(1)}, f32[21,22,3]{2,0,1:T(8,128)S(1)}, u32[]{:S(2)}, u32[]{:S(2)}) collective-permute-start(f32[21,22,3]{2,0,1:T(8,128)S(1)} %get-tuple-element.223), channel_id=1, source_target_pairs={{0,1},{1,2},{2,3},{4,5},{5,6},{6,7},{8,9},{9,10},{10,11},{12,13},{... | collective-permute-start | bytes 16640 | tf_op jit(solution)/shard_map/ppermute | solution.py:25
  81.0 9.7 %collective-permute-start.11 = (f32[21,22,3]{2,0,1:T(8,128)S(1)}, f32[21,22,3]{2,0,1:T(8,128)S(1)}, u32[]{:S(2)}, u32[]{:S(2)}) collective-permute-start(f32[21,22,3]{2,0,1:T(8,128)S(1)} %get-tuple-element.224), channel_id=1, source_target_pairs={{1,0},{2,1},{3,2},{5,4},{6,5},{7,6},{9,8},{10,9},{11,10},{13,12},{... | collective-permute-start | bytes 16640 | tf_op jit(solution)/shard_map/ppermute | solution.py:28
  97.7 6.5 %collective-permute-start.12 = (f32[21,3,128]{2,0,1:T(8,128)S(1)}, f32[21,3,128]{2,0,1:T(8,128)S(1)}, u32[]{:S(2)}, u32[]{:S(2)}) collective-permute-start(f32[21,3,128]{2,0,1:T(8,128)S(1)} %get-tuple-element.234), channel_id=1, source_target_pairs={{0,4},{4,8},{8,12},{12,16},{16,20},{20,24},{24,28},{1,5},{5,9},{9,... | collective-permute-start | bytes 96776 | tf_op jit(solution)/shard_map/ppermute | solution.py:25
  99.6 6.2 %collective-permute-start.13 = (f32[21,3,128]{2,0,1:T(8,128)S(1)}, f32[21,3,128]{2,0,1:T(8,128)S(1)}, u32[]{:S(2)}, u32[]{:S(2)}) collective-permute-start(f32[21,3,128]{2,0,1:T(8,128)S(1)} %get-tuple-element.235), channel_id=1, source_target_pairs={{4,0},{8,4},{12,8},{16,12},{20,16},{24,20},{28,24},{5,1},{9,5},{13... | collective-permute-start | bytes 96776 | tf_op jit(solution)/shard_map/ppermute | solution.py:28
  106.0 7.4 %collective-permute-start.14 = (f32[21,22,3]{2,0,1:T(8,128)S(1)}, f32[21,22,3]{2,0,1:T(8,128)S(1)}, u32[]{:S(2)}, u32[]{:S(2)}) collective-permute-start(f32[21,22,3]{2,0,1:T(8,128)S(1)} %get-tuple-element.219), channel_id=1, source_target_pairs={{0,1},{1,2},{2,3},{4,5},{5,6},{6,7},{8,9},{9,10},{10,11},{12,13},{... | collective-permute-start | bytes 16640 | tf_op jit(solution)/shard_map/ppermute | solution.py:25
  109.4 8.4 %collective-permute-start.15 = (f32[21,22,3]{2,0,1:T(8,128)S(1)}, f32[21,22,3]{2,0,1:T(8,128)S(1)}, u32[]{:S(2)}, u32[]{:S(2)}) collective-permute-start(f32[21,22,3]{2,0,1:T(8,128)S(1)} %get-tuple-element.220), channel_id=1, source_target_pairs={{1,0},{2,1},{3,2},{5,4},{6,5},{7,6},{9,8},{10,9},{11,10},{13,12},{... | collective-permute-start | bytes 16640 | tf_op jit(solution)/shard_map/ppermute | solution.py:28
  131.2 62.9 %copy-start.126 = (f32[16,128]{1,0:T(8,128)S(1)}, f32[16,128]{1,0:T(8,128)}, u32[]{:S(2)}) copy-start(f32[16,128]{1,0:T(8,128)} %get-tuple-element.15) | copy-start | bytes 24580
  131.2 63.0 %copy-start.125 = (f32[16,128]{1,0:T(8,128)S(1)}, f32[16,128]{1,0:T(8,128)}, u32[]{:S(2)}) copy-start(f32[16,128]{1,0:T(8,128)} %get-tuple-element.14) | copy-start | bytes 24580
  131.2 63.0 %copy-start.130 = (f32[16,128]{1,0:T(8,128)S(1)}, f32[16,128]{1,0:T(8,128)}, u32[]{:S(2)}) copy-start(f32[16,128]{1,0:T(8,128)} %get-tuple-element.8) | copy-start | bytes 24580
  131.2 63.0 %copy-start.129 = (f32[16,128]{1,0:T(8,128)S(1)}, f32[16,128]{1,0:T(8,128)}, u32[]{:S(2)}) copy-start(f32[16,128]{1,0:T(8,128)} %get-tuple-element.7) | copy-start | bytes 24580
  131.2 63.0 %copy-start.128 = (f32[16,128]{1,0:T(8,128)S(1)}, f32[16,128]{1,0:T(8,128)}, u32[]{:S(2)}) copy-start(f32[16,128]{1,0:T(8,128)} %get-tuple-element.6) | copy-start | bytes 24580
  176.0 18.2 %collective-permute-start.16 = (f32[21,3,128]{2,0,1:T(8,128)S(1)}, f32[21,3,128]{2,0,1:T(8,128)S(1)}, u32[]{:S(2)}, u32[]{:S(2)}) collective-permute-start(f32[21,3,128]{2,0,1:T(8,128)S(1)} %get-tuple-element.232), channel_id=1, source_target_pairs={{0,4},{4,8},{8,12},{12,16},{16,20},{20,24},{24,28},{1,5},{5,9},{9,... | collective-permute-start | bytes 96776 | tf_op jit(solution)/shard_map/ppermute | solution.py:25
  177.9 16.3 %collective-permute-start.17 = (f32[21,3,128]{2,0,1:T(8,128)S(1)}, f32[21,3,128]{2,0,1:T(8,128)S(1)}, u32[]{:S(2)}, u32[]{:S(2)}) collective-permute-start(f32[21,3,128]{2,0,1:T(8,128)S(1)} %get-tuple-element.233), channel_id=1, source_target_pairs={{4,0},{8,4},{12,8},{16,12},{20,16},{24,20},{28,24},{5,1},{9,5},{13... | collective-permute-start | bytes 96776 | tf_op jit(solution)/shard_map/ppermute | solution.py:28
  194.4 7.7 %collective-permute-start.18 = (f32[21,22,3]{2,0,1:T(8,128)S(1)}, f32[21,22,3]{2,0,1:T(8,128)S(1)}, u32[]{:S(2)}, u32[]{:S(2)}) collective-permute-start(f32[21,22,3]{2,0,1:T(8,128)S(1)} %get-tuple-element.215), channel_id=1, source_target_pairs={{0,1},{1,2},{2,3},{4,5},{5,6},{6,7},{8,9},{9,10},{10,11},{12,13},{... | collective-permute-start | bytes 16640 | tf_op jit(solution)/shard_map/ppermute | solution.py:25
  196.7 9.5 %collective-permute-start.19 = (f32[21,22,3]{2,0,1:T(8,128)S(1)}, f32[21,22,3]{2,0,1:T(8,128)S(1)}, u32[]{:S(2)}, u32[]{:S(2)}) collective-permute-start(f32[21,22,3]{2,0,1:T(8,128)S(1)} %get-tuple-element.216), channel_id=1, source_target_pairs={{1,0},{2,1},{3,2},{5,4},{6,5},{7,6},{9,8},{10,9},{11,10},{13,12},{... | collective-permute-start | bytes 16640 | tf_op jit(solution)/shard_map/ppermute | solution.py:28
  (112 other events, 2465.9 us)
where the time goes:
time: 249 us; the launch traced here: 244 us
  other arithmetic  84.1 us (34%)
  starting transfers between devices  57.6 us (23%)
  blocking collectives  43 us (17%)
  waiting for transfers between devices  37.6 us (15%)
  local copies, waits for them, and re-layouts  14.4 us (6%)
  between operations  4 us (2%)
  matrix products  3.53 us (1%)
    psum x1, blocking collectives, on_device(): lax.psum(compat_sum, ('rows', 'cols')) / math.sqrt(total_pixels)  43 us
    ppermute x10, starting transfers between devices, with_halo(): lax.ppermute(lax.slice_in_dim(block, 0, width, axis=dim), axis, backward)  29.8 us
    ppermute x10, starting transfers between devices, with_halo(): lax.ppermute(lax.slice_in_dim(block, block.shape[dim] - width, None, axis...  27.9 us
    ppermute x10, waiting for transfers between devices, with_halo(): lax.ppermute(lax.slice_in_dim(block, 0, width, axis=dim), axis, backward)  24 us
    reduce_sum x16, other arithmetic, pair_terms(): jnp.sum(grad_center * prob_shift + grad_shift * prob_center, axis=0)  16.8 us
    mul x24, other arithmetic, affinity(): spatial_weight(row_step, col_step) * jnp.exp(-distance * factor)  14 us
    sub x1, other arithmetic, softmax_grad(): return prob * (cotangent - jnp.sum(cotangent * prob, axis=0, keepdims=True))  13.9 us
    ppermute x10, waiting for transfers between devices, with_halo(): lax.ppermute(lax.slice_in_dim(block, block.shape[dim] - width, None, axis...  13.6 us
  transfers between devices with their start and end apart: 20, of which 12 were waited for; matrix products, arithmetic and copies ran while one was open for 5% of the time, Pallas kernels for 0%

commit v1 on v0

v1 whole, which is shorter than its diff:
```python
import functools
import math

import jax
import jax.numpy as jnp
from jax import lax
from jax.experimental import pallas as pl
from jax.experimental.pallas import tpu as pltpu
from jax.sharding import PartitionSpec as P

ITERS = 2
REACH = 3
HALO = 2 * ITERS * REACH
STRIP = 16
PAD = 24
LOW = -1e30
VMEM = pl.BlockSpec(memory_space=pltpu.VMEM)
SMEM = pl.BlockSpec(memory_space=pltpu.SMEM)
HIGH = lax.Precision.HIGHEST


def params():
    return pltpu.CompilerParams(vmem_limit_bytes=56 * 1024 * 1024)


def sublane(width=128):
    return lax.broadcasted_iota(jnp.int32, (8, width), 0)


def lane(width=128):
    return lax.broadcasted_iota(jnp.int32, (1, width), 1)


def shifted(value, step):
    width = value.shape[-1]
    return pltpu.roll(value, (-step) % width, axis=value.ndim - 1)


def merge(parts):
    row = sublane(parts[0].shape[-1])
    bit = 1
    while len(parts) > 1:
        low = (row & bit) == 0
        parts = [
            jnp.where(low, first, second)
            + pltpu.roll(jnp.where(low, second, first), 8 - bit, axis=0)
            for first, second in zip(parts[::2], parts[1::2])
        ]
        bit *= 2
    return parts[0]


def fold(value):
    total = value[0:8]
    for start in range(8, value.shape[0], 8):
        total = total + value[start : start + 8]
    return total


def pack_kernel(feat, unary, grad, centre, left, right, wide):
    channels, height, _ = feat.shape
    classes = unary.shape[0] // height
    wide[...] = feat[...].astype(jnp.float32).reshape(channels * height, 128) * (
        1.0 / math.sqrt(channels)
    )
    empty = jnp.zeros((PAD - classes, 128), jnp.float32)
    side = lane()
    ends = [[], []]
    for y in range(height):
        rows = jnp.concatenate(
            [
                wide[pl.ds(y, channels, stride=height), :],
                unary[pl.ds(y, classes, stride=height), :],
                empty + LOW,
                grad[pl.ds(y, classes, stride=height), :],
                empty,
            ],
            axis=0,
        )
        centre[y] = rows
        at = (y % 8) * STRIP
        here = (side >= at) & (side < at + STRIP)
        for end, shift in ((0, at), (1, (at + STRIP) % 128)):
            moved = pltpu.roll(rows, shift, axis=1)
            if y % 8 == 0:
                ends[end].append(moved)
            else:
                ends[end][-1] = jnp.where(here, moved, ends[end][-1])
    for slot in range(height // 8):
        left[slot] = ends[0][slot]
        right[slot] = ends[1][slot]


def pack(feat, unary, grad):
    channels, height, _ = feat.shape
    depth = channels + 2 * PAD
    strips = jax.ShapeDtypeStruct((height // 8, depth, 128), jnp.float32)
    return pl.pallas_call(
        pack_kernel,
        out_shape=(jax.ShapeDtypeStruct((height, depth, 128), jnp.float32), strips, strips),
        in_specs=[VMEM] * 3,
        out_specs=(VMEM,) * 3,
        scratch_shapes=[pltpu.VMEM((channels * height, 128), jnp.float32)],
        compiler_params=params(),
        name="pack",
    )(feat, unary.reshape(-1, 128), grad.reshape(-1, 128))


def pass_row(y, kern, field, turned):
    def weight(row, at):
        return kern[row, pl.ds(at, 1), :]

    total = None

    def plus(total, term):
        return term if total is None else total + term

    for group in range(REACH):
        step = group + 1
        for a in range(-REACH, REACH + 1):
            total = plus(
                total, weight(y, 8 * group + a + REACH) * turned[group, y + a + REACH]
            )
        total = total + weight(y, 8 * group + 7) * field[y + step + REACH]
        total = total + weight(y - step, 8 * group + 7) * field[y - step + REACH]
    for group in range(REACH):
        back = None
        for a in range(-REACH, REACH + 1):
            back = plus(
                back, weight(y - a, 8 * group + a + REACH) * field[y - a + REACH]
            )
        total = total + shifted(back, -(group + 1))
    return total


def turn(field, turned, low, high):
    def body(row, carry):
        value = field[row]
        for group in range(REACH):
            turned[group, row] = shifted(value, group + 1)
        return carry

    lax.fori_loop(low, high, body, 0)


def softmax(value):
    top = jnp.max(value, axis=0, keepdims=True)
    power = jnp.exp(value - top)
    return power * (1.0 / jnp.sum(power, axis=0, keepdims=True))


def field_kernel(
    place, compat, compat_t, centre, first, second, from_left, from_right,
    feat_out, kern_out, prob0_out, prob1_out, grad1_out, grad0_out, unary_out, share,
    feat, feat_turned, norm, norm_turned, kern, unary, grad, prob0, prob1, grad1, grad0,
    turned, message0, message1, logit,
):
    height = centre.shape[0]
    rows = height + 2 * HALO
    channels = feat.shape[1]
    side = lane()

    feat[pl.ds(0, REACH)] = jnp.zeros((REACH,) + feat.shape[1:], jnp.float32)
    feat[pl.ds(rows + REACH, REACH)] = jnp.zeros((REACH,) + feat.shape[1:], jnp.float32)

    def put(row, main, left, right, slot):
        moved_right = pltpu.roll(right, (128 - slot * STRIP) % 128, axis=1)
        moved_left = pltpu.roll(left, (128 - STRIP - slot * STRIP) % 128, axis=1)
        edge = jnp.where(side < 64, moved_right, moved_left)
        feat[row + REACH, :, 0:128] = main[0:channels]
        feat[row + REACH, :, 128:256] = edge[0:channels]
        unary[row, :, 0:128] = main[channels : channels + PAD]
        unary[row, :, 128:256] = edge[channels : channels + PAD]
        grad[row, :, 0:128] = main[channels + PAD :]
        grad[row, :, 128:256] = edge[channels + PAD :]

    for y in range(height):
        put(HALO + y, centre[y], from_left[y // 8], from_right[y // 8], y % 8)
    strips = height // 8
    for source, above in ((first, place[0] == 0), (second, place[0] == 1)):
        base = jnp.where(above, 0, HALO + height)
        for y in range(HALO):
            gap = height - HALO

            @pl.when(above)
            def _(y=y, source=source):
                at = y + gap
                put(
                    y, source[y], source[HALO + at // 8], source[HALO + strips + at // 8], at % 8
                )

            @pl.when(jnp.logical_not(above))
            def _(y=y, source=source):
                put(
                    HALO + height + y, source[y], source[HALO + y // 8],
                    source[HALO + strips + y // 8], y % 8,
                )

    wide_lane = lane(256)
    inside_lane = (
        (wide_lane < 128)
        | ((wide_lane < 192) & (place[2] == 0))
        | ((wide_lane >= 192) & (place[1] == 0))
    )

    def inside(y):
        row = place[3] + y
        return inside_lane & (row >= 0) & (row < place[4])

    def turn_feat(row, carry):
        value = feat[row]
        size = fold(value * value) * 0.5
        norm[row] = size
        for group in range(REACH):
            feat_turned[group, row] = shifted(value, group + 1)
            norm_turned[group, row] = shifted(size, group + 1)
        return carry

    lax.fori_loop(0, rows + 2 * REACH, turn_feat, 0)

    sub = sublane()

    def affinity_row(y, carry):
        for tile in range(2):
            cols = pl.ds(128 * tile, 128)
            here = feat[y + REACH, :, cols]
            size = norm[y + REACH, :, cols]
            for group in range(REACH):
                parts = []
                for a in range(-REACH, REACH + 1):
                    there = feat_turned[group, y + a + REACH, :, cols]
                    parts.append(
                        fold(here * there) - (size + norm_turned[group, y + a + REACH, :, cols])
                    )
                below = y + group + 1 + REACH
                parts.append(fold(here * feat[below, :, cols]) - (size + norm[below, :, cols]))
                step_a = jnp.where(sub == 7, group + 1, sub - REACH)
                step_b = jnp.where(sub == 7, 0, group + 1)
                far = (step_a * step_a + step_b * step_b).astype(jnp.float32)
                kern[y, pl.ds(8 * group, 8), cols] = jnp.exp(
                    merge(parts) - far * (1.0 / (2.0 * REACH * REACH))
                )
        return carry

    lax.fori_loop(0, rows, affinity_row, 0)

    for ref in (prob0, prob1, grad1, grad0):
        ref[...] = jnp.zeros_like(ref)

    def start(y, carry):
        prob0[y + REACH] = jnp.where(inside(y), softmax(unary[y]), 0.0)
        return carry

    lax.fori_loop(0, rows, start, 0)

    def run_pass(field, out, low, high):
        turn(field, turned, low, high + 2 * REACH)

        def body(y, carry):
            out[y] = pass_row(y, kern, field, turned)
            return carry

        lax.fori_loop(low, high, body, 0)

    def dot(left, right):
        return jnp.dot(left, right, precision=HIGH, preferred_element_type=jnp.float32)

    def outer(left, right):
        return lax.dot_general(
            left, right, (((1,), (1,)), ((), ())), precision=HIGH,
            preferred_element_type=jnp.float32,
        )

    run_pass(prob0, message0, REACH, rows - REACH)

    def mix(y, carry):
        prob1[y + REACH] = jnp.where(
            inside(y), softmax(unary[y] - dot(compat[...], message0[y])), 0.0
        )
        return carry

    lax.fori_loop(REACH, rows - REACH, mix, 0)
    run_pass(prob1, message1, 2 * REACH, rows - 2 * REACH)

    def back1(y, carry):
        prob = softmax(unary[y] - dot(compat[...], message1[y]))
        cot = grad[y]
        change = prob * (cot - jnp.sum(cot * prob, axis=0, keepdims=True))
        logit[y] = change
        grad1[y + REACH] = jnp.where(inside(y), -dot(compat_t[...], change), 0.0)
        return carry

    lax.fori_loop(2 * REACH, rows - 2 * REACH, back1, 0)
    total = jnp.zeros((PAD, PAD), jnp.float32)

    def add_share(message):
        def body(y, carry):
            return carry - outer(logit[y, :, 0:128], message[y, :, 0:128])

        return body

    total = lax.fori_loop(HALO, HALO + height, add_share(message1), total)

    def keep(y, carry):
        unary_out[y - HALO] = logit[y, :, 0:128]
        return carry

    lax.fori_loop(HALO, HALO + height, keep, 0)
    run_pass(grad1, message1, 3 * REACH, rows - 3 * REACH)

    def back0(y, carry):
        prob = prob1[y + REACH]
        cot = message1[y]
        change = prob * (cot - jnp.sum(cot * prob, axis=0, keepdims=True))
        logit[y] = change
        grad0[y + REACH] = jnp.where(inside(y), -dot(compat_t[...], change), 0.0)
        return carry

    lax.fori_loop(3 * REACH, rows - 3 * REACH, back0, 0)
    total = lax.fori_loop(HALO, HALO + height, add_share(message0), total)

    def keep0(y, carry):
        unary_out[y - HALO] += logit[y, :, 0:128]
        return carry

    lax.fori_loop(HALO, HALO + height, keep0, 0)

    total = jnp.concatenate([total, jnp.zeros((PAD, 128 - PAD), jnp.float32)], axis=1)
    packed = (
        total[0:8]
        + pltpu.roll(total[8:16], 32, axis=1)
        + pltpu.roll(total[16:24], 64, axis=1)
    )
    for slot in range(share.shape[0]):
        share[slot] = packed

    near = height + 2 * REACH

    def copy(row, carry):
        at = row + HALO
        feat_out[row] = feat[at]
        prob0_out[row] = prob0[at]
        prob1_out[row] = prob1[at]
        grad1_out[row] = grad1[at]
        grad0_out[row] = grad0[at]
        kern_out[row] = kern[at - REACH]
        return carry

    lax.fori_loop(0, near, copy, 0)


def iterate(place, compat, centre, first, second, from_left, from_right, devices):
    height, depth, _ = centre.shape
    channels = depth - 2 * PAD
    rows = height + 2 * HALO
    tall = rows + 2 * REACH
    near = height + 2 * REACH

    def shape(*dims):
        return jax.ShapeDtypeStruct(dims, jnp.float32)

    def room(*dims):
        return pltpu.VMEM(dims, jnp.float32)

    return pl.pallas_call(
        field_kernel,
        out_shape=(
            shape(near, channels, 256),
            shape(near, PAD, 256),
            shape(near, PAD, 256),
            shape(near, PAD, 256),
            shape(near, PAD, 256),
            shape(near, PAD, 256),
            shape(height, PAD, 128),
            shape(devices, 8, 128),
        ),
        in_specs=[SMEM] + [VMEM] * 7,
        out_specs=(VMEM,) * 8,
        scratch_shapes=[
            room(tall, channels, 256),
            room(REACH, tall, channels, 256),
            room(tall, 8, 256),
            room(REACH, tall, 8, 256),
            room(rows, PAD, 256),
            room(rows, PAD, 256),
            room(rows, PAD, 256),
            room(tall, PAD, 256),
            room(tall, PAD, 256),
            room(tall, PAD, 256),
            room(tall, PAD, 256),
            room(REACH, tall, PAD, 256),
            room(rows, PAD, 256),
            room(rows, PAD, 256),
            room(rows, PAD, 256),
        ],
        compiler_params=params(),
        name="iterate",
    )(place, compat, compat.T, centre, first, second, from_left, from_right)


def finish_kernel(
    feat, kern, prob0, prob1, grad1, grad0, partial, unary_out, feat_out,
    feat_turned, all_turned, turned, kern_back, weights,
):
    height = partial.shape[0]
    near = height + 2 * REACH
    channels = feat.shape[1]
    classes = unary_out.shape[0] // height
    steps = range(-REACH, REACH + 1)

    def prepare(row, carry):
        value = feat[row]
        for b in steps:
            feat_turned[b + REACH, row] = shifted(value, b)[:, 0:128] if b else value[:, 0:128]
        for place, field in enumerate((prob0, prob1, grad1, grad0)):
            value = field[row]
            for b in steps:
                moved = shifted(value, b) if b else value
                all_turned[b + REACH, row, pl.ds(place * PAD, PAD), :] = moved[:, 0:128]
                if field is grad0 and b > 0:
                    turned[b - 1, row] = moved
        for group in range(REACH):
            value = kern[row, pl.ds(8 * group, 8), :]
            kern_back[row, pl.ds(8 * group, 8), :] = jnp.where(
                sublane() == 7, value[:, 0:128], shifted(value, -(group + 1))[:, 0:128]
            )
        return carry

    lax.fori_loop(0, near, prepare, 0)

    def unary_row(y, carry):
        cot = pass_row(y + REACH, kern, _Offset(grad0), _Offset(turned, 1))[:, 0:128]
        prob = prob0[y + REACH, :, 0:128]
        value = partial[y] + prob * (cot - jnp.sum(cot * prob, axis=0, keepdims=True))
        for start in range(0, classes, 8):
            size = min(8, classes - start)
            unary_out[pl.ds(start * height + y, size, stride=height), :] = value[
                start : start + size
            ]
        return carry

    lax.fori_loop(0, height, unary_row, 0)
    sub = sublane()

    def feature_row(y, carry):
        row = y + REACH
        own = all_turned[REACH, row]
        mate = jnp.concatenate(
            [own[3 * PAD :], own[2 * PAD : 3 * PAD], own[PAD : 2 * PAD], own[0:PAD]], axis=0
        )
        total = None
        whole = None
        for sign in (1, -1):
            for group in range(REACH):
                parts = []
                places = []
                for s in range(8):
                    a, b = (s - REACH, group + 1) if s < 7 else (group + 1, 0)
                    a, b = sign * a, sign * b
                    places.append((a, b))
                    parts.append(fold(mate * all_turned[b + REACH, row + a]))
                if sign > 0:
                    weight = kern[row, pl.ds(8 * group, 8), 0:128]
                else:
                    weight = kern_back[row - (group + 1), pl.ds(8 * group, 8), :]
                    for s in range(7):
                        weight = jnp.where(
                            sub == s, kern_back[row - (s - REACH), pl.ds(8 * group, 8), :], weight
                        )
                weight = weight * merge(parts)
                whole = weight if whole is None else whole + weight
                at = 8 * (group + (0 if sign > 0 else REACH))
                weights[y, pl.ds(at, 8), :] = weight
                for s, (a, b) in enumerate(places):
                    term = weights[y, pl.ds(at + s, 1), :] * feat_turned[b + REACH, row + a]
                    total = term if total is None else total + term
        whole = jnp.sum(whole, axis=0, keepdims=True)
        total = total - whole * feat_turned[REACH, row]
        feat_out[pl.ds(y, channels, stride=height), :] = total * (1.0 / math.sqrt(channels))
        return carry

    lax.fori_loop(0, height, feature_row, 0)


class _Offset:
    def __init__(self, ref, axis=0):
        self.ref, self.axis = ref, axis

    def __getitem__(self, index):
        if self.axis:
            return self.ref[index[0], index[1] - REACH]
        return self.ref[index - REACH]


def finish(feat, kern, prob0, prob1, grad1, grad0, partial, classes):
    near, channels, _ = feat.shape
    height = partial.shape[0]

    def room(*dims):
        return pltpu.VMEM(dims, jnp.float32)

    return pl.pallas_call(
        finish_kernel,
        out_shape=(
            jax.ShapeDtypeStruct((classes * height, 128), jnp.float32),
            jax.ShapeDtypeStruct((channels * height, 128), jnp.float32),
        ),
        in_specs=[VMEM] * 7,
        out_specs=(VMEM,) * 2,
        scratch_shapes=[
            room(2 * REACH + 1, near, channels, 128),
            room(2 * REACH + 1, near, 4 * PAD, 128),
            room(REACH, near, PAD, 256),
            room(near, PAD, 128),
            room(height, 6 * 8, 128),
        ],
        compiler_params=params(),
        cost_estimate=pl.CostEstimate(flops=200_000_000, bytes_accessed=8_000_000, transcendentals=0),
        name="finish",
    )(feat, kern, prob0, prob1, grad1, grad0, partial)


def on_device(unary, features, compat, grad_output):
    classes, height, width = unary.shape
    n_rows, n_cols = lax.axis_size("rows"), lax.axis_size("cols")
    row, col = lax.axis_index("rows"), lax.axis_index("cols")
    odd = row % 2

    centre, left, right = pack(features, unary, grad_output)
    forward = [(i, i + 1) for i in range(n_cols - 1)]
    backward = [(i + 1, i) for i in range(n_cols - 1)]
    from_left = lax.ppermute(right, "cols", forward)
    from_right = lax.ppermute(left, "cols", backward)
    strips = jnp.concatenate([from_left, from_right], axis=0)

    top = jnp.concatenate([centre[:HALO], strips], axis=0)
    bottom = jnp.concatenate([centre[height - HALO :], strips], axis=0)
    below = [pair for i in range(0, n_rows, 2) for pair in ((i, i + 1), (i + 1, i))]
    above = [
        pair
        for i in range(1, n_rows, 2)
        for pair in ((i, (i + 1) % n_rows), ((i + 1) % n_rows, i))
    ]
    first = lax.ppermute(jnp.where(odd == 0, bottom, top), "rows", below)
    second = lax.ppermute(jnp.where(odd == 0, top, bottom), "rows", above)

    place = jnp.stack(
        [1 - odd, col == 0, col == n_cols - 1, row * height - HALO, n_rows * height]
    ).astype(jnp.int32)
    square = jnp.pad(compat, ((0, PAD - classes), (0, PAD - classes)))
    devices = n_rows * n_cols
    *fields, partial, share = iterate(
        place, square, centre, first, second, from_left, from_right, devices
    )
    shares = lax.all_to_all(share, ("rows", "cols"), 0, 0)
    unary_grad, feature_grad = finish(*fields, partial, classes)
    summed = jnp.sum(shares, axis=0) / math.sqrt(n_rows * height * n_cols * width)
    compat_grad = jnp.concatenate(
        [summed[:, 0:PAD], summed[:, 32 : 32 + PAD], summed[:, 64 : 64 + PAD]], axis=0
    )[:classes, :classes]
    return (
        unary_grad.reshape(unary.shape),
        feature_grad.reshape(features.shape),
        compat_grad,
    )


def solution(mesh):
    placed = (P(None, "rows", "cols"), P(None, "rows", "cols"), P(), P(None, "rows", "cols"))
    return jax.shard_map(
        on_device,
        mesh=mesh,
        in_specs=placed,
        out_specs=(P(None, "rows", "cols"), P(None, "rows", "cols"), P()),
        check_vma=False,
    )
```

time: 249 us -> 131 us (0.53)
  the two profiles are of different devices: /device:TPU:4 before, /device:TPU:0 now
where the time goes in v1:
time: 131 us
  Pallas kernels  87.6 us (67%)
  waiting for transfers between devices  24.2 us (18%)
  starting transfers between devices  10.9 us (8%)
  local copies, waits for them, and re-layouts  5.35 us (4%)
  other arithmetic  1.71 us (1%)
    pallas_call x1, Pallas kernels, iterate(): pl.pallas_call(field_kernel, out_shape=(shape(near, channels, 256), shape...  67.4 us
    ppermute x1, waiting for transfers between devices, on_device(): second = lax.ppermute(jnp.where(odd == 0, top, bottom), 'rows', above)  20.1 us
    pallas_call x1, Pallas kernels, finish(): pl.pallas_call(finish_kernel, out_shape=(jax.ShapeDtypeStruct((classes *...  17.7 us
    ppermute x1, starting transfers between devices, on_device(): from_left = lax.ppermute(right, 'cols', forward)  4.92 us
    ppermute x1, waiting for transfers between devices, on_device(): from_right = lax.ppermute(left, 'cols', backward)  4.16 us
    all_to_all x1, starting transfers between devices, on_device(): shares = lax.all_to_all(share, ('rows', 'cols'), 0, 0)  3.13 us
  transfers between devices with their start and end apart: 5, of which 2 were waited for; matrix products, arithmetic and copies ran while one was open for 3% of the time, Pallas kernels for 14%

profile of v1, /device:TPU:0, one launch (start us, length us, event | category | flops | bytes accessed | tf_op | source)
XLA Modules:
  0.0 130.5 jit_solution(2350757996108169640)
XLA Ops:
  0.6 2.6 %pack.1 = (f32[16,112,128]{2,1,0:T(8,128)}, f32[2,112,128]{2,1,0:T(8,128)}, f32[2,112,128]{2,1,0:T(8,128)}) custom-call(bf16[64,16,128]{2,1,0:T(8,128)(2,1)} %feat.1, f32[336,128]{1,0:T(8,128)} %bitcast.10, f32[336,128]{1,0:T(8,128)} %bitcast.11), custom_call_target="tpu_custom_call" | custom-call | tf_op jit(solution)/shard_map/pack/pallas_call | solution.py:98
  3.2 4.9 %collective-permute-start = (f32[2,112,128]{2,1,0:T(8,128)}, f32[2,112,128]{2,1,0:T(8,128)S(1)}, u32[]{:S(2)}, u32[]{:S(2)}) collective-permute-start(f32[2,112,128]{2,1,0:T(8,128)} %get-tuple-element.17), channel_id=1, source_target_pairs={{0,1},{1,2},{2,3},{4,5},{5,6},{6,7},{8,9},{9,10},{10,11},{12,13},{... | collective-permute-start | bytes 344072 | tf_op jit(solution)/shard_map/ppermute | solution.py:532
  8.1 1.3 collective-permute-start.1
  9.4 1.4 %fusion.2 = (f32[12,112,128]{2,1,0:T(8,128)S(1)}, f32[12,112,128]{2,1,0:T(8,128)S(1)}) fusion(f32[16,112,128]{2,1,0:T(8,128)} %get-tuple-element.16.centre), kind=kLoop, calls=%fused_computation.10 | loop fusion | bytes 2752512 | tf_op jit(solution)/shard_map/slice | solution.py:536
  10.8 0.0 collective-permute-done.from_left
  10.8 0.0 copy-start.2
  10.9 4.2 %collective-permute-done.1.from_right = f32[2,112,128]{2,1,0:T(8,128)S(1)} collective-permute-done((f32[2,112,128]{2,1,0:T(8,128)}, f32[2,112,128]{2,1,0:T(8,128)S(1)}, u32[]{:S(2)}, u32[]{:S(2)}) %collective-permute-start.1) | collective-permute-done | bytes 114720 | tf_op jit(solution)/shard_map/ppermute | solution.py:533
  15.0 0.0 copy-start.3
  15.0 0.0 copy-start.4
  15.0 1.1 fusion
  16.1 0.0 copy-done.2
  16.1 0.0 copy-done.3
  16.1 0.5 collective-permute-start.3
  16.5 1.1 collective-permute-start.2
  17.7 0.0 copy-done.4
  17.7 0.1 copy.7
  17.8 0.1 copy.9
  17.9 0.6 pad.4.clone.compat
  18.5 0.6 stack.27.place
  19.1 0.6 pad_bitcast_fusion.compat_t
  19.7 20.1 %collective-permute-done.3.second = f32[16,112,128]{2,1,0:T(8,128)S(1)} collective-permute-done((f32[16,112,128]{2,1,0:T(8,128)}, f32[16,112,128]{2,1,0:T(8,128)S(1)}, u32[]{:S(2)}, u32[]{:S(2)}) %collective-permute-start.3) | collective-permute-done | bytes 917536 | tf_op jit(solution)/shard_map/ppermute | solution.py:545
  39.7 0.0 copy-start
  39.7 0.0 collective-permute-done.2.first
  39.7 0.9 copy-done
  40.7 0.0 copy-start.1
  40.7 0.9 copy-done.1
  41.6 67.4 %iterate.1 = (f32[22,64,256]{2,1,0:T(8,128)}, f32[22,24,256]{2,1,0:T(8,128)}, f32[22,24,256]{2,1,0:T(8,128)}, f32[22,24,256]{2,1,0:T(8,128)}, f32[22,24,256]{2,1...) custom-call(s32[5]{0:T(128)} %stack.27.place, f32[24,24]{1,0:T(8,128)} %pad.4.clone.compat, ...), custom_call_target="tpu_custom_call" | custom-call | tf_op jit(solution)/shard_map/iterate/pallas_call | solution.py:365
  109.0 3.1 %all-to-all-start = ((f32[32,8,128]{2,1,0:T(8,128)}), f32[32,8,128]{2,1,0:T(8,128)S(1)}, u32[]{:S(2)}, u32[]{:S(2)}) async-start(f32[32,8,128]{2,1,0:T(8,128)} %get-tuple-element.28), calls=%async_computation | async-start | bytes 262144 | tf_op jit(solution)/shard_map/all_to_all | solution.py:555
  112.1 17.7 %finish.1 = (f32[336,128]{1,0:T(8,128)}, f32[1024,128]{1,0:T(8,128)}) custom-call(f32[22,64,256]{2,1,0:T(8,128)} %get-tuple-element.19.feat, f32[22,24,256]{2,1,0:T(8,128)} %get-tuple-element.20.kern, f32[22,24,256]{2,1,0:T(8,128)} %get-tuple-element.21.prob0, f32[22,24,256]{2,1,0:T(8,128)} %get-tuple-element.22.prob1, ...), custom_call_target="tpu_custom_call" | custom-call | flops 200000000 | bytes 8000000 | tf_op jit(solution)/shard_map/finish/pallas_call | solution.py:502
  129.8 0.0 all-to-all-done
  129.8 0.1 fusion.3
  129.9 0.6 pad_maximum_fusion.4
  (2 shorter events, 0.0 us)
Async XLA Ops:
  3.2 7.6 %collective-permute-start = (f32[2,112,128]{2,1,0:T(8,128)}, f32[2,112,128]{2,1,0:T(8,128)S(1)}, u32[]{:S(2)}, u32[]{:S(2)}) collective-permute-start(f32[2,112,128]{2,1,0:T(8,128)} %get-tuple-element.17), channel_id=1, source_target_pairs={{0,1},{1,2},{2,3},{4,5},{5,6},{6,7},{8,9},{9,10},{10,11},{12,13},{... | collective-permute-start | bytes 344072 | tf_op jit(solution)/shard_map/ppermute | solution.py:532
  8.1 6.9 %collective-permute-start.1 = (f32[2,112,128]{2,1,0:T(8,128)}, f32[2,112,128]{2,1,0:T(8,128)S(1)}, u32[]{:S(2)}, u32[]{:S(2)}) collective-permute-start(f32[2,112,128]{2,1,0:T(8,128)} %get-tuple-element.18), channel_id=1, source_target_pairs={{1,0},{2,1},{3,2},{5,4},{6,5},{7,6},{9,8},{10,9},{11,10},{13,12},{... | collective-permute-start | bytes 344072 | tf_op jit(solution)/shard_map/ppermute | solution.py:533
  10.8 5.2 %copy-start.2 = (f32[2,112,128]{2,1,0:T(8,128)}, f32[2,112,128]{2,1,0:T(8,128)S(1)}, u32[]{:S(2)}) copy-start(f32[2,112,128]{2,1,0:T(8,128)S(1)} %collective-permute-done.from_left) | copy-start | bytes 344068
  15.0 1.1 copy-start.3
  15.0 2.7 %copy-start.4 = (f32[21,21]{1,0:T(8,128)S(1)}, f32[21,21]{1,0:T(8,128)}, u32[]{:S(2)}) copy-start(f32[21,21]{1,0:T(8,128)} %param.6) | copy-start | bytes 5296
  16.1 23.7 %collective-permute-start.3 = (f32[16,112,128]{2,1,0:T(8,128)}, f32[16,112,128]{2,1,0:T(8,128)S(1)}, u32[]{:S(2)}, u32[]{:S(2)}) collective-permute-start(f32[16,112,128]{2,1,0:T(8,128)} %get-tuple-element.29), channel_id=1, source_target_pairs={{4,8},{8,4},{12,16},{16,12},{20,24},{24,20},{28,0},{0,28},{5,9},{9... | collective-permute-start | bytes 2752520 | tf_op jit(solution)/shard_map/ppermute | solution.py:545
  16.5 23.2 %collective-permute-start.2 = (f32[16,112,128]{2,1,0:T(8,128)S(1)}, f32[16,112,128]{2,1,0:T(8,128)S(1)}, u32[]{:S(2)}, u32[]{:S(2)}) collective-permute-start(f32[16,112,128]{2,1,0:T(8,128)S(1)} %get-tuple-element.30), channel_id=1, source_target_pairs={{0,4},{4,0},{8,12},{12,8},{16,20},{20,16},{24,28},{28,24},{1,5},{5... | collective-permute-start | bytes 2752520 | tf_op jit(solution)/shard_map/ppermute | solution.py:544
  39.7 0.9 copy-start
  40.7 0.9 copy-start.1
  109.0 20.8 %all-to-all-start = ((f32[32,8,128]{2,1,0:T(8,128)}), f32[32,8,128]{2,1,0:T(8,128)S(1)}, u32[]{:S(2)}, u32[]{:S(2)}) async-start(f32[32,8,128]{2,1,0:T(8,128)} %get-tuple-element.28), calls=%async_computation | async-start | bytes 262144 | tf_op jit(solution)/shard_map/all_to_all | solution.py:555

commit v2 on v1

--- a/solution.py
+++ b/solution.py
@@ -13,10 +13,10 @@
 HALO = 2 * ITERS * REACH
 STRIP = 16
 PAD = 24
+DEEP = 32
 LOW = -1e30
 VMEM = pl.BlockSpec(memory_space=pltpu.VMEM)
 SMEM = pl.BlockSpec(memory_space=pltpu.SMEM)
-HIGH = lax.Precision.HIGHEST
 
 
 def params():
@@ -32,8 +32,66 @@
 
 
 def shifted(value, step):
-    width = value.shape[-1]
-    return pltpu.roll(value, (-step) % width, axis=value.ndim - 1)
+    low, high = value[:, 0:128], value[:, 128:256]
+    column = lane() + step
+    here = (column >= 0) & (column < 128)
+    low = pltpu.roll(low, (-step) % 128, axis=1)
+    high = pltpu.roll(high, (-step) % 128, axis=1)
+    return jnp.concatenate([jnp.where(here, low, high), jnp.where(here, high, low)], axis=1)
+
+
+def each_row(low, high, step, body):
+    def some(turn, carry):
+        for at in range(step):
+            body(low + turn * step + at)
+        return carry
+
+    turns = (high - low) // step
+    lax.fori_loop(0, turns, some, 0)
+    for y in range(low + turns * step, high):
+        body(y)
+
+
+def split(value):
+    parts = []
+    for _ in range(2):
+        part = value.astype(jnp.bfloat16)
+        parts.append(part)
+        value = value - part.astype(jnp.float32)
+    return parts + [value.astype(jnp.bfloat16)]
+
+
+def deep(value):
+    return jnp.concatenate([value, jnp.zeros((DEEP - PAD, value.shape[1]), value.dtype)], axis=0)
+
+
+def apply(square, value):
+    high, middle, low = split(deep(value))
+    stack = jnp.concatenate([high, middle, high, low, middle, high], axis=0)
+    return jnp.dot(square, stack, preferred_element_type=jnp.float32)[0:PAD]
+
+
+def spread(square):
+    size = DEEP - square.shape[0]
+    square = jnp.pad(square, ((0, size), (0, size)))
+    high = lax.reduce_precision(square, 8, 7)
+    middle = lax.reduce_precision(square - high, 8, 7)
+    low = square - high - middle
+    return jnp.concatenate([high, high, middle, high, middle, low], axis=1).astype(jnp.bfloat16)
+
+
+def outer(left, right):
+    left = jnp.concatenate(split(deep(left)), axis=0)
+    right = jnp.concatenate(split(deep(right)), axis=0)
+    full = lax.dot_general(
+        left, right, (((1,), (1,)), ((), ())), preferred_element_type=jnp.float32
+    )
+    total = None
+    for i in range(3):
+        for j in range(3 - i):
+            term = full[i * DEEP : i * DEEP + PAD, j * DEEP : j * DEEP + PAD]
+            total = term if total is None else total + term
+    return total
 
 
 def merge(parts):
@@ -117,30 +175,15 @@
 
     for group in range(REACH):
         step = group + 1
-        for a in range(-REACH, REACH + 1):
-            total = plus(
-                total, weight(y, 8 * group + a + REACH) * turned[group, y + a + REACH]
-            )
-        total = total + weight(y, 8 * group + 7) * field[y + step + REACH]
-        total = total + weight(y - step, 8 * group + 7) * field[y - step + REACH]
-    for group in range(REACH):
         back = None
         for a in range(-REACH, REACH + 1):
-            back = plus(
-                back, weight(y - a, 8 * group + a + REACH) * field[y - a + REACH]
-            )
-        total = total + shifted(back, -(group + 1))
+            at = 8 * group + a + REACH
+            total = plus(total, weight(y, at) * turned[group, y + a])
+            back = plus(back, weight(y - a, at) * field[y - a])
+        total = total + weight(y, 8 * group + 7) * field[y + step]
+        total = total + weight(y - step, 8 * group + 7) * field[y - step]
+        total = total + shifted(back, -step)
     return total
-
-
-def turn(field, turned, low, high):
-    def body(row, carry):
-        value = field[row]
-        for group in range(REACH):
-            turned[group, row] = shifted(value, group + 1)
-        return carry
-
-    lax.fori_loop(low, high, body, 0)
 
 
 def softmax(value):
@@ -153,7 +196,7 @@
     place, compat, compat_t, centre, first, second, from_left, from_right,
     feat_out, kern_out, prob0_out, prob1_out, grad1_out, grad0_out, unary_out, share,
     feat, feat_turned, norm, norm_turned, kern, unary, grad, prob0, prob1, grad1, grad0,
-    turned, message0, message1, logit,
+    turned, message0, message1, logit1, logit0,
 ):
     height = centre.shape[0]
     rows = height + 2 * HALO
@@ -207,20 +250,19 @@
         row = place[3] + y
         return inside_lane & (row >= 0) & (row < place[4])
 
-    def turn_feat(row, carry):
+    def turn_feat(row):
         value = feat[row]
         size = fold(value * value) * 0.5
         norm[row] = size
         for group in range(REACH):
             feat_turned[group, row] = shifted(value, group + 1)
             norm_turned[group, row] = shifted(size, group + 1)
-        return carry
-
-    lax.fori_loop(0, rows + 2 * REACH, turn_feat, 0)
+
+    each_row(0, rows + 2 * REACH, 2, turn_feat)
 
     sub = sublane()
 
-    def affinity_row(y, carry):
+    def affinity_row(y):
         for tile in range(2):
             cols = pl.ds(128 * tile, 128)
             here = feat[y + REACH, :, cols]
@@ -240,90 +282,65 @@
                 kern[y, pl.ds(8 * group, 8), cols] = jnp.exp(
                     merge(parts) - far * (1.0 / (2.0 * REACH * REACH))
                 )
-        return carry
-
-    lax.fori_loop(0, rows, affinity_row, 0)
-
-    for ref in (prob0, prob1, grad1, grad0):
-        ref[...] = jnp.zeros_like(ref)
-
-    def start(y, carry):
-        prob0[y + REACH] = jnp.where(inside(y), softmax(unary[y]), 0.0)
-        return carry
-
-    lax.fori_loop(0, rows, start, 0)
+
+    each_row(0, rows, 1, affinity_row)
+
+    def put_field(field, y, value):
+        field[y] = value
+        for group in range(REACH):
+            turned[group, y] = shifted(value, group + 1)
+
+    def start(y):
+        put_field(prob0, y, jnp.where(inside(y), softmax(unary[y]), 0.0))
+
+    each_row(0, rows, 4, start)
 
     def run_pass(field, out, low, high):
-        turn(field, turned, low, high + 2 * REACH)
-
-        def body(y, carry):
+        def body(y):
             out[y] = pass_row(y, kern, field, turned)
-            return carry
-
-        lax.fori_loop(low, high, body, 0)
-
-    def dot(left, right):
-        return jnp.dot(left, right, precision=HIGH, preferred_element_type=jnp.float32)
-
-    def outer(left, right):
-        return lax.dot_general(
-            left, right, (((1,), (1,)), ((), ())), precision=HIGH,
-            preferred_element_type=jnp.float32,
-        )
+
+        each_row(low, high, 2, body)
 
     run_pass(prob0, message0, REACH, rows - REACH)
 
-    def mix(y, carry):
-        prob1[y + REACH] = jnp.where(
-            inside(y), softmax(unary[y] - dot(compat[...], message0[y])), 0.0
-        )
-        return carry
-
-    lax.fori_loop(REACH, rows - REACH, mix, 0)
+    def mix(y):
+        value = softmax(unary[y] - apply(compat[...], message0[y]))
+        put_field(prob1, y, jnp.where(inside(y), value, 0.0))
+
+    each_row(REACH, rows - REACH, 4, mix)
     run_pass(prob1, message1, 2 * REACH, rows - 2 * REACH)
 
-    def back1(y, carry):
-        prob = softmax(unary[y] - dot(compat[...], message1[y]))
+    def back1(y):
+        prob = softmax(unary[y] - apply(compat[...], message1[y]))
         cot = grad[y]
         change = prob * (cot - jnp.sum(cot * prob, axis=0, keepdims=True))
-        logit[y] = change
-        grad1[y + REACH] = jnp.where(inside(y), -dot(compat_t[...], change), 0.0)
-        return carry
-
-    lax.fori_loop(2 * REACH, rows - 2 * REACH, back1, 0)
+        logit1[y] = change
+        put_field(grad1, y, jnp.where(inside(y), -apply(compat_t[...], change), 0.0))
+
+    each_row(2 * REACH, rows - 2 * REACH, 4, back1)
     total = jnp.zeros((PAD, PAD), jnp.float32)
 
-    def add_share(message):
-        def body(y, carry):
-            return carry - outer(logit[y, :, 0:128], message[y, :, 0:128])
+    def add_share(change, message):
+        def body(turn, carry):
+            at = HALO + 4 * turn
+            left = jnp.concatenate([change[at + i, :, 0:128] for i in range(4)], axis=1)
+            right = jnp.concatenate([message[at + i, :, 0:128] for i in range(4)], axis=1)
+            return carry - outer(left, right)
 
         return body
 
-    total = lax.fori_loop(HALO, HALO + height, add_share(message1), total)
-
-    def keep(y, carry):
-        unary_out[y - HALO] = logit[y, :, 0:128]
-        return carry
-
-    lax.fori_loop(HALO, HALO + height, keep, 0)
+    total = lax.fori_loop(0, height // 4, add_share(logit1, message1), total)
     run_pass(grad1, message1, 3 * REACH, rows - 3 * REACH)
 
-    def back0(y, carry):
-        prob = prob1[y + REACH]
+    def back0(y):
+        prob = prob1[y]
         cot = message1[y]
         change = prob * (cot - jnp.sum(cot * prob, axis=0, keepdims=True))
-        logit[y] = change
-        grad0[y + REACH] = jnp.where(inside(y), -dot(compat_t[...], change), 0.0)
-        return carry
-
-    lax.fori_loop(3 * REACH, rows - 3 * REACH, back0, 0)
-    total = lax.fori_loop(HALO, HALO + height, add_share(message0), total)
-
-    def keep0(y, carry):
-        unary_out[y - HALO] += logit[y, :, 0:128]
-        return carry
-
-    lax.fori_loop(HALO, HALO + height, keep0, 0)
+        logit0[y] = change
+        grad0[y] = jnp.where(inside(y), -apply(compat_t[...], change), 0.0)
+
+    each_row(3 * REACH, rows - 3 * REACH, 4, back0)
+    total = lax.fori_loop(0, height // 4, add_share(logit0, message0), total)
 
     total = jnp.concatenate([total, jnp.zeros((PAD, 128 - PAD), jnp.float32)], axis=1)
     packed = (
@@ -336,17 +353,21 @@
 
     near = height + 2 * REACH
 
-    def copy(row, carry):
-        at = row + HALO
-        feat_out[row] = feat[at]
+    def copy(row):
+        at = row + HALO - REACH
+        feat_out[row] = feat[at + REACH]
         prob0_out[row] = prob0[at]
         prob1_out[row] = prob1[at]
         grad1_out[row] = grad1[at]
         grad0_out[row] = grad0[at]
-        kern_out[row] = kern[at - REACH]
-        return carry
-
-    lax.fori_loop(0, near, copy, 0)
+        kern_out[row] = kern[at]
+
+    each_row(0, near, 2, copy)
+
+    def add_logit(y):
+        unary_out[y] = logit0[y + HALO, :, 0:128] + logit1[y + HALO, :, 0:128]
+
+    each_row(0, height, 4, add_logit)
 
 
 def iterate(place, compat, centre, first, second, from_left, from_right, devices):
@@ -381,21 +402,13 @@
             room(REACH, tall, channels, 256),
             room(tall, 8, 256),
             room(REACH, tall, 8, 256),
-            room(rows, PAD, 256),
-            room(rows, PAD, 256),
-            room(rows, PAD, 256),
-            room(tall, PAD, 256),
-            room(tall, PAD, 256),
-            room(tall, PAD, 256),
-            room(tall, PAD, 256),
-            room(REACH, tall, PAD, 256),
-            room(rows, PAD, 256),
-            room(rows, PAD, 256),
-            room(rows, PAD, 256),
+            *[room(rows, PAD, 256)] * 7,
+            room(REACH, rows, PAD, 256),
+            *[room(rows, PAD, 256)] * 4,
         ],
         compiler_params=params(),
         name="iterate",
-    )(place, compat, compat.T, centre, first, second, from_left, from_right)
+    )(place, spread(compat), spread(compat.T), centre, first, second, from_left, from_right)
 
 
 def finish_kernel(
@@ -429,7 +442,7 @@
     lax.fori_loop(0, near, prepare, 0)
 
     def unary_row(y, carry):
-        cot = pass_row(y + REACH, kern, _Offset(grad0), _Offset(turned, 1))[:, 0:128]
+        cot = pass_row(y + REACH, kern, grad0, turned)[:, 0:128]
         prob = prob0[y + REACH, :, 0:128]
         value = partial[y] + prob * (cot - jnp.sum(cot * prob, axis=0, keepdims=True))
         for start in range(0, classes, 8):
@@ -482,16 +495,6 @@
     lax.fori_loop(0, height, feature_row, 0)
 
 
-class _Offset:
-    def __init__(self, ref, axis=0):
-        self.ref, self.axis = ref, axis
-
-    def __getitem__(self, index):
-        if self.axis:
-            return self.ref[index[0], index[1] - REACH]
-        return self.ref[index - REACH]
-
-
 def finish(feat, kern, prob0, prob1, grad1, grad0, partial, classes):
     near, channels, _ = feat.shape
     height = partial.shape[0]
@@ -547,10 +550,9 @@
     place = jnp.stack(
         [1 - odd, col == 0, col == n_cols - 1, row * height - HALO, n_rows * height]
     ).astype(jnp.int32)
-    square = jnp.pad(compat, ((0, PAD - classes), (0, PAD - classes)))
     devices = n_rows * n_cols
     *fields, partial, share = iterate(
-        place, square, centre, first, second, from_left, from_right, devices
+        place, compat, centre, first, second, from_left, from_right, devices
     )
     shares = lax.all_to_all(share, ("rows", "cols"), 0, 0)
     unary_grad, feature_grad = finish(*fields, partial, classes)

time: 131 us -> 99.1 us (0.76)
  Pallas kernels: 87.6 us -> 55.9 us
    pallas_call x1, Pallas kernels: 67.4 us -> 36.1 us  [iterate(): pl.pallas_call(field_kernel, out_shape=(shape(near, channels, 256), shape...]
    concatenate x0 -> x2, local copies, waits for them, and re-layouts: none -> 1.39 us  [spread(): jnp.concatenate([high, high, middle, high, middle, low], axis=1)]
  transfers between devices with their start and end apart: 5 -> 5, of which waited for: 2 -> 2; matrix products, arithmetic and copies ran while one was open for 3% -> 4% of each run, Pallas kernels for 14% -> 17%
where the time goes in v2:
time: 99.1 us; the launch traced here: 98.8 us
  Pallas kernels  55.9 us (56%)
  waiting for transfers between devices  24.1 us (24%)
  starting transfers between devices  10.9 us (11%)
  local copies, waits for them, and re-layouts  5.44 us (5%)
  other arithmetic  1.73 us (2%)
    pallas_call x1, Pallas kernels, iterate(): pl.pallas_call(field_kernel, out_shape=(shape(near, channels, 256), shape...  36.1 us
    ppermute x1, waiting for transfers between devices, on_device(): second = lax.ppermute(jnp.where(odd == 0, top, bottom), 'rows', above)  20 us
    pallas_call x1, Pallas kernels, finish(): pl.pallas_call(finish_kernel, out_shape=(jax.ShapeDtypeStruct((classes *...  17.2 us
    ppermute x1, starting transfers between devices, on_device(): from_left = lax.ppermute(right, 'cols', forward)  4.92 us
    ppermute x1, waiting for transfers between devices, on_device(): from_right = lax.ppermute(left, 'cols', backward)  4.16 us
    all_to_all x1, starting transfers between devices, on_device(): shares = lax.all_to_all(share, ('rows', 'cols'), 0, 0)  3.13 us
    pallas_call x1, Pallas kernels, pack(): pl.pallas_call(pack_kernel, out_shape=(jax.ShapeDtypeStruct((height, dept...  2.55 us
    unnamed x11, local copies, waits for them, and re-layouts  2.01 us
  transfers between devices with their start and end apart: 5, of which 2 were waited for; matrix products, arithmetic and copies ran while one was open for 4% of the time, Pallas kernels for 17%

profile of v2, /device:TPU:0, one launch (start us, length us, event | category | flops | bytes accessed | tf_op | source)
XLA Modules:
  0.0 98.8 jit_solution(5670661809635006472)
XLA Ops:
  0.6 2.6 %pack.1 = (f32[16,112,128]{2,1,0:T(8,128)}, f32[2,112,128]{2,1,0:T(8,128)}, f32[2,112,128]{2,1,0:T(8,128)}) custom-call(bf16[64,16,128]{2,1,0:T(8,128)(2,1)} %feat.1, f32[336,128]{1,0:T(8,128)} %bitcast.9, f32[336,128]{1,0:T(8,128)} %bitcast.10), custom_call_target="tpu_custom_call" | custom-call | tf_op jit(solution)/shard_map/pack/pallas_call | solution.py:156
  3.2 4.9 %collective-permute-start = (f32[2,112,128]{2,1,0:T(8,128)}, f32[2,112,128]{2,1,0:T(8,128)S(1)}, u32[]{:S(2)}, u32[]{:S(2)}) collective-permute-start(f32[2,112,128]{2,1,0:T(8,128)} %get-tuple-element.17), channel_id=1, source_target_pairs={{0,1},{1,2},{2,3},{4,5},{5,6},{6,7},{8,9},{9,10},{10,11},{12,13},{... | collective-permute-start | bytes 344072 | tf_op jit(solution)/shard_map/ppermute | solution.py:535
  8.1 1.3 %collective-permute-start.1 = (f32[2,112,128]{2,1,0:T(8,128)}, f32[2,112,128]{2,1,0:T(8,128)S(1)}, u32[]{:S(2)}, u32[]{:S(2)}) collective-permute-start(f32[2,112,128]{2,1,0:T(8,128)} %get-tuple-element.18), channel_id=1, source_target_pairs={{1,0},{2,1},{3,2},{5,4},{6,5},{7,6},{9,8},{10,9},{11,10},{13,12},{... | collective-permute-start | bytes 344072 | tf_op jit(solution)/shard_map/ppermute | solution.py:536
  9.4 1.4 %fusion.4 = (f32[12,112,128]{2,1,0:T(8,128)S(1)}, f32[12,112,128]{2,1,0:T(8,128)S(1)}) fusion(f32[16,112,128]{2,1,0:T(8,128)} %get-tuple-element.16.centre), kind=kLoop, calls=%fused_computation.19 | loop fusion | bytes 2752512 | tf_op jit(solution)/shard_map/slice | solution.py:539
  10.8 0.0 collective-permute-done.from_left
  10.8 0.0 copy-start.2
  10.9 4.2 %collective-permute-done.1.from_right = f32[2,112,128]{2,1,0:T(8,128)S(1)} collective-permute-done((f32[2,112,128]{2,1,0:T(8,128)}, f32[2,112,128]{2,1,0:T(8,128)S(1)}, u32[]{:S(2)}, u32[]{:S(2)}) %collective-permute-start.1) | collective-permute-done | bytes 114720 | tf_op jit(solution)/shard_map/ppermute | solution.py:536
  15.0 0.0 copy-start.3
  15.0 0.0 copy-start.4
  15.0 1.1 %fusion = (f32[16,112,128]{2,1,0:T(8,128)}, f32[16,112,128]{2,1,0:T(8,128)S(1)}) fusion(f32[2,112,128]{2,1,0:T(8,128)S(1)} %collective-permute-done.1.from_right, f32[2,112,128]{2,1,0:T(8,128)S(1)} %collective-permute-done.from_left, f32[12,112,128]{2,1,0:T(8,128)S(1)} %get-tuple-element.32, f32[12,112,128]{2,1,0:T(8,128)S(1)} %get-tuple-element.31, pred[]{:T(512)S(6)} %eq.14), kind=kLoop, calls=%fused_computation.4 | loop fusion | flops 1376256 | bytes 3440641 | tf_op jit(solution)/shard_map/jit(_where)/select_n | solution.py:548
  16.1 0.0 copy-done.2
  16.1 0.0 copy-done.3
  16.1 0.5 collective-permute-start.3
  16.5 1.1 %collective-permute-start.2 = (f32[16,112,128]{2,1,0:T(8,128)S(1)}, f32[16,112,128]{2,1,0:T(8,128)S(1)}, u32[]{:S(2)}, u32[]{:S(2)}) collective-permute-start(f32[16,112,128]{2,1,0:T(8,128)S(1)} %get-tuple-element.30), channel_id=1, source_target_pairs={{0,4},{4,0},{8,12},{12,8},{16,20},{20,16},{24,28},{28,24},{1,5},{5... | collective-permute-start | bytes 2752520 | tf_op jit(solution)/shard_map/ppermute | solution.py:547
  17.7 0.0 copy-done.4
  17.7 0.1 copy.7
  17.8 0.7 concatenate.21.compat_t
  18.5 0.7 concatenate.20.compat
  19.2 0.6 stack.27.place
  19.8 20.0 %collective-permute-done.3.second = f32[16,112,128]{2,1,0:T(8,128)S(1)} collective-permute-done((f32[16,112,128]{2,1,0:T(8,128)}, f32[16,112,128]{2,1,0:T(8,128)S(1)}, u32[]{:S(2)}, u32[]{:S(2)}) %collective-permute-start.3) | collective-permute-done | bytes 917536 | tf_op jit(solution)/shard_map/ppermute | solution.py:548
  39.7 0.0 copy-start
  39.7 0.0 collective-permute-done.2.first
  39.7 0.9 copy-done
  40.7 0.0 copy-start.1
  40.7 0.9 copy-done.1
  41.6 36.1 %iterate.1 = (f32[22,64,256]{2,1,0:T(8,128)}, f32[22,24,256]{2,1,0:T(8,128)}, f32[22,24,256]{2,1,0:T(8,128)}, f32[22,24,256]{2,1,0:T(8,128)}, f32[22,24,256]{2,1...) custom-call(s32[5]{0:T(128)} %stack.27.place, ...), custom_call_target="tpu_custom_call" | custom-call | tf_op jit(solution)/shard_map/iterate/pallas_call | solution.py:386
  77.7 3.1 %all-to-all-start = ((f32[32,8,128]{2,1,0:T(8,128)}), f32[32,8,128]{2,1,0:T(8,128)S(1)}, u32[]{:S(2)}, u32[]{:S(2)}) async-start(f32[32,8,128]{2,1,0:T(8,128)} %get-tuple-element.28), calls=%async_computation | async-start | bytes 262144 | tf_op jit(solution)/shard_map/all_to_all | solution.py:557
  80.9 17.2 %finish.1 = (f32[336,128]{1,0:T(8,128)}, f32[1024,128]{1,0:T(8,128)}) custom-call(f32[22,64,256]{2,1,0:T(8,128)} %get-tuple-element.19.feat, f32[22,24,256]{2,1,0:T(8,128)} %get-tuple-element.20.kern, f32[22,24,256]{2,1,0:T(8,128)} %get-tuple-element.21.prob0, f32[22,24,256]{2,1,0:T(8,128)} %get-tuple-element.22.prob1, ...), custom_call_target="tpu_custom_call" | custom-call | flops 200000000 | bytes 8000000 | tf_op jit(solution)/shard_map/finish/pallas_call | solution.py:505
  98.1 0.0 all-to-all-done
  98.1 0.1 fusion.5
  98.2 0.6 pad_maximum_fusion.4
  (4 shorter events, 0.1 us)
Async XLA Ops:
  3.2 7.6 %collective-permute-start = (f32[2,112,128]{2,1,0:T(8,128)}, f32[2,112,128]{2,1,0:T(8,128)S(1)}, u32[]{:S(2)}, u32[]{:S(2)}) collective-permute-start(f32[2,112,128]{2,1,0:T(8,128)} %get-tuple-element.17), channel_id=1, source_target_pairs={{0,1},{1,2},{2,3},{4,5},{5,6},{6,7},{8,9},{9,10},{10,11},{12,13},{... | collective-permute-start | bytes 344072 | tf_op jit(solution)/shard_map/ppermute | solution.py:535
  8.1 6.9 %collective-permute-start.1 = (f32[2,112,128]{2,1,0:T(8,128)}, f32[2,112,128]{2,1,0:T(8,128)S(1)}, u32[]{:S(2)}, u32[]{:S(2)}) collective-permute-start(f32[2,112,128]{2,1,0:T(8,128)} %get-tuple-element.18), channel_id=1, source_target_pairs={{1,0},{2,1},{3,2},{5,4},{6,5},{7,6},{9,8},{10,9},{11,10},{13,12},{... | collective-permute-start | bytes 344072 | tf_op jit(solution)/shard_map/ppermute | solution.py:536
  10.8 5.2 %copy-start.2 = (f32[2,112,128]{2,1,0:T(8,128)}, f32[2,112,128]{2,1,0:T(8,128)S(1)}, u32[]{:S(2)}) copy-start(f32[2,112,128]{2,1,0:T(8,128)S(1)} %collective-permute-done.from_left) | copy-start | bytes 344068
  15.0 1.1 %copy-start.3 = (f32[2,112,128]{2,1,0:T(8,128)}, f32[2,112,128]{2,1,0:T(8,128)S(1)}, u32[]{:S(2)}) copy-start(f32[2,112,128]{2,1,0:T(8,128)S(1)} %collective-permute-done.1.from_right) | copy-start | bytes 344068
  15.0 2.7 %copy-start.4 = (f32[21,21]{1,0:T(8,128)S(1)}, f32[21,21]{1,0:T(8,128)}, u32[]{:S(2)}) copy-start(f32[21,21]{1,0:T(8,128)} %param.6) | copy-start | bytes 5296
  16.1 23.7 %collective-permute-start.3 = (f32[16,112,128]{2,1,0:T(8,128)}, f32[16,112,128]{2,1,0:T(8,128)S(1)}, u32[]{:S(2)}, u32[]{:S(2)}) collective-permute-start(f32[16,112,128]{2,1,0:T(8,128)} %get-tuple-element.29), channel_id=1, source_target_pairs={{4,8},{8,4},{12,16},{16,12},{20,24},{24,20},{28,0},{0,28},{5,9},{9... | collective-permute-start | bytes 2752520 | tf_op jit(solution)/shard_map/ppermute | solution.py:548
  16.5 23.2 %collective-permute-start.2 = (f32[16,112,128]{2,1,0:T(8,128)S(1)}, f32[16,112,128]{2,1,0:T(8,128)S(1)}, u32[]{:S(2)}, u32[]{:S(2)}) collective-permute-start(f32[16,112,128]{2,1,0:T(8,128)S(1)} %get-tuple-element.30), channel_id=1, source_target_pairs={{0,4},{4,0},{8,12},{12,8},{16,20},{20,16},{24,28},{28,24},{1,5},{5... | collective-permute-start | bytes 2752520 | tf_op jit(solution)/shard_map/ppermute | solution.py:547
  39.7 1.0 copy-start
  40.7 1.0 copy-start.1
  77.7 20.4 %all-to-all-start = ((f32[32,8,128]{2,1,0:T(8,128)}), f32[32,8,128]{2,1,0:T(8,128)S(1)}, u32[]{:S(2)}, u32[]{:S(2)}) async-start(f32[32,8,128]{2,1,0:T(8,128)} %get-tuple-element.28), calls=%async_computation | async-start | bytes 262144 | tf_op jit(solution)/shard_map/all_to_all | solution.py:557

commit v3 on v2

--- a/solution.py
+++ b/solution.py
@@ -115,7 +115,9 @@
     return total
 
 
-def pack_kernel(feat, unary, grad, centre, left, right, wide):
+def pack_kernel(
+    place, feat, unary, grad, centre, left, right, inner, outer_feat, outer_rest, wide
+):
     channels, height, _ = feat.shape
     classes = unary.shape[0] // height
     wide[...] = feat[...].astype(jnp.float32).reshape(channels * height, 128) * (
@@ -147,21 +149,72 @@
     for slot in range(height // 8):
         left[slot] = ends[0][slot]
         right[slot] = ends[1][slot]
-
-
-def pack(feat, unary, grad):
+    even = place[0] == 1
+    low = height - HALO
+    inner_base = jnp.where(even, low, 0)
+    outer_base = jnp.where(even, 0, low)
+    grad_base = jnp.where(even, 0, height - HALO // 2)
+    for i in range(HALO):
+        inner[i] = centre[inner_base + i]
+        outer_feat[i] = centre[outer_base + i, 0:channels].astype(jnp.bfloat16)
+        outer_rest[i] = centre[outer_base + i, channels : channels + PAD]
+    for i in range(HALO // 2):
+        outer_rest[HALO + i] = centre[grad_base + i, channels + PAD :]
+
+
+def pack(place, feat, unary, grad):
     channels, height, _ = feat.shape
     depth = channels + 2 * PAD
-    strips = jax.ShapeDtypeStruct((height // 8, depth, 128), jnp.float32)
+
+    def shape(*dims, dtype=jnp.float32):
+        return jax.ShapeDtypeStruct(dims, dtype)
+
     return pl.pallas_call(
         pack_kernel,
-        out_shape=(jax.ShapeDtypeStruct((height, depth, 128), jnp.float32), strips, strips),
-        in_specs=[VMEM] * 3,
-        out_specs=(VMEM,) * 3,
+        out_shape=(
+            shape(height, depth, 128),
+            shape(height // 8, depth, 128),
+            shape(height // 8, depth, 128),
+            shape(HALO, depth, 128),
+            shape(HALO, channels, 128, dtype=jnp.bfloat16),
+            shape(HALO + HALO // 2, PAD, 128),
+        ),
+        in_specs=[SMEM] + [VMEM] * 3,
+        out_specs=(VMEM,) * 6,
         scratch_shapes=[pltpu.VMEM((channels * height, 128), jnp.float32)],
         compiler_params=params(),
         name="pack",
-    )(feat, unary.reshape(-1, 128), grad.reshape(-1, 128))
+    )(place, feat, unary.reshape(-1, 128), grad.reshape(-1, 128))
+
+
+def corner_kernel(place, left, right, inner, outer):
+    depth = left.shape[1]
+    short = depth - PAD
+    even = place[0] == 1
+    side = lane()
+    for out, top in ((inner, jnp.logical_not(even)), (outer, even)):
+        whole = jnp.where(top, 0, 1)
+        out[pl.ds(0, depth)] = left[whole]
+        out[pl.ds(depth, depth)] = right[whole]
+        mine = (side < 64) == top
+        out[pl.ds(2 * depth, short)] = jnp.where(
+            mine,
+            left[1 - whole, 0:short],
+            pltpu.roll(right[1 - whole, 0:short], 64, axis=1),
+        )
+
+
+def corners(place, left, right):
+    depth = left.shape[1]
+    out = jax.ShapeDtypeStruct((3 * depth - PAD, 128), jnp.float32)
+    return pl.pallas_call(
+        corner_kernel,
+        out_shape=(out, out),
+        in_specs=[SMEM] + [VMEM] * 2,
+        out_specs=(VMEM,) * 2,
+        compiler_params=params(),
+        name="corners",
+    )(place, left, right)
 
 
 def pass_row(y, kern, field, turned):
@@ -193,8 +246,8 @@
 
 
 def field_kernel(
-    place, compat, compat_t, centre, first, second, from_left, from_right,
-    feat_out, kern_out, prob0_out, prob1_out, grad1_out, grad0_out, unary_out, share,
+    place, compat, compat_t, centre, inner, outer_feat, outer_rest, inner_corner, outer_corner,
+    from_left, from_right, feat_out, kern_out, prob0_out, prob1_out, grad1_out, grad0_out, unary_out, share,
     feat, feat_turned, norm, norm_turned, kern, unary, grad, prob0, prob1, grad1, grad0,
     turned, message0, message1, logit1, logit0,
 ):
@@ -206,38 +259,57 @@
     feat[pl.ds(0, REACH)] = jnp.zeros((REACH,) + feat.shape[1:], jnp.float32)
     feat[pl.ds(rows + REACH, REACH)] = jnp.zeros((REACH,) + feat.shape[1:], jnp.float32)
 
-    def put(row, main, left, right, slot):
-        moved_right = pltpu.roll(right, (128 - slot * STRIP) % 128, axis=1)
-        moved_left = pltpu.roll(left, (128 - STRIP - slot * STRIP) % 128, axis=1)
+    def put(row, main, left, left_at, right, right_at):
+        moved_right = pltpu.roll(right, (128 - right_at) % 128, axis=1)
+        moved_left = pltpu.roll(left, (128 - STRIP - left_at) % 128, axis=1)
         edge = jnp.where(side < 64, moved_right, moved_left)
-        feat[row + REACH, :, 0:128] = main[0:channels]
-        feat[row + REACH, :, 128:256] = edge[0:channels]
-        unary[row, :, 0:128] = main[channels : channels + PAD]
-        unary[row, :, 128:256] = edge[channels : channels + PAD]
-        grad[row, :, 0:128] = main[channels + PAD :]
-        grad[row, :, 128:256] = edge[channels + PAD :]
+        for value, cols in ((main, slice(0, 128)), (edge, slice(128, 256))):
+            feat[row + REACH, :, cols] = value[0:channels]
+            unary[row, :, cols] = value[channels : channels + PAD]
+            if value.shape[0] > channels + PAD:
+                grad[row, :, cols] = value[channels + PAD :]
 
     for y in range(height):
-        put(HALO + y, centre[y], from_left[y // 8], from_right[y // 8], y % 8)
-    strips = height // 8
-    for source, above in ((first, place[0] == 0), (second, place[0] == 1)):
-        base = jnp.where(above, 0, HALO + height)
-        for y in range(HALO):
-            gap = height - HALO
-
-            @pl.when(above)
-            def _(y=y, source=source):
-                at = y + gap
-                put(
-                    y, source[y], source[HALO + at // 8], source[HALO + strips + at // 8], at % 8
-                )
-
-            @pl.when(jnp.logical_not(above))
-            def _(y=y, source=source):
-                put(
-                    HALO + height + y, source[y], source[HALO + y // 8],
-                    source[HALO + strips + y // 8], y % 8,
-                )
+        at = (y % 8) * STRIP
+        put(HALO + y, centre[y], from_left[y // 8], at, from_right[y // 8], at)
+
+    depth = channels + 2 * PAD
+    short = channels + PAD
+    near = HALO // 2
+
+    def put_inner(i, top):
+        return inner[i]
+
+    def put_outer(i, top):
+        parts = [outer_feat[i].astype(jnp.float32), outer_rest[i]]
+        row = i if top else i - near
+        if 0 <= row < near:
+            parts.append(outer_rest[HALO + row])
+        return jnp.concatenate(parts, axis=0)
+
+    def put_rows(main, corner, top):
+        base = HALO + height if top else 0
+        half = HALO - 8
+        for i in range(HALO):
+            at = (i if top else i - half) * STRIP
+            if 0 <= at < 128:
+                left, right = corner[pl.ds(0, depth)], corner[pl.ds(depth, depth)]
+                left_at = right_at = at
+            else:
+                left = right = corner[pl.ds(2 * depth, short)]
+                left_at = (i - 8) * STRIP if top else 64 + i * STRIP
+                right_at = (left_at + 64) % 128
+            rows_main = main(i, top)
+            size = min(rows_main.shape[0], left.shape[0])
+            put(base + i, rows_main[0:size], left[0:size], left_at, right[0:size], right_at)
+
+    even = place[0] == 1
+    for main, corner, below in (
+        (put_inner, inner_corner, even),
+        (put_outer, outer_corner, jnp.logical_not(even)),
+    ):
+        pl.when(below)(functools.partial(put_rows, main, corner, True))
+        pl.when(jnp.logical_not(below))(functools.partial(put_rows, main, corner, False))
 
     wide_lane = lane(256)
     inside_lane = (
@@ -351,8 +423,6 @@
     for slot in range(share.shape[0]):
         share[slot] = packed
 
-    near = height + 2 * REACH
-
     def copy(row):
         at = row + HALO - REACH
         feat_out[row] = feat[at + REACH]
@@ -362,7 +432,7 @@
         grad0_out[row] = grad0[at]
         kern_out[row] = kern[at]
 
-    each_row(0, near, 2, copy)
+    each_row(0, height + 2 * REACH, 2, copy)
 
     def add_logit(y):
         unary_out[y] = logit0[y + HALO, :, 0:128] + logit1[y + HALO, :, 0:128]
@@ -370,7 +440,7 @@
     each_row(0, height, 4, add_logit)
 
 
-def iterate(place, compat, centre, first, second, from_left, from_right, devices):
+def iterate(place, compat, centre, received, devices):
     height, depth, _ = centre.shape
     channels = depth - 2 * PAD
     rows = height + 2 * HALO
@@ -395,7 +465,7 @@
             shape(height, PAD, 128),
             shape(devices, 8, 128),
         ),
-        in_specs=[SMEM] + [VMEM] * 7,
+        in_specs=[SMEM] + [VMEM] * 10,
         out_specs=(VMEM,) * 8,
         scratch_shapes=[
             room(tall, channels, 256),
@@ -408,7 +478,7 @@
         ],
         compiler_params=params(),
         name="iterate",
-    )(place, spread(compat), spread(compat.T), centre, first, second, from_left, from_right)
+    )(place, spread(compat), spread(compat.T), centre, *received)
 
 
 def finish_kernel(
@@ -529,30 +599,36 @@
     row, col = lax.axis_index("rows"), lax.axis_index("cols")
     odd = row % 2
 
-    centre, left, right = pack(features, unary, grad_output)
-    forward = [(i, i + 1) for i in range(n_cols - 1)]
-    backward = [(i + 1, i) for i in range(n_cols - 1)]
-    from_left = lax.ppermute(right, "cols", forward)
-    from_right = lax.ppermute(left, "cols", backward)
-    strips = jnp.concatenate([from_left, from_right], axis=0)
-
-    top = jnp.concatenate([centre[:HALO], strips], axis=0)
-    bottom = jnp.concatenate([centre[height - HALO :], strips], axis=0)
+    place = jnp.stack(
+        [1 - odd, col == 0, col == n_cols - 1, row * height - HALO, n_rows * height]
+    ).astype(jnp.int32)
+
     below = [pair for i in range(0, n_rows, 2) for pair in ((i, i + 1), (i + 1, i))]
     above = [
         pair
         for i in range(1, n_rows, 2)
         for pair in ((i, (i + 1) % n_rows), ((i + 1) % n_rows, i))
     ]
-    first = lax.ppermute(jnp.where(odd == 0, bottom, top), "rows", below)
-    second = lax.ppermute(jnp.where(odd == 0, top, bottom), "rows", above)
-
-    place = jnp.stack(
-        [1 - odd, col == 0, col == n_cols - 1, row * height - HALO, n_rows * height]
-    ).astype(jnp.int32)
+    forward = [(i, i + 1) for i in range(n_cols - 1)]
+    backward = [(i + 1, i) for i in range(n_cols - 1)]
+    centre, left, right, inner, outer_feat, outer_rest = pack(
+        place, features, unary, grad_output
+    )
+    from_left = lax.ppermute(right, "cols", forward)
+    from_right = lax.ppermute(left, "cols", backward)
+    outer_feat = lax.ppermute(outer_feat, "rows", above)
+    outer_rest = lax.ppermute(outer_rest, "rows", above)
+    inner = lax.ppermute(inner, "rows", below)
+    inner_corner, outer_corner = corners(place, from_left, from_right)
+    outer_corner = lax.ppermute(outer_corner, "rows", above)
+    inner_corner = lax.ppermute(inner_corner, "rows", below)
+    received = (
+        inner, outer_feat, outer_rest, inner_corner, outer_corner, from_left, from_right
+    )
+
     devices = n_rows * n_cols
     *fields, partial, share = iterate(
-        place, compat, centre, first, second, from_left, from_right, devices
+        place, compat, centre, received, devices
     )
     shares = lax.all_to_all(share, ("rows", "cols"), 0, 0)
     unary_grad, feature_grad = finish(*fields, partial, classes)

time: 99.1 us -> 86.9 us (0.88)
  waiting for transfers between devices: 24.1 us -> 5.53 us
  starting transfers between devices: 10.9 us -> 17.8 us
    ppermute x2 -> x5, waiting for transfers between devices: 20 us -> 2.97 us  [the longest x1 2.96 us: on_device(): outer_corner = lax.ppermute(outer_corner, 'rows', above)]
    ppermute x2 -> x5, starting transfers between devices: 1.61 us -> 5.71 us  [the longest x1 2.56 us: on_device(): outer_corner = lax.ppermute(outer_corner, 'rows', above)]
    all_to_all x1, starting transfers between devices: 3.13 us -> 6.33 us  [on_device(): shares = lax.all_to_all(share, ('rows', 'cols'), 0, 0)]
    pallas_call x1 -> x2, Pallas kernels: 2.55 us -> 4.97 us  [the longest x1 3.21 us: pack(): pl.pallas_call(pack_kernel, out_shape=(shape(height, depth, 128), shape(h...]
    pallas_call x1, Pallas kernels: 36.1 us -> 34.4 us  [iterate(): pl.pallas_call(field_kernel, out_shape=(shape(near, channels, 256), shape...]
    ppermute x1, waiting for transfers between devices: 4.16 us -> 2.56 us  [on_device(): from_right = lax.ppermute(left, 'cols', backward)]
    slice x1 -> x0, local copies, waits for them, and re-layouts: 1.4 us -> none  [on_device(): top = jnp.concatenate([centre[:HALO], strips], axis=0)]
    select_n x1 -> x0, other arithmetic: 1.05 us -> none  [on_device(): second = lax.ppermute(jnp.where(odd == 0, top, bottom), 'rows', above)]
  transfers between devices with their start and end apart: 5 -> 8, of which waited for: 2 -> 2; matrix products, arithmetic and copies ran while one was open for 4% -> 3% of each run, Pallas kernels for 17% -> 22%
where the time goes in v3:
time: 86.9 us; the launch traced here: 86.5 us
  Pallas kernels  56.6 us (65%)
  starting transfers between devices  17.8 us (20%)
  waiting for transfers between devices  5.53 us (6%)
  local copies, waits for them, and re-layouts  4.46 us (5%)
  other arithmetic  1.38 us (2%)
    pallas_call x1, Pallas kernels, iterate(): pl.pallas_call(field_kernel, out_shape=(shape(near, channels, 256), shape...  34.4 us
    pallas_call x1, Pallas kernels, finish(): pl.pallas_call(finish_kernel, out_shape=(jax.ShapeDtypeStruct((classes *...  17.2 us
    all_to_all x1, starting transfers between devices, on_device(): shares = lax.all_to_all(share, ('rows', 'cols'), 0, 0)  6.33 us
    ppermute x1, starting transfers between devices, on_device(): from_left = lax.ppermute(right, 'cols', forward)  4.5 us
    pallas_call x1, Pallas kernels, pack(): pl.pallas_call(pack_kernel, out_shape=(shape(height, depth, 128), shape(h...  3.21 us
    ppermute x1, waiting for transfers between devices, on_device(): outer_corner = lax.ppermute(outer_corner, 'rows', above)  2.96 us
    ppermute x1, starting transfers between devices, on_device(): outer_corner = lax.ppermute(outer_corner, 'rows', above)  2.56 us
    ppermute x1, waiting for transfers between devices, on_device(): from_right = lax.ppermute(left, 'cols', backward)  2.56 us
  transfers between devices with their start and end apart: 8, of which 2 were waited for; matrix products, arithmetic and copies ran while one was open for 3% of the time, Pallas kernels for 22%

profile of v3, /device:TPU:0, one launch (start us, length us, event | category | flops | bytes accessed | tf_op | source)
XLA Modules:
  0.0 86.5 jit_solution(11039931178744855395)
XLA Ops:
  0.6 0.7 stack.27.place
  1.3 3.2 %pack.1 = (f32[16,112,128]{2,1,0:T(8,128)}, f32[2,112,128]{2,1,0:T(8,128)}, f32[2,112,128]{2,1,0:T(8,128)}, f32[12,112,128]{2,1,0:T(8,128)}, bf16[12,64,128]{2,1,0:T(8,128)(2,1)}, /*index=5*/f32[18,24,128]{2,1,0:T(8,128)}) custom-call(s32[5]{0:T(128)} %stack.27.place, bf16[64,16,128]{2,1,0:T(8,128)(2,1)} %feat.1, f32[336,128]{1,0:T(8,128)} %bitcast.9, ...), custom_call_target="tpu_custom_call" | custom-call | tf_op jit(solution)/shard_map/pack/pallas_call | solution.py:172
  4.5 0.4 collective-permute-start
  5.0 4.5 %collective-permute-start.3 = (f32[2,112,128]{2,1,0:T(8,128)}, f32[2,112,128]{2,1,0:T(8,128)S(1)}, u32[]{:S(2)}, u32[]{:S(2)}) collective-permute-start(f32[2,112,128]{2,1,0:T(8,128)} %get-tuple-element.25), channel_id=1, source_target_pairs={{0,1},{1,2},{2,3},{4,5},{5,6},{6,7},{8,9},{9,10},{10,11},{12,13},{... | collective-permute-start | bytes 344072 | tf_op jit(solution)/shard_map/ppermute | solution.py:617
  9.5 1.3 %collective-permute-start.4 = (f32[2,112,128]{2,1,0:T(8,128)}, f32[2,112,128]{2,1,0:T(8,128)S(1)}, u32[]{:S(2)}, u32[]{:S(2)}) collective-permute-start(f32[2,112,128]{2,1,0:T(8,128)} %get-tuple-element.26), channel_id=1, source_target_pairs={{1,0},{2,1},{3,2},{5,4},{6,5},{7,6},{9,8},{10,9},{11,10},{13,12},{... | collective-permute-start | bytes 344072 | tf_op jit(solution)/shard_map/ppermute | solution.py:618
  10.8 2.3 %collective-permute-start.1 = (bf16[12,64,128]{2,1,0:T(8,128)(2,1)}, bf16[12,64,128]{2,1,0:T(8,128)(2,1)S(1)}, u32[]{:S(2)}, u32[]{:S(2)}) collective-permute-start(bf16[12,64,128]{2,1,0:T(8,128)(2,1)} %get-tuple-element.23), channel_id=1, source_target_pairs={{4,8},{8,4},{12,16},{16,12},{20,24},{24,20},{28,0},{0,28},{5,9},{9... | collective-permute-start | bytes 589832 | tf_op jit(solution)/shard_map/ppermute | solution.py:619
  13.1 0.4 collective-permute-start.2
  13.5 0.8 copy.7
  14.3 0.0 collective-permute-done.3.left.from_left
  14.3 0.0 copy-start.1
  14.3 2.6 %collective-permute-done.4.right.from_right = f32[2,112,128]{2,1,0:T(8,128)S(1)} collective-permute-done((f32[2,112,128]{2,1,0:T(8,128)}, f32[2,112,128]{2,1,0:T(8,128)S(1)}, u32[]{:S(2)}, u32[]{:S(2)}) %collective-permute-start.4) | collective-permute-done | bytes 114720 | tf_op jit(solution)/shard_map/ppermute | solution.py:618
  16.8 0.0 copy-done.1
  16.8 0.0 copy-start.2
  16.8 0.6 copy-done.2
  17.5 1.8 %corners.1 = (f32[312,128]{1,0:T(8,128)}, f32[312,128]{1,0:T(8,128)}) custom-call(s32[5]{0:T(128)} %stack.27.place, f32[2,112,128]{2,1,0:T(8,128)} %copy-done.1, f32[2,112,128]{2,1,0:T(8,128)} %copy-done.2), custom_call_target="tpu_custom_call" | custom-call | tf_op jit(solution)/shard_map/corners/pallas_call | solution.py:210
  19.2 0.0 collective-permute-start.5
  19.2 2.6 %collective-permute-start.6 = (f32[312,128]{1,0:T(8,128)}, f32[312,128]{1,0:T(8,128)S(1)}, u32[]{:S(2)}, u32[]{:S(2)}) collective-permute-start(f32[312,128]{1,0:T(8,128)} %get-tuple-element.28), channel_id=1, source_target_pairs={{4,8},{8,4},{12,16},{16,12},{20,24},{24,20},{28,0},{0,28},{5,9},{9... | collective-permute-start | bytes 479240 | tf_op jit(solution)/shard_map/ppermute | solution.py:623
  21.8 0.7 concatenate.12.compat_t
  22.5 0.7 fusion
  23.2 0.7 concatenate.11.compat
  23.9 0.0 collective-permute-done.1.outer_feat
  23.9 0.0 copy-start.4
  23.9 0.0 collective-permute-done.2.outer_rest
  23.9 0.0 copy-start.3
  23.9 0.0 collective-permute-done.5.inner_corner
  24.0 0.0 copy-start.5
  24.0 3.0 %collective-permute-done.6.outer_corner = f32[312,128]{1,0:T(8,128)S(1)} collective-permute-done((f32[312,128]{1,0:T(8,128)}, f32[312,128]{1,0:T(8,128)S(1)}, u32[]{:S(2)}, u32[]{:S(2)}) %collective-permute-start.6) | collective-permute-done | bytes 159776 | tf_op jit(solution)/shard_map/ppermute | solution.py:623
  26.9 0.0 copy-start.6
  26.9 0.0 collective-permute-done.inner
  26.9 0.0 copy-start
  26.9 0.0 copy-done.4
  26.9 0.0 copy-done.3
  26.9 0.0 copy-done.5
  27.0 0.6 copy-done.6
  27.6 0.3 copy-done
  27.8 34.4 %iterate.1 = (f32[22,64,256]{2,1,0:T(8,128)}, f32[22,24,256]{2,1,0:T(8,128)}, f32[22,24,256]{2,1,0:T(8,128)}, f32[22,24,256]{2,1,0:T(8,128)}, f32[22,24,256]{2,1...) custom-call(s32[5]{0:T(128)} %stack.27.place, ...), custom_call_target="tpu_custom_call" | custom-call | tf_op jit(solution)/shard_map/iterate/pallas_call | solution.py:456
  62.2 6.3 %all-to-all-start = ((f32[32,8,128]{2,1,0:T(8,128)}), f32[32,8,128]{2,1,0:T(8,128)S(1)}, u32[]{:S(2)}, u32[]{:S(2)}) async-start(f32[32,8,128]{2,1,0:T(8,128)} %get-tuple-element.38), calls=%async_computation | async-start | bytes 262144 | tf_op jit(solution)/shard_map/all_to_all | solution.py:633
  68.6 17.2 %finish.1 = (f32[336,128]{1,0:T(8,128)}, f32[1024,128]{1,0:T(8,128)}) custom-call(f32[22,64,256]{2,1,0:T(8,128)} %get-tuple-element.29.feat, f32[22,24,256]{2,1,0:T(8,128)} %get-tuple-element.30.kern, f32[22,24,256]{2,1,0:T(8,128)} %get-tuple-element.31.prob0, f32[22,24,256]{2,1,0:T(8,128)} %get-tuple-element.32.prob1, ...), custom_call_target="tpu_custom_call" | custom-call | flops 200000000 | bytes 8000000 | tf_op jit(solution)/shard_map/finish/pallas_call | solution.py:575
  85.8 0.0 all-to-all-done
  85.8 0.1 fusion.2
  85.9 0.6 pad_maximum_fusion
  (3 shorter events, 0.1 us)
Async XLA Ops:
  4.5 22.4 %collective-permute-start = (f32[12,112,128]{2,1,0:T(8,128)}, f32[12,112,128]{2,1,0:T(8,128)S(1)}, u32[]{:S(2)}, u32[]{:S(2)}) collective-permute-start(f32[12,112,128]{2,1,0:T(8,128)} %get-tuple-element.22), channel_id=1, source_target_pairs={{0,4},{4,0},{8,12},{12,8},{16,20},{20,16},{24,28},{28,24},{1,5},{5... | collective-permute-start | bytes 2064392 | tf_op jit(solution)/shard_map/ppermute | solution.py:621
  5.0 9.3 %collective-permute-start.3 = (f32[2,112,128]{2,1,0:T(8,128)}, f32[2,112,128]{2,1,0:T(8,128)S(1)}, u32[]{:S(2)}, u32[]{:S(2)}) collective-permute-start(f32[2,112,128]{2,1,0:T(8,128)} %get-tuple-element.25), channel_id=1, source_target_pairs={{0,1},{1,2},{2,3},{4,5},{5,6},{6,7},{8,9},{9,10},{10,11},{12,13},{... | collective-permute-start | bytes 344072 | tf_op jit(solution)/shard_map/ppermute | solution.py:617
  9.5 7.4 %collective-permute-start.4 = (f32[2,112,128]{2,1,0:T(8,128)}, f32[2,112,128]{2,1,0:T(8,128)S(1)}, u32[]{:S(2)}, u32[]{:S(2)}) collective-permute-start(f32[2,112,128]{2,1,0:T(8,128)} %get-tuple-element.26), channel_id=1, source_target_pairs={{1,0},{2,1},{3,2},{5,4},{6,5},{7,6},{9,8},{10,9},{11,10},{13,12},{... | collective-permute-start | bytes 344072 | tf_op jit(solution)/shard_map/ppermute | solution.py:618
  10.8 13.2 %collective-permute-start.1 = (bf16[12,64,128]{2,1,0:T(8,128)(2,1)}, bf16[12,64,128]{2,1,0:T(8,128)(2,1)S(1)}, u32[]{:S(2)}, u32[]{:S(2)}) collective-permute-start(bf16[12,64,128]{2,1,0:T(8,128)(2,1)} %get-tuple-element.23), channel_id=1, source_target_pairs={{4,8},{8,4},{12,16},{16,12},{20,24},{24,20},{28,0},{0,28},{5,9},{9... | collective-permute-start | bytes 589832 | tf_op jit(solution)/shard_map/ppermute | solution.py:619
  13.1 10.8 %collective-permute-start.2 = (f32[18,24,128]{2,1,0:T(8,128)}, f32[18,24,128]{2,1,0:T(8,128)S(1)}, u32[]{:S(2)}, u32[]{:S(2)}) collective-permute-start(f32[18,24,128]{2,1,0:T(8,128)} %get-tuple-element.24), channel_id=1, source_target_pairs={{4,8},{8,4},{12,16},{16,12},{20,24},{24,20},{28,0},{0,28},{5,9},{9... | collective-permute-start | bytes 663560 | tf_op jit(solution)/shard_map/ppermute | solution.py:620
  14.3 2.6 %copy-start.1 = (f32[2,112,128]{2,1,0:T(8,128)}, f32[2,112,128]{2,1,0:T(8,128)S(1)}, u32[]{:S(2)}) copy-start(f32[2,112,128]{2,1,0:T(8,128)S(1)} %collective-permute-done.3.left.from_left) | copy-start | bytes 344068
  16.8 0.7 copy-start.2
  19.2 4.7 %collective-permute-start.5 = (f32[312,128]{1,0:T(8,128)}, f32[312,128]{1,0:T(8,128)S(1)}, u32[]{:S(2)}, u32[]{:S(2)}) collective-permute-start(f32[312,128]{1,0:T(8,128)} %get-tuple-element.27), channel_id=1, source_target_pairs={{0,4},{4,0},{8,12},{12,8},{16,20},{20,16},{24,28},{28,24},{1,5},{5... | collective-permute-start | bytes 479240 | tf_op jit(solution)/shard_map/ppermute | solution.py:624
  19.2 7.7 %collective-permute-start.6 = (f32[312,128]{1,0:T(8,128)}, f32[312,128]{1,0:T(8,128)S(1)}, u32[]{:S(2)}, u32[]{:S(2)}) collective-permute-start(f32[312,128]{1,0:T(8,128)} %get-tuple-element.28), channel_id=1, source_target_pairs={{4,8},{8,4},{12,16},{16,12},{20,24},{24,20},{28,0},{0,28},{5,9},{9... | collective-permute-start | bytes 479240 | tf_op jit(solution)/shard_map/ppermute | solution.py:623
  23.9 3.0 %copy-start.4 = (bf16[12,64,128]{2,1,0:T(8,128)(2,1)}, bf16[12,64,128]{2,1,0:T(8,128)(2,1)S(1)}, u32[]{:S(2)}) copy-start(bf16[12,64,128]{2,1,0:T(8,128)(2,1)S(1)} %collective-permute-done.1.outer_feat) | copy-start | bytes 589828
  23.9 3.0 %copy-start.3 = (f32[18,24,128]{2,1,0:T(8,128)}, f32[18,24,128]{2,1,0:T(8,128)S(1)}, u32[]{:S(2)}) copy-start(f32[18,24,128]{2,1,0:T(8,128)S(1)} %collective-permute-done.2.outer_rest) | copy-start | bytes 663556
  24.0 3.0 %copy-start.5 = (f32[312,128]{1,0:T(8,128)}, f32[312,128]{1,0:T(8,128)S(1)}, u32[]{:S(2)}) copy-start(f32[312,128]{1,0:T(8,128)S(1)} %collective-permute-done.5.inner_corner) | copy-start | bytes 479236
  26.9 0.7 copy-start.6
  26.9 0.9 %copy-start = (f32[12,112,128]{2,1,0:T(8,128)}, f32[12,112,128]{2,1,0:T(8,128)S(1)}, u32[]{:S(2)}) copy-start(f32[12,112,128]{2,1,0:T(8,128)S(1)} %collective-permute-done.inner) | copy-start | bytes 2064388
  62.2 23.6 %all-to-all-start = ((f32[32,8,128]{2,1,0:T(8,128)}), f32[32,8,128]{2,1,0:T(8,128)S(1)}, u32[]{:S(2)}, u32[]{:S(2)}) async-start(f32[32,8,128]{2,1,0:T(8,128)} %get-tuple-element.38), calls=%async_computation | async-start | bytes 262144 | tf_op jit(solution)/shard_map/all_to_all | solution.py:633

commit v4 on v3

--- a/solution.py
+++ b/solution.py
@@ -16,11 +16,21 @@
 DEEP = 32
 LOW = -1e30
 VMEM = pl.BlockSpec(memory_space=pltpu.VMEM)
-SMEM = pl.BlockSpec(memory_space=pltpu.SMEM)
 
 
 def params():
     return pltpu.CompilerParams(vmem_limit_bytes=56 * 1024 * 1024)
+
+
+def position(height):
+    row, col = lax.axis_index("rows"), lax.axis_index("cols")
+    return (
+        row % 2 == 0,
+        col > 0,
+        col < lax.axis_size("cols") - 1,
+        row * height - HALO,
+        lax.axis_size("rows") * height,
+    )
 
 
 def sublane(width=128):
@@ -38,6 +48,14 @@
     low = pltpu.roll(low, (-step) % 128, axis=1)
     high = pltpu.roll(high, (-step) % 128, axis=1)
     return jnp.concatenate([jnp.where(here, low, high), jnp.where(here, high, low)], axis=1)
+
+
+def turns(steps, width):
+    source = lax.broadcasted_iota(jnp.int32, (256, width), 0)
+    target = lax.broadcasted_iota(jnp.int32, (256, width), 1)
+    return jnp.concatenate(
+        [(source == (target + step) % 256).astype(jnp.bfloat16) for step in steps], axis=1
+    )
 
 
 def each_row(low, high, step, body):
@@ -116,7 +134,7 @@
 
 
 def pack_kernel(
-    place, feat, unary, grad, centre, left, right, inner, outer_feat, outer_rest, wide
+    feat, unary, grad, centre, left, right, inner, outer_feat, outer_rest, wide
 ):
     channels, height, _ = feat.shape
     classes = unary.shape[0] // height
@@ -125,31 +143,28 @@
     )
     empty = jnp.zeros((PAD - classes, 128), jnp.float32)
     side = lane()
-    ends = [[], []]
-    for y in range(height):
-        rows = jnp.concatenate(
-            [
-                wide[pl.ds(y, channels, stride=height), :],
-                unary[pl.ds(y, classes, stride=height), :],
-                empty + LOW,
-                grad[pl.ds(y, classes, stride=height), :],
-                empty,
-            ],
-            axis=0,
-        )
-        centre[y] = rows
-        at = (y % 8) * STRIP
-        here = (side >= at) & (side < at + STRIP)
-        for end, shift in ((0, at), (1, (at + STRIP) % 128)):
-            moved = pltpu.roll(rows, shift, axis=1)
-            if y % 8 == 0:
-                ends[end].append(moved)
-            else:
-                ends[end][-1] = jnp.where(here, moved, ends[end][-1])
     for slot in range(height // 8):
-        left[slot] = ends[0][slot]
-        right[slot] = ends[1][slot]
-    even = place[0] == 1
+        ends = [None, None]
+        for i in range(8):
+            y = 8 * slot + i
+            rows = jnp.concatenate(
+                [
+                    wide[pl.ds(y, channels, stride=height), :],
+                    unary[pl.ds(y, classes, stride=height), :],
+                    empty + LOW,
+                    grad[pl.ds(y, classes, stride=height), :],
+                    empty,
+                ],
+                axis=0,
+            )
+            centre[y] = rows
+            at = i * STRIP
+            here = (side >= at) & (side < at + STRIP)
+            for end, shift in ((0, at), (1, (at + STRIP) % 128)):
+                moved = pltpu.roll(rows, shift, axis=1)
+                ends[end] = moved if i == 0 else jnp.where(here, moved, ends[end])
+        left[slot], right[slot] = ends
+    even = position(height)[0]
     low = height - HALO
     inner_base = jnp.where(even, low, 0)
     outer_base = jnp.where(even, 0, low)
@@ -162,7 +177,7 @@
         outer_rest[HALO + i] = centre[grad_base + i, channels + PAD :]
 
 
-def pack(place, feat, unary, grad):
+def pack(feat, unary, grad):
     channels, height, _ = feat.shape
     depth = channels + 2 * PAD
 
@@ -179,18 +194,18 @@
             shape(HALO, channels, 128, dtype=jnp.bfloat16),
             shape(HALO + HALO // 2, PAD, 128),
         ),
-        in_specs=[SMEM] + [VMEM] * 3,
+        in_specs=[VMEM] * 3,
         out_specs=(VMEM,) * 6,
         scratch_shapes=[pltpu.VMEM((channels * height, 128), jnp.float32)],
         compiler_params=params(),
         name="pack",
-    )(place, feat, unary.reshape(-1, 128), grad.reshape(-1, 128))
-
-
-def corner_kernel(place, left, right, inner, outer):
+    )(feat, unary.reshape(-1, 128), grad.reshape(-1, 128))
+
+
+def corner_kernel(left, right, _, inner, outer):
     depth = left.shape[1]
     short = depth - PAD
-    even = place[0] == 1
+    even = position(8 * left.shape[0])[0]
     side = lane()
     for out, top in ((inner, jnp.logical_not(even)), (outer, even)):
         whole = jnp.where(top, 0, 1)
@@ -204,17 +219,17 @@
         )
 
 
-def corners(place, left, right):
+def corners(left, right, earlier):
     depth = left.shape[1]
     out = jax.ShapeDtypeStruct((3 * depth - PAD, 128), jnp.float32)
     return pl.pallas_call(
         corner_kernel,
         out_shape=(out, out),
-        in_specs=[SMEM] + [VMEM] * 2,
+        in_specs=[VMEM, VMEM, pl.BlockSpec(memory_space=pl.ANY)],
         out_specs=(VMEM,) * 2,
         compiler_params=params(),
         name="corners",
-    )(place, left, right)
+    )(left, right, earlier)
 
 
 def pass_row(y, kern, field, turned):
@@ -246,10 +261,10 @@
 
 
 def field_kernel(
-    place, compat, compat_t, centre, inner, outer_feat, outer_rest, inner_corner, outer_corner,
+    compat, compat_t, centre, inner, outer_feat, outer_rest, inner_corner, outer_corner,
     from_left, from_right, feat_out, kern_out, prob0_out, prob1_out, grad1_out, grad0_out, unary_out, share,
     feat, feat_turned, norm, norm_turned, kern, unary, grad, prob0, prob1, grad1, grad0,
-    turned, message0, message1, logit1, logit0,
+    turned, message0, message1, logit1, logit0, turner,
 ):
     height = centre.shape[0]
     rows = height + 2 * HALO
@@ -303,7 +318,7 @@
             size = min(rows_main.shape[0], left.shape[0])
             put(base + i, rows_main[0:size], left[0:size], left_at, right[0:size], right_at)
 
-    even = place[0] == 1
+    even, has_left, has_right, first_row, all_rows = position(height)
     for main, corner, below in (
         (put_inner, inner_corner, even),
         (put_outer, outer_corner, jnp.logical_not(even)),
@@ -314,23 +329,37 @@
     wide_lane = lane(256)
     inside_lane = (
         (wide_lane < 128)
-        | ((wide_lane < 192) & (place[2] == 0))
-        | ((wide_lane >= 192) & (place[1] == 0))
+        | ((wide_lane < 192) & has_right)
+        | ((wide_lane >= 192) & has_left)
     )
 
     def inside(y):
-        row = place[3] + y
-        return inside_lane & (row >= 0) & (row < place[4])
-
-    def turn_feat(row):
+        row = first_row + y
+        return inside_lane & (row >= 0) & (row < all_rows)
+
+    turner[...] = turns(range(1, REACH + 1), 256)
+    block = (rows + 2 * REACH) // 2
+
+    def turn_feat(at):
+        value = feat[pl.ds(at * block, block)].reshape(block * channels, 256)
+        moved = jnp.dot(
+            value.astype(jnp.bfloat16), turner[...], preferred_element_type=jnp.float32
+        )
+        for group in range(REACH):
+            feat_turned[group, pl.ds(at * block, block)] = moved[
+                :, 256 * group : 256 * group + 256
+            ].reshape(block, channels, 256)
+
+    each_row(0, (rows + 2 * REACH) // block, 1, turn_feat)
+
+    def turn_norm(row):
         value = feat[row]
         size = fold(value * value) * 0.5
         norm[row] = size
         for group in range(REACH):
-            feat_turned[group, row] = shifted(value, group + 1)
             norm_turned[group, row] = shifted(size, group + 1)
 
-    each_row(0, rows + 2 * REACH, 2, turn_feat)
+    each_row(0, rows + 2 * REACH, 6, turn_norm)
 
     sub = sublane()
 
@@ -425,7 +454,7 @@
 
     def copy(row):
         at = row + HALO - REACH
-        feat_out[row] = feat[at + REACH]
+        feat_out[row] = feat[at + REACH].astype(jnp.bfloat16)
         prob0_out[row] = prob0[at]
         prob1_out[row] = prob1[at]
         grad1_out[row] = grad1[at]
@@ -440,7 +469,7 @@
     each_row(0, height, 4, add_logit)
 
 
-def iterate(place, compat, centre, received, devices):
+def iterate(compat, centre, received, devices):
     height, depth, _ = centre.shape
     channels = depth - 2 * PAD
     rows = height + 2 * HALO
@@ -456,7 +485,7 @@
     return pl.pallas_call(
         field_kernel,
         out_shape=(
-            shape(near, channels, 256),
+            jax.ShapeDtypeStruct((near, channels, 256), jnp.bfloat16),
             shape(near, PAD, 256),
             shape(near, PAD, 256),
             shape(near, PAD, 256),
@@ -465,7 +494,7 @@
             shape(height, PAD, 128),
             shape(devices, 8, 128),
         ),
-        in_specs=[SMEM] + [VMEM] * 10,
+        in_specs=[VMEM] * 10,
         out_specs=(VMEM,) * 8,
         scratch_shapes=[
             room(tall, channels, 256),
@@ -475,15 +504,16 @@
             *[room(rows, PAD, 256)] * 7,
             room(REACH, rows, PAD, 256),
             *[room(rows, PAD, 256)] * 4,
+            pltpu.VMEM((256, REACH * 256), jnp.bfloat16),
         ],
         compiler_params=params(),
         name="iterate",
-    )(place, spread(compat), spread(compat.T), centre, *received)
+    )(spread(compat), spread(compat.T), centre, *received)
 
 
 def finish_kernel(
     feat, kern, prob0, prob1, grad1, grad0, partial, unary_out, feat_out,
-    feat_turned, all_turned, turned, kern_back, weights,
+    feat_turned, all_turned, kern_back, weights, turner,
 ):
     height = partial.shape[0]
     near = height + 2 * REACH
@@ -491,28 +521,60 @@
     classes = unary_out.shape[0] // height
     steps = range(-REACH, REACH + 1)
 
-    def prepare(row, carry):
-        value = feat[row]
-        for b in steps:
-            feat_turned[b + REACH, row] = shifted(value, b)[:, 0:128] if b else value[:, 0:128]
+    turner[...] = turns(steps, 128)
+    block = near // 2
+    column = lane()
+
+    def moved(main, edge, b):
+        if b == 0:
+            return main
+        mixed = jnp.where((column < b) if b > 0 else (column >= 128 + b), edge, main)
+        return pltpu.roll(mixed, (-b) % 128, axis=1)
+
+    def prepare_feat(at):
+        value = feat[pl.ds(at * block, block)].reshape(block * channels, 256)
+        full = jnp.dot(value, turner[...], preferred_element_type=jnp.float32)
+        for place in range(len(steps)):
+            feat_turned[place, pl.ds(at * block, block)] = full[
+                :, 128 * place : 128 * place + 128
+            ].reshape(block, channels, 128)
+
+    each_row(0, near // block, 1, prepare_feat)
+
+    def prepare(row):
         for place, field in enumerate((prob0, prob1, grad1, grad0)):
-            value = field[row]
+            main, edge = field[row, :, 0:128], field[row, :, 128:256]
             for b in steps:
-                moved = shifted(value, b) if b else value
-                all_turned[b + REACH, row, pl.ds(place * PAD, PAD), :] = moved[:, 0:128]
-                if field is grad0 and b > 0:
-                    turned[b - 1, row] = moved
+                all_turned[b + REACH, row, pl.ds(place * PAD, PAD), :] = moved(main, edge, b)
         for group in range(REACH):
-            value = kern[row, pl.ds(8 * group, 8), :]
-            kern_back[row, pl.ds(8 * group, 8), :] = jnp.where(
-                sublane() == 7, value[:, 0:128], shifted(value, -(group + 1))[:, 0:128]
+            rows = pl.ds(8 * group, 8)
+            main, edge = kern[row, rows, 0:128], kern[row, rows, 128:256]
+            kern_back[row, rows, :] = jnp.where(
+                sublane() == 7, main, moved(main, edge, -(group + 1))
             )
-        return carry
-
-    lax.fori_loop(0, near, prepare, 0)
-
-    def unary_row(y, carry):
-        cot = pass_row(y + REACH, kern, grad0, turned)[:, 0:128]
+
+    each_row(0, near, 2, prepare)
+
+    def pass_centre(y):
+        total = jnp.zeros((PAD, 128), jnp.float32)
+        last = pl.ds(3 * PAD, PAD)
+        for group in range(REACH):
+            step = group + 1
+            back = [jnp.zeros((PAD, 128), jnp.float32)] * 2
+            for a in range(-REACH, REACH + 1):
+                one = pl.ds(8 * group + a + REACH, 1)
+                total = total + kern[y, one, 0:128] * all_turned[step + REACH, y + a, last, :]
+                for tile in range(2):
+                    cols = slice(128 * tile, 128 * tile + 128)
+                    back[tile] = back[tile] + kern[y - a, one, cols] * grad0[y - a, :, cols]
+            one = pl.ds(8 * group + 7, 1)
+            total = total + kern[y, one, 0:128] * grad0[y + step, :, 0:128]
+            total = total + kern[y - step, one, 0:128] * grad0[y - step, :, 0:128]
+            total = total + moved(back[0], back[1], -step)
+        return total
+
+    def unary_row(y):
+        cot = pass_centre(y + REACH)
         prob = prob0[y + REACH, :, 0:128]
         value = partial[y] + prob * (cot - jnp.sum(cot * prob, axis=0, keepdims=True))
         for start in range(0, classes, 8):
@@ -520,12 +582,11 @@
             unary_out[pl.ds(start * height + y, size, stride=height), :] = value[
                 start : start + size
             ]
-        return carry
-
-    lax.fori_loop(0, height, unary_row, 0)
+
+    each_row(0, height, 2, unary_row)
     sub = sublane()
 
-    def feature_row(y, carry):
+    def feature_row(y):
         row = y + REACH
         own = all_turned[REACH, row]
         mate = jnp.concatenate(
@@ -560,9 +621,8 @@
         whole = jnp.sum(whole, axis=0, keepdims=True)
         total = total - whole * feat_turned[REACH, row]
         feat_out[pl.ds(y, channels, stride=height), :] = total * (1.0 / math.sqrt(channels))
-        return carry
-
-    lax.fori_loop(0, height, feature_row, 0)
+
+    each_row(0, height, 1, feature_row)
 
 
 def finish(feat, kern, prob0, prob1, grad1, grad0, partial, classes):
@@ -583,9 +643,9 @@
         scratch_shapes=[
             room(2 * REACH + 1, near, channels, 128),
             room(2 * REACH + 1, near, 4 * PAD, 128),
-            room(REACH, near, PAD, 256),
             room(near, PAD, 128),
             room(height, 6 * 8, 128),
+            pltpu.VMEM((256, (2 * REACH + 1) * 128), jnp.bfloat16),
         ],
         compiler_params=params(),
         cost_estimate=pl.CostEstimate(flops=200_000_000, bytes_accessed=8_000_000, transcendentals=0),
@@ -596,12 +656,6 @@
 def on_device(unary, features, compat, grad_output):
     classes, height, width = unary.shape
     n_rows, n_cols = lax.axis_size("rows"), lax.axis_size("cols")
-    row, col = lax.axis_index("rows"), lax.axis_index("cols")
-    odd = row % 2
-
-    place = jnp.stack(
-        [1 - odd, col == 0, col == n_cols - 1, row * height - HALO, n_rows * height]
-    ).astype(jnp.int32)
 
     below = [pair for i in range(0, n_rows, 2) for pair in ((i, i + 1), (i + 1, i))]
     above = [
@@ -611,15 +665,13 @@
     ]
     forward = [(i, i + 1) for i in range(n_cols - 1)]
     backward = [(i + 1, i) for i in range(n_cols - 1)]
-    centre, left, right, inner, outer_feat, outer_rest = pack(
-        place, features, unary, grad_output
-    )
+    centre, left, right, inner, outer_feat, outer_rest = pack(features, unary, grad_output)
+    inner = lax.ppermute(inner, "rows", below)
+    outer_feat = lax.ppermute(outer_feat, "rows", above)
+    outer_rest = lax.ppermute(outer_rest, "rows", above)
     from_left = lax.ppermute(right, "cols", forward)
     from_right = lax.ppermute(left, "cols", backward)
-    outer_feat = lax.ppermute(outer_feat, "rows", above)
-    outer_rest = lax.ppermute(outer_rest, "rows", above)
-    inner = lax.ppermute(inner, "rows", below)
-    inner_corner, outer_corner = corners(place, from_left, from_right)
+    inner_corner, outer_corner = corners(from_left, from_right, outer_feat)
     outer_corner = lax.ppermute(outer_corner, "rows", above)
     inner_corner = lax.ppermute(inner_corner, "rows", below)
     received = (
@@ -628,7 +680,7 @@
 
     devices = n_rows * n_cols
     *fields, partial, share = iterate(
-        place, compat, centre, received, devices
+        compat, centre, received, devices
     )
     shares = lax.all_to_all(share, ("rows", "cols"), 0, 0)
     unary_grad, feature_grad = finish(*fields, partial, classes)

time: 86.9 us -> 78.8 us (0.907)
  Pallas kernels: 56.6 us -> 50.2 us
  starting transfers between devices: 17.8 us -> 12.4 us
  waiting for transfers between devices: 5.53 us -> 10.7 us
    pallas_call x1, Pallas kernels: 17.2 us -> 12.7 us  [finish(): pl.pallas_call(finish_kernel, out_shape=(jax.ShapeDtypeStruct((classes *...]
    all_to_all x1, starting transfers between devices: 6.33 us -> 2.95 us  [on_device(): shares = lax.all_to_all(share, ('rows', 'cols'), 0, 0)]
    ppermute x1, waiting for transfers between devices: 2.96 us -> 5.27 us  [on_device(): outer_corner = lax.ppermute(outer_corner, 'rows', above)]
    ppermute x1, starting transfers between devices: 2.56 us -> 0.65 us  [on_device(): outer_corner = lax.ppermute(outer_corner, 'rows', above)]
    pallas_call x2, Pallas kernels: 36.1 us -> 34.3 us  [the longest x1 32.5 us: iterate(): pl.pallas_call(field_kernel, out_shape=(jax.ShapeDtypeStruct((near, chann...]
    ppermute x1, waiting for transfers between devices: 2.56 us -> 4.23 us  [on_device(): from_right = lax.ppermute(left, 'cols', backward)]
    ppermute x1, starting transfers between devices: 2.33 us -> 3.57 us  [on_device(): outer_feat = lax.ppermute(outer_feat, 'rows', above)]
    ppermute x1, waiting for transfers between devices: 0.01 us -> 1.18 us  [on_device(): from_left = lax.ppermute(right, 'cols', forward)]
  transfers between devices with their start and end apart: 8 -> 8, of which waited for: 2 -> 3; matrix products, arithmetic and copies ran while one was open for 3% -> 2% of each run, Pallas kernels for 22% -> 18%
where the time goes in v4:
time: 78.8 us; the launch traced here: 78.5 us
  Pallas kernels  50.2 us (64%)
  starting transfers between devices  12.4 us (16%)
  waiting for transfers between devices  10.7 us (14%)
  local copies, waits for them, and re-layouts  3.75 us (5%)
    pallas_call x1, Pallas kernels, iterate(): pl.pallas_call(field_kernel, out_shape=(jax.ShapeDtypeStruct((near, chann...  32.5 us
    pallas_call x1, Pallas kernels, finish(): pl.pallas_call(finish_kernel, out_shape=(jax.ShapeDtypeStruct((classes *...  12.7 us
    ppermute x1, waiting for transfers between devices, on_device(): outer_corner = lax.ppermute(outer_corner, 'rows', above)  5.27 us
    ppermute x1, waiting for transfers between devices, on_device(): from_right = lax.ppermute(left, 'cols', backward)  4.23 us
    ppermute x1, starting transfers between devices, on_device(): outer_feat = lax.ppermute(outer_feat, 'rows', above)  3.57 us
    ppermute x1, starting transfers between devices, on_device(): from_left = lax.ppermute(right, 'cols', forward)  3.47 us
    pallas_call x1, Pallas kernels, pack(): pl.pallas_call(pack_kernel, out_shape=(shape(height, depth, 128), shape(h...  3.19 us
    all_to_all x1, starting transfers between devices, on_device(): shares = lax.all_to_all(share, ('rows', 'cols'), 0, 0)  2.95 us
  transfers between devices with their start and end apart: 8, of which 3 were waited for; matrix products, arithmetic and copies ran while one was open for 2% of the time, Pallas kernels for 18%

profile of v4, /device:TPU:0, one launch (start us, length us, event | category | flops | bytes accessed | tf_op | source)
XLA Modules:
  0.0 78.5 jit_solution(18067141681346527169)
XLA Ops:
  0.6 0.0 copy-start.7
  0.6 3.2 %pack.1 = (f32[16,112,128]{2,1,0:T(8,128)}, f32[2,112,128]{2,1,0:T(8,128)}, f32[2,112,128]{2,1,0:T(8,128)}, f32[12,112,128]{2,1,0:T(8,128)}, bf16[12,64,128]{2,1,0:T(8,128)(2,1)}, /*index=5*/f32[18,24,128]{2,1,0:T(8,128)}) custom-call(bf16[64,16,128]{2,1,0:T(8,128)(2,1)} %feat.1, f32[336,128]{1,0:T(8,128)} %bitcast.5, f32[336,128]{1,0:T(8,128)} %bitcast.6), custom_call_target="tpu_custom_call" | custom-call | tf_op jit(solution)/shard_map/pack/pallas_call | solution.py:187
  3.8 0.4 collective-permute-start
  4.3 3.6 %collective-permute-start.1 = (bf16[12,64,128]{2,1,0:T(8,128)(2,1)}, bf16[12,64,128]{2,1,0:T(8,128)(2,1)S(1)}, u32[]{:S(2)}, u32[]{:S(2)}) collective-permute-start(bf16[12,64,128]{2,1,0:T(8,128)(2,1)} %get-tuple-element.23), channel_id=1, source_target_pairs={{4,8},{8,4},{12,16},{16,12},{20,24},{24,20},{28,0},{0,28},{5,9},{9... | collective-permute-start | bytes 589832 | tf_op jit(solution)/shard_map/ppermute | solution.py:670
  7.8 3.5 %collective-permute-start.3 = (f32[2,112,128]{2,1,0:T(8,128)}, f32[2,112,128]{2,1,0:T(8,128)S(1)}, u32[]{:S(2)}, u32[]{:S(2)}) collective-permute-start(f32[2,112,128]{2,1,0:T(8,128)} %get-tuple-element.25), channel_id=1, source_target_pairs={{0,1},{1,2},{2,3},{4,5},{5,6},{6,7},{8,9},{9,10},{10,11},{12,13},{... | collective-permute-start | bytes 344072 | tf_op jit(solution)/shard_map/ppermute | solution.py:672
  11.3 1.3 %collective-permute-start.4 = (f32[2,112,128]{2,1,0:T(8,128)}, f32[2,112,128]{2,1,0:T(8,128)S(1)}, u32[]{:S(2)}, u32[]{:S(2)}) collective-permute-start(f32[2,112,128]{2,1,0:T(8,128)} %get-tuple-element.26), channel_id=1, source_target_pairs={{1,0},{2,1},{3,2},{5,4},{6,5},{7,6},{9,8},{10,9},{11,10},{13,12},{... | collective-permute-start | bytes 344072 | tf_op jit(solution)/shard_map/ppermute | solution.py:673
  12.6 0.1 collective-permute-start.2
  12.7 0.0 copy-done.7
  12.7 0.1 copy.7
  12.8 1.2 %collective-permute-done.3.left.from_left = f32[2,112,128]{2,1,0:T(8,128)S(1)} collective-permute-done((f32[2,112,128]{2,1,0:T(8,128)}, f32[2,112,128]{2,1,0:T(8,128)S(1)}, u32[]{:S(2)}, u32[]{:S(2)}) %collective-permute-start.3) | collective-permute-done | bytes 114720 | tf_op jit(solution)/shard_map/ppermute | solution.py:672
  14.0 0.0 copy-start.2
  14.0 4.2 %collective-permute-done.4.right.from_right = f32[2,112,128]{2,1,0:T(8,128)S(1)} collective-permute-done((f32[2,112,128]{2,1,0:T(8,128)}, f32[2,112,128]{2,1,0:T(8,128)S(1)}, u32[]{:S(2)}, u32[]{:S(2)}) %collective-permute-start.4) | collective-permute-done | bytes 114720 | tf_op jit(solution)/shard_map/ppermute | solution.py:673
  18.2 0.0 copy-start.3
  18.2 0.0 collective-permute-done.1._.outer_feat
  18.2 0.0 copy-done.2
  18.2 0.6 copy-done.3
  18.9 0.0 copy-start
  18.9 0.7 copy-done
  19.5 1.7 %corners.1 = (f32[312,128]{1,0:T(8,128)}, f32[312,128]{1,0:T(8,128)}) custom-call(f32[2,112,128]{2,1,0:T(8,128)} %copy-done.2, f32[2,112,128]{2,1,0:T(8,128)} %copy-done.3, bf16[12,64,128]{2,1,0:T(8,128)(2,1)} %copy-done), custom_call_target="tpu_custom_call" | custom-call | tf_op jit(solution)/shard_map/corners/pallas_call | solution.py:225
  21.3 0.0 collective-permute-start.5
  21.3 0.6 collective-permute-start.6
  21.9 0.7 concatenate.12.compat_t
  22.7 0.7 concatenate.11.compat
  23.4 0.0 collective-permute-done.2.outer_rest
  23.4 0.0 copy-start.4
  23.4 0.0 collective-permute-done.5.inner_corner
  23.4 0.0 copy-start.5
  23.4 5.3 %collective-permute-done.6.outer_corner = f32[312,128]{1,0:T(8,128)S(1)} collective-permute-done((f32[312,128]{1,0:T(8,128)}, f32[312,128]{1,0:T(8,128)S(1)}, u32[]{:S(2)}, u32[]{:S(2)}) %collective-permute-start.6) | collective-permute-done | bytes 159776 | tf_op jit(solution)/shard_map/ppermute | solution.py:675
  28.6 0.0 copy-start.6
  28.6 0.0 collective-permute-done.inner
  28.6 0.0 copy-start.1
  28.6 0.0 copy-done.4
  28.7 0.0 copy-done.5
  28.7 0.7 copy-done.6
  29.3 0.2 copy-done.1
  29.5 32.5 %iterate.1 = (bf16[22,64,256]{2,1,0:T(8,128)(2,1)}, f32[22,24,256]{2,1,0:T(8,128)}, f32[22,24,256]{2,1,0:T(8,128)}, f32[22,24,256]{2,1,0:T(8,128)}, f32[22,24,25...) custom-call(bf16[32,192]{1,0:T(8,128)(2,1)} %concatenate.11.compat, ...), custom_call_target="tpu_custom_call" | custom-call | tf_op jit(solution)/shard_map/iterate/pallas_call | solution.py:485
  62.1 2.9 %all-to-all-start = ((f32[32,8,128]{2,1,0:T(8,128)}), f32[32,8,128]{2,1,0:T(8,128)S(1)}, u32[]{:S(2)}, u32[]{:S(2)}) async-start(f32[32,8,128]{2,1,0:T(8,128)} %get-tuple-element.38), calls=%async_computation | async-start | bytes 262144 | tf_op jit(solution)/shard_map/all_to_all | solution.py:685
  65.0 12.7 %finish.1 = (f32[336,128]{1,0:T(8,128)}, f32[1024,128]{1,0:T(8,128)}) custom-call(bf16[22,64,256]{2,1,0:T(8,128)(2,1)} %get-tuple-element.29.feat, f32[22,24,256]{2,1,0:T(8,128)} %get-tuple-element.30.kern, f32[22,24,256]{2,1,0:T(8,128)} %get-tuple-element.31.prob0, f32[22,24,256]{2,1,0:T(8,128)} %get-tuple-element.32.prob1, ...), custom_call_target="tpu_custom_call" | custom-call | flops 200000000 | bytes 8000000 | tf_op jit(solution)/shard_map/finish/pallas_call | solution.py:635
  77.7 0.0 all-to-all-done
  77.8 0.1 fusion.2
  77.9 0.6 pad_maximum_fusion
  (4 shorter events, 0.1 us)
Async XLA Ops:
  0.6 12.1 %copy-start.7 = (f32[21,21]{1,0:T(8,128)S(1)}, f32[21,21]{1,0:T(8,128)}, u32[]{:S(2)}) copy-start(f32[21,21]{1,0:T(8,128)} %param.6) | copy-start | bytes 5296
  3.8 24.8 %collective-permute-start = (f32[12,112,128]{2,1,0:T(8,128)}, f32[12,112,128]{2,1,0:T(8,128)S(1)}, u32[]{:S(2)}, u32[]{:S(2)}) collective-permute-start(f32[12,112,128]{2,1,0:T(8,128)} %get-tuple-element.22), channel_id=1, source_target_pairs={{0,4},{4,0},{8,12},{12,8},{16,20},{20,16},{24,28},{28,24},{1,5},{5... | collective-permute-start | bytes 2064392 | tf_op jit(solution)/shard_map/ppermute | solution.py:669
  4.3 14.0 %collective-permute-start.1 = (bf16[12,64,128]{2,1,0:T(8,128)(2,1)}, bf16[12,64,128]{2,1,0:T(8,128)(2,1)S(1)}, u32[]{:S(2)}, u32[]{:S(2)}) collective-permute-start(bf16[12,64,128]{2,1,0:T(8,128)(2,1)} %get-tuple-element.23), channel_id=1, source_target_pairs={{4,8},{8,4},{12,16},{16,12},{20,24},{24,20},{28,0},{0,28},{5,9},{9... | collective-permute-start | bytes 589832 | tf_op jit(solution)/shard_map/ppermute | solution.py:670
  7.8 6.1 %collective-permute-start.3 = (f32[2,112,128]{2,1,0:T(8,128)}, f32[2,112,128]{2,1,0:T(8,128)S(1)}, u32[]{:S(2)}, u32[]{:S(2)}) collective-permute-start(f32[2,112,128]{2,1,0:T(8,128)} %get-tuple-element.25), channel_id=1, source_target_pairs={{0,1},{1,2},{2,3},{4,5},{5,6},{6,7},{8,9},{9,10},{10,11},{12,13},{... | collective-permute-start | bytes 344072 | tf_op jit(solution)/shard_map/ppermute | solution.py:672
  11.3 6.9 %collective-permute-start.4 = (f32[2,112,128]{2,1,0:T(8,128)}, f32[2,112,128]{2,1,0:T(8,128)S(1)}, u32[]{:S(2)}, u32[]{:S(2)}) collective-permute-start(f32[2,112,128]{2,1,0:T(8,128)} %get-tuple-element.26), channel_id=1, source_target_pairs={{1,0},{2,1},{3,2},{5,4},{6,5},{7,6},{9,8},{10,9},{11,10},{13,12},{... | collective-permute-start | bytes 344072 | tf_op jit(solution)/shard_map/ppermute | solution.py:673
  12.6 10.7 %collective-permute-start.2 = (f32[18,24,128]{2,1,0:T(8,128)}, f32[18,24,128]{2,1,0:T(8,128)S(1)}, u32[]{:S(2)}, u32[]{:S(2)}) collective-permute-start(f32[18,24,128]{2,1,0:T(8,128)} %get-tuple-element.24), channel_id=1, source_target_pairs={{4,8},{8,4},{12,16},{16,12},{20,24},{24,20},{28,0},{0,28},{5,9},{9... | collective-permute-start | bytes 663560 | tf_op jit(solution)/shard_map/ppermute | solution.py:671
  14.0 4.2 %copy-start.2 = (f32[2,112,128]{2,1,0:T(8,128)}, f32[2,112,128]{2,1,0:T(8,128)S(1)}, u32[]{:S(2)}) copy-start(f32[2,112,128]{2,1,0:T(8,128)S(1)} %collective-permute-done.3.left.from_left) | copy-start | bytes 344068
  18.2 0.6 copy-start.3
  18.9 0.7 copy-start
  21.3 2.1 %collective-permute-start.5 = (f32[312,128]{1,0:T(8,128)}, f32[312,128]{1,0:T(8,128)S(1)}, u32[]{:S(2)}, u32[]{:S(2)}) collective-permute-start(f32[312,128]{1,0:T(8,128)} %get-tuple-element.27), channel_id=1, source_target_pairs={{0,4},{4,0},{8,12},{12,8},{16,20},{20,16},{24,28},{28,24},{1,5},{5... | collective-permute-start | bytes 479240 | tf_op jit(solution)/shard_map/ppermute | solution.py:676
  21.3 7.4 %collective-permute-start.6 = (f32[312,128]{1,0:T(8,128)}, f32[312,128]{1,0:T(8,128)S(1)}, u32[]{:S(2)}, u32[]{:S(2)}) collective-permute-start(f32[312,128]{1,0:T(8,128)} %get-tuple-element.28), channel_id=1, source_target_pairs={{4,8},{8,4},{12,16},{16,12},{20,24},{24,20},{28,0},{0,28},{5,9},{9... | collective-permute-start | bytes 479240 | tf_op jit(solution)/shard_map/ppermute | solution.py:675
  23.4 5.3 %copy-start.4 = (f32[18,24,128]{2,1,0:T(8,128)}, f32[18,24,128]{2,1,0:T(8,128)S(1)}, u32[]{:S(2)}) copy-start(f32[18,24,128]{2,1,0:T(8,128)S(1)} %collective-permute-done.2.outer_rest) | copy-start | bytes 663556
  23.4 5.3 %copy-start.5 = (f32[312,128]{1,0:T(8,128)}, f32[312,128]{1,0:T(8,128)S(1)}, u32[]{:S(2)}) copy-start(f32[312,128]{1,0:T(8,128)S(1)} %collective-permute-done.5.inner_corner) | copy-start | bytes 479236
  28.6 0.7 copy-start.6
  28.6 0.9 %copy-start.1 = (f32[12,112,128]{2,1,0:T(8,128)}, f32[12,112,128]{2,1,0:T(8,128)S(1)}, u32[]{:S(2)}) copy-start(f32[12,112,128]{2,1,0:T(8,128)S(1)} %collective-permute-done.inner) | copy-start | bytes 2064388
  62.1 15.7 %all-to-all-start = ((f32[32,8,128]{2,1,0:T(8,128)}), f32[32,8,128]{2,1,0:T(8,128)S(1)}, u32[]{:S(2)}, u32[]{:S(2)}) async-start(f32[32,8,128]{2,1,0:T(8,128)} %get-tuple-element.38), calls=%async_computation | async-start | bytes 262144 | tf_op jit(solution)/shard_map/all_to_all | solution.py:685

commit v5 on v4

--- a/solution.py
+++ b/solution.py
@@ -65,7 +65,10 @@
         return carry
 
     turns = (high - low) // step
-    lax.fori_loop(0, turns, some, 0)
+    if turns > 1:
+        lax.fori_loop(0, turns, some, 0)
+    else:
+        turns = 0
     for y in range(low + turns * step, high):
         body(y)
 
@@ -84,14 +87,14 @@
 
 
 def apply(square, value):
-    high, middle, low = split(deep(value))
+    high, middle, low = [part.astype(jnp.float32) for part in split(value)]
     stack = jnp.concatenate([high, middle, high, low, middle, high], axis=0)
-    return jnp.dot(square, stack, preferred_element_type=jnp.float32)[0:PAD]
+    return jnp.dot(square, stack.astype(jnp.bfloat16), preferred_element_type=jnp.float32)[0:PAD]
 
 
 def spread(square):
-    size = DEEP - square.shape[0]
-    square = jnp.pad(square, ((0, size), (0, size)))
+    size = square.shape[0]
+    square = jnp.pad(square, ((0, DEEP - size), (0, PAD - size)))
     high = lax.reduce_precision(square, 8, 7)
     middle = lax.reduce_precision(square - high, 8, 7)
     low = square - high - middle
@@ -338,19 +341,16 @@
         return inside_lane & (row >= 0) & (row < all_rows)
 
     turner[...] = turns(range(1, REACH + 1), 256)
-    block = (rows + 2 * REACH) // 2
-
-    def turn_feat(at):
-        value = feat[pl.ds(at * block, block)].reshape(block * channels, 256)
-        moved = jnp.dot(
-            value.astype(jnp.bfloat16), turner[...], preferred_element_type=jnp.float32
+    tall = rows + 2 * REACH
+    moved = jnp.dot(
+        feat[...].reshape(tall * channels, 256).astype(jnp.bfloat16),
+        turner[...],
+        preferred_element_type=jnp.float32,
+    )
+    for group in range(REACH):
+        feat_turned[group] = moved[:, 256 * group : 256 * group + 256].reshape(
+            tall, channels, 256
         )
-        for group in range(REACH):
-            feat_turned[group, pl.ds(at * block, block)] = moved[
-                :, 256 * group : 256 * group + 256
-            ].reshape(block, channels, 256)
-
-    each_row(0, (rows + 2 * REACH) // block, 1, turn_feat)
 
     def turn_norm(row):
         value = feat[row]
@@ -359,32 +359,39 @@
         for group in range(REACH):
             norm_turned[group, row] = shifted(size, group + 1)
 
-    each_row(0, rows + 2 * REACH, 6, turn_norm)
+    each_row(0, rows + 2 * REACH, (rows + 2 * REACH) // 2, turn_norm)
 
     sub = sublane()
 
-    def affinity_row(y):
+    def affinity_rows(y):
         for tile in range(2):
             cols = pl.ds(128 * tile, 128)
-            here = feat[y + REACH, :, cols]
-            size = norm[y + REACH, :, cols]
+            here = [feat[y + i + REACH, :, cols] for i in range(2)]
+            size = [norm[y + i + REACH, :, cols] for i in range(2)]
             for group in range(REACH):
-                parts = []
-                for a in range(-REACH, REACH + 1):
-                    there = feat_turned[group, y + a + REACH, :, cols]
-                    parts.append(
-                        fold(here * there) - (size + norm_turned[group, y + a + REACH, :, cols])
-                    )
-                below = y + group + 1 + REACH
-                parts.append(fold(here * feat[below, :, cols]) - (size + norm[below, :, cols]))
+                parts = [[], []]
+                for row in range(-REACH, REACH + 2):
+                    there = feat_turned[group, y + row + REACH, :, cols]
+                    other = norm_turned[group, y + row + REACH, :, cols]
+                    for i in range(2):
+                        if -REACH <= row - i <= REACH:
+                            parts[i].append(fold(here[i] * there) - (size[i] + other))
                 step_a = jnp.where(sub == 7, group + 1, sub - REACH)
                 step_b = jnp.where(sub == 7, 0, group + 1)
                 far = (step_a * step_a + step_b * step_b).astype(jnp.float32)
-                kern[y, pl.ds(8 * group, 8), cols] = jnp.exp(
-                    merge(parts) - far * (1.0 / (2.0 * REACH * REACH))
-                )
-
-    each_row(0, rows, 1, affinity_row)
+                for i in range(2):
+                    below = y + i + group + 1 + REACH
+                    parts[i].append(
+                        fold(here[i] * feat[below, :, cols]) - (size[i] + norm[below, :, cols])
+                    )
+                    kern[y + i, pl.ds(8 * group, 8), cols] = jnp.exp(
+                        merge(parts[i]) - far * (1.0 / (2.0 * REACH * REACH))
+                    )
+
+    def affinity_turn(turn):
+        affinity_rows(2 * turn)
+
+    each_row(0, rows // 2, 1, affinity_turn)
 
     def put_field(field, y, value):
         field[y] = value
@@ -394,7 +401,7 @@
     def start(y):
         put_field(prob0, y, jnp.where(inside(y), softmax(unary[y]), 0.0))
 
-    each_row(0, rows, 4, start)
+    each_row(0, rows, rows // 2, start)
 
     def run_pass(field, out, low, high):
         def body(y):
@@ -408,7 +415,7 @@
         value = softmax(unary[y] - apply(compat[...], message0[y]))
         put_field(prob1, y, jnp.where(inside(y), value, 0.0))
 
-    each_row(REACH, rows - REACH, 4, mix)
+    each_row(REACH, rows - REACH, rows, mix)
     run_pass(prob1, message1, 2 * REACH, rows - 2 * REACH)
 
     def back1(y):
@@ -418,19 +425,14 @@
         logit1[y] = change
         put_field(grad1, y, jnp.where(inside(y), -apply(compat_t[...], change), 0.0))
 
-    each_row(2 * REACH, rows - 2 * REACH, 4, back1)
-    total = jnp.zeros((PAD, PAD), jnp.float32)
-
-    def add_share(change, message):
-        def body(turn, carry):
-            at = HALO + 4 * turn
-            left = jnp.concatenate([change[at + i, :, 0:128] for i in range(4)], axis=1)
-            right = jnp.concatenate([message[at + i, :, 0:128] for i in range(4)], axis=1)
-            return carry - outer(left, right)
-
-        return body
-
-    total = lax.fori_loop(0, height // 4, add_share(logit1, message1), total)
+    each_row(2 * REACH, rows - 2 * REACH, rows, back1)
+    def share_of(change, message):
+        block = range(HALO, HALO + height)
+        left = jnp.concatenate([change[y, :, 0:128] for y in block], axis=1)
+        right = jnp.concatenate([message[y, :, 0:128] for y in block], axis=1)
+        return outer(left, right)
+
+    total = -share_of(logit1, message1)
     run_pass(grad1, message1, 3 * REACH, rows - 3 * REACH)
 
     def back0(y):
@@ -440,8 +442,8 @@
         logit0[y] = change
         grad0[y] = jnp.where(inside(y), -apply(compat_t[...], change), 0.0)
 
-    each_row(3 * REACH, rows - 3 * REACH, 4, back0)
-    total = lax.fori_loop(0, height // 4, add_share(logit0, message0), total)
+    each_row(3 * REACH, rows - 3 * REACH, rows, back0)
+    total = total - share_of(logit0, message0)
 
     total = jnp.concatenate([total, jnp.zeros((PAD, 128 - PAD), jnp.float32)], axis=1)
     packed = (
@@ -522,7 +524,6 @@
     steps = range(-REACH, REACH + 1)
 
     turner[...] = turns(steps, 128)
-    block = near // 2
     column = lane()
 
     def moved(main, edge, b):
@@ -531,15 +532,11 @@
         mixed = jnp.where((column < b) if b > 0 else (column >= 128 + b), edge, main)
         return pltpu.roll(mixed, (-b) % 128, axis=1)
 
-    def prepare_feat(at):
-        value = feat[pl.ds(at * block, block)].reshape(block * channels, 256)
-        full = jnp.dot(value, turner[...], preferred_element_type=jnp.float32)
-        for place in range(len(steps)):
-            feat_turned[place, pl.ds(at * block, block)] = full[
-                :, 128 * place : 128 * place + 128
-            ].reshape(block, channels, 128)
-
-    each_row(0, near // block, 1, prepare_feat)
+    full = jnp.dot(
+        feat[...].reshape(near * channels, 256), turner[...], preferred_element_type=jnp.float32
+    )
+    for place in range(len(steps)):
+        feat_turned[place] = full[:, 128 * place : 128 * place + 128].reshape(near, channels, 128)
 
     def prepare(row):
         for place, field in enumerate((prob0, prob1, grad1, grad0)):
@@ -553,7 +550,7 @@
                 sublane() == 7, main, moved(main, edge, -(group + 1))
             )
 
-    each_row(0, near, 2, prepare)
+    each_row(0, near, near, prepare)
 
     def pass_centre(y):
         total = jnp.zeros((PAD, 128), jnp.float32)
@@ -583,7 +580,7 @@
                 start : start + size
             ]
 
-    each_row(0, height, 2, unary_row)
+    each_row(0, height, 4, unary_row)
     sub = sublane()
 
     def feature_row(y):

time: 78.8 us -> 68.8 us (0.87)
  Pallas kernels: 50.2 us -> 40.2 us
    pallas_call x1, Pallas kernels: 32.5 us -> 24.5 us  [iterate(): pl.pallas_call(field_kernel, out_shape=(jax.ShapeDtypeStruct((near, chann...]
    pallas_call x1, Pallas kernels: 12.7 us -> 10.8 us  [finish(): pl.pallas_call(finish_kernel, out_shape=(jax.ShapeDtypeStruct((classes *...]
where the time goes in v5:
time: 68.8 us; the launch traced here: 68.5 us
  Pallas kernels  40.2 us (58%)
  starting transfers between devices  12.4 us (18%)
  waiting for transfers between devices  10.7 us (16%)
  local copies, waits for them, and re-layouts  3.76 us (5%)
  between operations  0.72 us (1%)
    pallas_call x1, Pallas kernels, iterate(): pl.pallas_call(field_kernel, out_shape=(jax.ShapeDtypeStruct((near, chann...  24.5 us
    pallas_call x1, Pallas kernels, finish(): pl.pallas_call(finish_kernel, out_shape=(jax.ShapeDtypeStruct((classes *...  10.8 us
    ppermute x1, waiting for transfers between devices, on_device(): outer_corner = lax.ppermute(outer_corner, 'rows', above)  5.26 us
    ppermute x1, waiting for transfers between devices, on_device(): from_right = lax.ppermute(left, 'cols', backward)  4.23 us
    ppermute x1, starting transfers between devices, on_device(): outer_feat = lax.ppermute(outer_feat, 'rows', above)  3.57 us
    ppermute x1, starting transfers between devices, on_device(): from_left = lax.ppermute(right, 'cols', forward)  3.47 us
    pallas_call x1, Pallas kernels, pack(): pl.pallas_call(pack_kernel, out_shape=(shape(height, depth, 128), shape(h...  3.19 us
    all_to_all x1, starting transfers between devices, on_device(): shares = lax.all_to_all(share, ('rows', 'cols'), 0, 0)  2.95 us
  transfers between devices with their start and end apart: 8, of which 3 were waited for; matrix products, arithmetic and copies ran while one was open for 2% of the time, Pallas kernels for 18%

profile of v5, /device:TPU:0, one launch (start us, length us, event | category | flops | bytes accessed | tf_op | source)
XLA Modules:
  0.0 68.5 jit_solution(2535199043000196537)
XLA Ops:
  0.6 0.0 copy-start.7
  0.6 3.2 %pack.1 = (f32[16,112,128]{2,1,0:T(8,128)}, f32[2,112,128]{2,1,0:T(8,128)}, f32[2,112,128]{2,1,0:T(8,128)}, f32[12,112,128]{2,1,0:T(8,128)}, bf16[12,64,128]{2,1,0:T(8,128)(2,1)}, /*index=5*/f32[18,24,128]{2,1,0:T(8,128)}) custom-call(bf16[64,16,128]{2,1,0:T(8,128)(2,1)} %feat.1, f32[336,128]{1,0:T(8,128)} %bitcast.5, f32[336,128]{1,0:T(8,128)} %bitcast.6), custom_call_target="tpu_custom_call" | custom-call | tf_op jit(solution)/shard_map/pack/pallas_call | solution.py:190
  3.8 0.4 collective-permute-start
  4.3 3.6 %collective-permute-start.1 = (bf16[12,64,128]{2,1,0:T(8,128)(2,1)}, bf16[12,64,128]{2,1,0:T(8,128)(2,1)S(1)}, u32[]{:S(2)}, u32[]{:S(2)}) collective-permute-start(bf16[12,64,128]{2,1,0:T(8,128)(2,1)} %get-tuple-element.23), channel_id=1, source_target_pairs={{4,8},{8,4},{12,16},{16,12},{20,24},{24,20},{28,0},{0,28},{5,9},{9... | collective-permute-start | bytes 589832 | tf_op jit(solution)/shard_map/ppermute | solution.py:667
  7.8 3.5 %collective-permute-start.3 = (f32[2,112,128]{2,1,0:T(8,128)}, f32[2,112,128]{2,1,0:T(8,128)S(1)}, u32[]{:S(2)}, u32[]{:S(2)}) collective-permute-start(f32[2,112,128]{2,1,0:T(8,128)} %get-tuple-element.25), channel_id=1, source_target_pairs={{0,1},{1,2},{2,3},{4,5},{5,6},{6,7},{8,9},{9,10},{10,11},{12,13},{... | collective-permute-start | bytes 344072 | tf_op jit(solution)/shard_map/ppermute | solution.py:669
  11.3 1.3 %collective-permute-start.4 = (f32[2,112,128]{2,1,0:T(8,128)}, f32[2,112,128]{2,1,0:T(8,128)S(1)}, u32[]{:S(2)}, u32[]{:S(2)}) collective-permute-start(f32[2,112,128]{2,1,0:T(8,128)} %get-tuple-element.26), channel_id=1, source_target_pairs={{1,0},{2,1},{3,2},{5,4},{6,5},{7,6},{9,8},{10,9},{11,10},{13,12},{... | collective-permute-start | bytes 344072 | tf_op jit(solution)/shard_map/ppermute | solution.py:670
  12.6 0.1 collective-permute-start.2
  12.7 0.0 copy-done.7
  12.7 0.1 copy.7
  12.8 1.2 %collective-permute-done.3.left.from_left = f32[2,112,128]{2,1,0:T(8,128)S(1)} collective-permute-done((f32[2,112,128]{2,1,0:T(8,128)}, f32[2,112,128]{2,1,0:T(8,128)S(1)}, u32[]{:S(2)}, u32[]{:S(2)}) %collective-permute-start.3) | collective-permute-done | bytes 114720 | tf_op jit(solution)/shard_map/ppermute | solution.py:669
  14.0 0.0 copy-start.2
  14.0 4.2 %collective-permute-done.4.right.from_right = f32[2,112,128]{2,1,0:T(8,128)S(1)} collective-permute-done((f32[2,112,128]{2,1,0:T(8,128)}, f32[2,112,128]{2,1,0:T(8,128)S(1)}, u32[]{:S(2)}, u32[]{:S(2)}) %collective-permute-start.4) | collective-permute-done | bytes 114720 | tf_op jit(solution)/shard_map/ppermute | solution.py:670
  18.2 0.0 copy-start.3
  18.2 0.0 collective-permute-done.1._.outer_feat
  18.2 0.0 copy-done.2
  18.2 0.6 copy-done.3
  18.9 0.0 copy-start
  18.9 0.7 copy-done
  19.5 1.7 %corners.1 = (f32[312,128]{1,0:T(8,128)}, f32[312,128]{1,0:T(8,128)}) custom-call(f32[2,112,128]{2,1,0:T(8,128)} %copy-done.2, f32[2,112,128]{2,1,0:T(8,128)} %copy-done.3, bf16[12,64,128]{2,1,0:T(8,128)(2,1)} %copy-done), custom_call_target="tpu_custom_call" | custom-call | tf_op jit(solution)/shard_map/corners/pallas_call | solution.py:228
  21.3 0.0 collective-permute-start.5
  21.3 0.6 collective-permute-start.6
  21.9 0.7 %concatenate.12.compat_t = bf16[32,144]{1,0:T(8,128)(2,1)} concatenate(bf16[32,24]{1,0:T(8,128)(2,1)S(1)} %get-tuple-element.41, bf16[32,24]{1,0:T(8,128)(2,1)S(1)} %get-tuple-element.41, bf16[32,24]{1,0:T(8,128)(2,1)S(1)} %get-tuple-element.40, bf16[32,24]{1,0:T(8,128)(2,1)S(1)} %get-tuple-element.41, bf16[32,24]{1,0:T(8,128)(2,1)S(1)} %get-tuple-element.40, ...), dimensions={1} | concatenate | bytes 18432 | tf_op jit(solution)/shard_map/concatenate | solution.py:101
  22.7 0.7 %concatenate.11.compat = bf16[32,144]{1,0:T(8,128)(2,1)} concatenate(bf16[32,24]{1,0:T(8,128)(2,1)S(1)} %get-tuple-element.44, bf16[32,24]{1,0:T(8,128)(2,1)S(1)} %get-tuple-element.44, bf16[32,24]{1,0:T(8,128)(2,1)S(1)} %get-tuple-element.43, bf16[32,24]{1,0:T(8,128)(2,1)S(1)} %get-tuple-element.44, bf16[32,24]{1,0:T(8,128)(2,1)S(1)} %get-tuple-element.43, ...), dimensions={1} | concatenate | bytes 18432 | tf_op jit(solution)/shard_map/concatenate | solution.py:101
  23.4 0.0 collective-permute-done.2.outer_rest
  23.4 0.0 copy-start.4
  23.4 0.0 collective-permute-done.5.inner_corner
  23.4 0.0 copy-start.5
  23.4 5.3 %collective-permute-done.6.outer_corner = f32[312,128]{1,0:T(8,128)S(1)} collective-permute-done((f32[312,128]{1,0:T(8,128)}, f32[312,128]{1,0:T(8,128)S(1)}, u32[]{:S(2)}, u32[]{:S(2)}) %collective-permute-start.6) | collective-permute-done | bytes 159776 | tf_op jit(solution)/shard_map/ppermute | solution.py:672
  28.6 0.0 copy-start.6
  28.6 0.0 collective-permute-done.inner
  28.6 0.0 copy-start.1
  28.6 0.0 copy-done.4
  28.7 0.0 copy-done.5
  28.7 0.7 copy-done.6
  29.3 0.2 copy-done.1
  29.5 24.5 %iterate.1 = (bf16[22,64,256]{2,1,0:T(8,128)(2,1)}, f32[22,24,256]{2,1,0:T(8,128)}, f32[22,24,256]{2,1,0:T(8,128)}, f32[22,24,256]{2,1,0:T(8,128)}, f32[22,24,25...) custom-call(bf16[32,144]{1,0:T(8,128)(2,1)} %concatenate.11.compat, ...), custom_call_target="tpu_custom_call" | custom-call | tf_op jit(solution)/shard_map/iterate/pallas_call | solution.py:487
  54.0 2.9 %all-to-all-start = ((f32[32,8,128]{2,1,0:T(8,128)}), f32[32,8,128]{2,1,0:T(8,128)S(1)}, u32[]{:S(2)}, u32[]{:S(2)}) async-start(f32[32,8,128]{2,1,0:T(8,128)} %get-tuple-element.38), calls=%async_computation | async-start | bytes 262144 | tf_op jit(solution)/shard_map/all_to_all | solution.py:682
  57.0 10.8 %finish.1 = (f32[336,128]{1,0:T(8,128)}, f32[1024,128]{1,0:T(8,128)}) custom-call(bf16[22,64,256]{2,1,0:T(8,128)(2,1)} %get-tuple-element.29.feat, f32[22,24,256]{2,1,0:T(8,128)} %get-tuple-element.30.kern, f32[22,24,256]{2,1,0:T(8,128)} %get-tuple-element.31.prob0, f32[22,24,256]{2,1,0:T(8,128)} %get-tuple-element.32.prob1, ...), custom_call_target="tpu_custom_call" | custom-call | flops 200000000 | bytes 8000000 | tf_op jit(solution)/shard_map/finish/pallas_call | solution.py:632
  67.8 0.0 all-to-all-done
  67.8 0.1 fusion.2
  67.9 0.6 pad_maximum_fusion
  (4 shorter events, 0.1 us)
Async XLA Ops:
  0.6 12.1 %copy-start.7 = (f32[21,21]{1,0:T(8,128)S(1)}, f32[21,21]{1,0:T(8,128)}, u32[]{:S(2)}) copy-start(f32[21,21]{1,0:T(8,128)} %param.6) | copy-start | bytes 5296
  3.8 24.8 %collective-permute-start = (f32[12,112,128]{2,1,0:T(8,128)}, f32[12,112,128]{2,1,0:T(8,128)S(1)}, u32[]{:S(2)}, u32[]{:S(2)}) collective-permute-start(f32[12,112,128]{2,1,0:T(8,128)} %get-tuple-element.22), channel_id=1, source_target_pairs={{0,4},{4,0},{8,12},{12,8},{16,20},{20,16},{24,28},{28,24},{1,5},{5... | collective-permute-start | bytes 2064392 | tf_op jit(solution)/shard_map/ppermute | solution.py:666
  4.3 14.0 %collective-permute-start.1 = (bf16[12,64,128]{2,1,0:T(8,128)(2,1)}, bf16[12,64,128]{2,1,0:T(8,128)(2,1)S(1)}, u32[]{:S(2)}, u32[]{:S(2)}) collective-permute-start(bf16[12,64,128]{2,1,0:T(8,128)(2,1)} %get-tuple-element.23), channel_id=1, source_target_pairs={{4,8},{8,4},{12,16},{16,12},{20,24},{24,20},{28,0},{0,28},{5,9},{9... | collective-permute-start | bytes 589832 | tf_op jit(solution)/shard_map/ppermute | solution.py:667
  7.8 6.1 %collective-permute-start.3 = (f32[2,112,128]{2,1,0:T(8,128)}, f32[2,112,128]{2,1,0:T(8,128)S(1)}, u32[]{:S(2)}, u32[]{:S(2)}) collective-permute-start(f32[2,112,128]{2,1,0:T(8,128)} %get-tuple-element.25), channel_id=1, source_target_pairs={{0,1},{1,2},{2,3},{4,5},{5,6},{6,7},{8,9},{9,10},{10,11},{12,13},{... | collective-permute-start | bytes 344072 | tf_op jit(solution)/shard_map/ppermute | solution.py:669
  11.3 6.9 %collective-permute-start.4 = (f32[2,112,128]{2,1,0:T(8,128)}, f32[2,112,128]{2,1,0:T(8,128)S(1)}, u32[]{:S(2)}, u32[]{:S(2)}) collective-permute-start(f32[2,112,128]{2,1,0:T(8,128)} %get-tuple-element.26), channel_id=1, source_target_pairs={{1,0},{2,1},{3,2},{5,4},{6,5},{7,6},{9,8},{10,9},{11,10},{13,12},{... | collective-permute-start | bytes 344072 | tf_op jit(solution)/shard_map/ppermute | solution.py:670
  12.6 10.7 %collective-permute-start.2 = (f32[18,24,128]{2,1,0:T(8,128)}, f32[18,24,128]{2,1,0:T(8,128)S(1)}, u32[]{:S(2)}, u32[]{:S(2)}) collective-permute-start(f32[18,24,128]{2,1,0:T(8,128)} %get-tuple-element.24), channel_id=1, source_target_pairs={{4,8},{8,4},{12,16},{16,12},{20,24},{24,20},{28,0},{0,28},{5,9},{9... | collective-permute-start | bytes 663560 | tf_op jit(solution)/shard_map/ppermute | solution.py:668
  14.0 4.2 %copy-start.2 = (f32[2,112,128]{2,1,0:T(8,128)}, f32[2,112,128]{2,1,0:T(8,128)S(1)}, u32[]{:S(2)}) copy-start(f32[2,112,128]{2,1,0:T(8,128)S(1)} %collective-permute-done.3.left.from_left) | copy-start | bytes 344068
  18.2 0.6 copy-start.3
  18.9 0.7 copy-start
  21.3 2.1 %collective-permute-start.5 = (f32[312,128]{1,0:T(8,128)}, f32[312,128]{1,0:T(8,128)S(1)}, u32[]{:S(2)}, u32[]{:S(2)}) collective-permute-start(f32[312,128]{1,0:T(8,128)} %get-tuple-element.27), channel_id=1, source_target_pairs={{0,4},{4,0},{8,12},{12,8},{16,20},{20,16},{24,28},{28,24},{1,5},{5... | collective-permute-start | bytes 479240 | tf_op jit(solution)/shard_map/ppermute | solution.py:673
  21.3 7.4 %collective-permute-start.6 = (f32[312,128]{1,0:T(8,128)}, f32[312,128]{1,0:T(8,128)S(1)}, u32[]{:S(2)}, u32[]{:S(2)}) collective-permute-start(f32[312,128]{1,0:T(8,128)} %get-tuple-element.28), channel_id=1, source_target_pairs={{4,8},{8,4},{12,16},{16,12},{20,24},{24,20},{28,0},{0,28},{5,9},{9... | collective-permute-start | bytes 479240 | tf_op jit(solution)/shard_map/ppermute | solution.py:672
  23.4 5.3 %copy-start.4 = (f32[18,24,128]{2,1,0:T(8,128)}, f32[18,24,128]{2,1,0:T(8,128)S(1)}, u32[]{:S(2)}) copy-start(f32[18,24,128]{2,1,0:T(8,128)S(1)} %collective-permute-done.2.outer_rest) | copy-start | bytes 663556
  23.4 5.3 %copy-start.5 = (f32[312,128]{1,0:T(8,128)}, f32[312,128]{1,0:T(8,128)S(1)}, u32[]{:S(2)}) copy-start(f32[312,128]{1,0:T(8,128)S(1)} %collective-permute-done.5.inner_corner) | copy-start | bytes 479236
  28.6 0.7 copy-start.6
  28.6 0.9 %copy-start.1 = (f32[12,112,128]{2,1,0:T(8,128)}, f32[12,112,128]{2,1,0:T(8,128)S(1)}, u32[]{:S(2)}) copy-start(f32[12,112,128]{2,1,0:T(8,128)S(1)} %collective-permute-done.inner) | copy-start | bytes 2064388
  54.0 13.7 %all-to-all-start = ((f32[32,8,128]{2,1,0:T(8,128)}), f32[32,8,128]{2,1,0:T(8,128)S(1)}, u32[]{:S(2)}, u32[]{:S(2)}) async-start(f32[32,8,128]{2,1,0:T(8,128)} %get-tuple-element.38), calls=%async_computation | async-start | bytes 262144 | tf_op jit(solution)/shard_map/all_to_all | solution.py:682

commit v6 on v5

--- a/solution.py
+++ b/solution.py
@@ -16,10 +16,26 @@
 DEEP = 32
 LOW = -1e30
 VMEM = pl.BlockSpec(memory_space=pltpu.VMEM)
-
-
-def params():
-    return pltpu.CompilerParams(vmem_limit_bytes=56 * 1024 * 1024)
+ANY = pl.BlockSpec(memory_space=pl.ANY)
+
+
+def params(mebibytes):
+    return pltpu.CompilerParams(vmem_limit_bytes=mebibytes * 1024 * 1024)
+
+
+def fetch(pairs, sems):
+    copies = [
+        pltpu.make_async_copy(source, target, sems.at[i])
+        for i, (source, target) in enumerate(pairs)
+    ]
+    for copy in copies:
+        copy.start()
+    for copy in copies:
+        copy.wait()
+
+
+def like(array):
+    return pltpu.VMEM(array.shape, array.dtype)
 
 
 def position(height):
@@ -137,7 +153,7 @@
 
 
 def pack_kernel(
-    feat, unary, grad, centre, left, right, inner, outer_feat, outer_rest, wide
+    feat, unary, grad, centre, left, right, inner_feat, inner_rest, outer_feat, outer_rest, wide
 ):
     channels, height, _ = feat.shape
     classes = unary.shape[0] // height
@@ -169,15 +185,17 @@
         left[slot], right[slot] = ends
     even = position(height)[0]
     low = height - HALO
-    inner_base = jnp.where(even, low, 0)
-    outer_base = jnp.where(even, 0, low)
-    grad_base = jnp.where(even, 0, height - HALO // 2)
-    for i in range(HALO):
-        inner[i] = centre[inner_base + i]
-        outer_feat[i] = centre[outer_base + i, 0:channels].astype(jnp.bfloat16)
-        outer_rest[i] = centre[outer_base + i, channels : channels + PAD]
-    for i in range(HALO // 2):
-        outer_rest[HALO + i] = centre[grad_base + i, channels + PAD :]
+    for feat_out, rest_out, top in (
+        (inner_feat, inner_rest, jnp.logical_not(even)),
+        (outer_feat, outer_rest, even),
+    ):
+        base = jnp.where(top, 0, low)
+        grad_base = jnp.where(top, 0, height - HALO // 2)
+        for i in range(HALO):
+            feat_out[i] = centre[base + i, 0:channels].astype(jnp.bfloat16)
+            rest_out[i] = centre[base + i, channels : channels + PAD]
+        for i in range(HALO // 2):
+            rest_out[HALO + i] = centre[grad_base + i, channels + PAD :]
 
 
 def pack(feat, unary, grad):
@@ -193,19 +211,21 @@
             shape(height, depth, 128),
             shape(height // 8, depth, 128),
             shape(height // 8, depth, 128),
-            shape(HALO, depth, 128),
+            shape(HALO, channels, 128, dtype=jnp.bfloat16),
+            shape(HALO + HALO // 2, PAD, 128),
             shape(HALO, channels, 128, dtype=jnp.bfloat16),
             shape(HALO + HALO // 2, PAD, 128),
         ),
         in_specs=[VMEM] * 3,
-        out_specs=(VMEM,) * 6,
+        out_specs=(VMEM,) * 7,
         scratch_shapes=[pltpu.VMEM((channels * height, 128), jnp.float32)],
-        compiler_params=params(),
+        compiler_params=params(56),
         name="pack",
     )(feat, unary.reshape(-1, 128), grad.reshape(-1, 128))
 
 
-def corner_kernel(left, right, _, inner, outer):
+def corner_kernel(left_in, right_in, _, inner, outer, left, right, sems):
+    fetch([(left_in, left), (right_in, right)], sems)
     depth = left.shape[1]
     short = depth - PAD
     even = position(8 * left.shape[0])[0]
@@ -228,9 +248,10 @@
     return pl.pallas_call(
         corner_kernel,
         out_shape=(out, out),
-        in_specs=[VMEM, VMEM, pl.BlockSpec(memory_space=pl.ANY)],
+        in_specs=[ANY] * 3,
         out_specs=(VMEM,) * 2,
-        compiler_params=params(),
+        scratch_shapes=[like(left), like(right), pltpu.SemaphoreType.DMA((2,))],
+        compiler_params=params(4),
         name="corners",
     )(left, right, earlier)
 
@@ -264,8 +285,9 @@
 
 
 def field_kernel(
-    compat, compat_t, centre, inner, outer_feat, outer_rest, inner_corner, outer_corner,
-    from_left, from_right, feat_out, kern_out, prob0_out, prob1_out, grad1_out, grad0_out, unary_out, share,
+    compat, compat_t, centre, inner_feat, inner_rest, outer_feat, outer_rest, inner_corner,
+    outer_corner, from_left, from_right, feat_out, kern_out, prob0_out, prob1_out, grad1_out,
+    grad0_out, unary_out, share,
     feat, feat_turned, norm, norm_turned, kern, unary, grad, prob0, prob1, grad1, grad0,
     turned, message0, message1, logit1, logit0, turner,
 ):
@@ -295,14 +317,11 @@
     short = channels + PAD
     near = HALO // 2
 
-    def put_inner(i, top):
-        return inner[i]
-
-    def put_outer(i, top):
-        parts = [outer_feat[i].astype(jnp.float32), outer_rest[i]]
+    def edge_row(feat_in, rest_in, i, top):
+        parts = [feat_in[i].astype(jnp.float32), rest_in[i]]
         row = i if top else i - near
         if 0 <= row < near:
-            parts.append(outer_rest[HALO + row])
+            parts.append(rest_in[HALO + row])
         return jnp.concatenate(parts, axis=0)
 
     def put_rows(main, corner, top):
@@ -323,8 +342,8 @@
 
     even, has_left, has_right, first_row, all_rows = position(height)
     for main, corner, below in (
-        (put_inner, inner_corner, even),
-        (put_outer, outer_corner, jnp.logical_not(even)),
+        (functools.partial(edge_row, inner_feat, inner_rest), inner_corner, even),
+        (functools.partial(edge_row, outer_feat, outer_rest), outer_corner, jnp.logical_not(even)),
     ):
         pl.when(below)(functools.partial(put_rows, main, corner, True))
         pl.when(jnp.logical_not(below))(functools.partial(put_rows, main, corner, False))
@@ -496,7 +515,7 @@
             shape(height, PAD, 128),
             shape(devices, 8, 128),
         ),
-        in_specs=[VMEM] * 10,
+        in_specs=[VMEM] * (3 + len(received)),
         out_specs=(VMEM,) * 8,
         scratch_shapes=[
             room(tall, channels, 256),
@@ -508,7 +527,7 @@
             *[room(rows, PAD, 256)] * 4,
             pltpu.VMEM((256, REACH * 256), jnp.bfloat16),
         ],
-        compiler_params=params(),
+        compiler_params=params(56),
         name="iterate",
     )(spread(compat), spread(compat.T), centre, *received)
 
@@ -644,7 +663,7 @@
             room(height, 6 * 8, 128),
             pltpu.VMEM((256, (2 * REACH + 1) * 128), jnp.bfloat16),
         ],
-        compiler_params=params(),
+        compiler_params=params(56),
         cost_estimate=pl.CostEstimate(flops=200_000_000, bytes_accessed=8_000_000, transcendentals=0),
         name="finish",
     )(feat, kern, prob0, prob1, grad1, grad0, partial)
@@ -662,17 +681,21 @@
     ]
     forward = [(i, i + 1) for i in range(n_cols - 1)]
     backward = [(i + 1, i) for i in range(n_cols - 1)]
-    centre, left, right, inner, outer_feat, outer_rest = pack(features, unary, grad_output)
-    inner = lax.ppermute(inner, "rows", below)
+    centre, left, right, inner_feat, inner_rest, outer_feat, outer_rest = pack(
+        features, unary, grad_output
+    )
+    inner_feat = lax.ppermute(inner_feat, "rows", below)
+    inner_rest = lax.ppermute(inner_rest, "rows", below)
     outer_feat = lax.ppermute(outer_feat, "rows", above)
     outer_rest = lax.ppermute(outer_rest, "rows", above)
     from_left = lax.ppermute(right, "cols", forward)
     from_right = lax.ppermute(left, "cols", backward)
-    inner_corner, outer_corner = corners(from_left, from_right, outer_feat)
+    inner_corner, outer_corner = corners(from_left, from_right, outer_rest)
     outer_corner = lax.ppermute(outer_corner, "rows", above)
     inner_corner = lax.ppermute(inner_corner, "rows", below)
     received = (
-        inner, outer_feat, outer_rest, inner_corner, outer_corner, from_left, from_right
+        inner_feat, inner_rest, outer_feat, outer_rest, inner_corner, outer_corner,
+        from_left, from_right,
     )
 
     devices = n_rows * n_cols

time: 68.8 us -> 66 us (0.959)
  waiting for transfers between devices: 10.7 us -> 8.94 us
  starting transfers between devices: 12.4 us -> 14.1 us
  Pallas kernels: 40.2 us -> 38.7 us
  local copies, waits for them, and re-layouts: 3.76 us -> 2.54 us
    ppermute x1, starting transfers between devices: 0.07 us -> 3.33 us  [on_device(): outer_rest = lax.ppermute(outer_rest, 'rows', above)]
    ppermute x1, starting transfers between devices: 3.57 us -> 0.68 us  [on_device(): outer_feat = lax.ppermute(outer_feat, 'rows', above)]
    pallas_call x1, Pallas kernels: 1.75 us -> 0.43 us  [corners(): pl.pallas_call(corner_kernel, out_shape=(out, out), in_specs=[ANY] * 3, o...]
    unnamed x17 -> x19, local copies, waits for them, and re-layouts: 2.29 us -> 1.06 us
    ppermute x1, waiting for transfers between devices: 5.26 us -> 4.19 us  [on_device(): outer_corner = lax.ppermute(outer_corner, 'rows', above)]
    all_to_all x1, starting transfers between devices: 2.95 us -> 3.96 us  [on_device(): shares = lax.all_to_all(share, ('rows', 'cols'), 0, 0)]
  transfers between devices with their start and end apart: 8 -> 9, of which waited for: 3 -> 3; matrix products, arithmetic and copies ran while one was open for 2% -> 2% of each run, Pallas kernels for 18% -> 17%
where the time goes in v6:
time: 66 us; the launch traced here: 65.7 us
  Pallas kernels  38.7 us (59%)
  starting transfers between devices  14.1 us (21%)
  waiting for transfers between devices  8.94 us (14%)
  local copies, waits for them, and re-layouts  2.54 us (4%)
  between operations  0.76 us (1%)
  other arithmetic  0.67 us (1%)
    pallas_call x1, Pallas kernels, iterate(): pl.pallas_call(field_kernel, out_shape=(jax.ShapeDtypeStruct((near, chann...  24.5 us
    pallas_call x1, Pallas kernels, finish(): pl.pallas_call(finish_kernel, out_shape=(jax.ShapeDtypeStruct((classes *...  10.8 us
    ppermute x1, waiting for transfers between devices, on_device(): from_right = lax.ppermute(left, 'cols', backward)  4.23 us
    ppermute x1, waiting for transfers between devices, on_device(): outer_corner = lax.ppermute(outer_corner, 'rows', above)  4.19 us
    all_to_all x1, starting transfers between devices, on_device(): shares = lax.all_to_all(share, ('rows', 'cols'), 0, 0)  3.96 us
    ppermute x1, starting transfers between devices, on_device(): from_left = lax.ppermute(right, 'cols', forward)  3.47 us
    ppermute x1, starting transfers between devices, on_device(): outer_rest = lax.ppermute(outer_rest, 'rows', above)  3.33 us
    pallas_call x1, Pallas kernels, pack(): pl.pallas_call(pack_kernel, out_shape=(shape(height, depth, 128), shape(h...  3.05 us
  transfers between devices with their start and end apart: 9, of which 3 were waited for; matrix products, arithmetic and copies ran while one was open for 2% of the time, Pallas kernels for 17%

profile of v6, /device:TPU:0, one launch (start us, length us, event | category | flops | bytes accessed | tf_op | source)
XLA Modules:
  0.0 65.7 jit_solution(5332134744467545730)
XLA Ops:
  0.6 0.0 copy-start.8
  0.6 3.1 %pack.1 = (f32[16,112,128]{2,1,0:T(8,128)}, f32[2,112,128]{2,1,0:T(8,128)}, f32[2,112,128]{2,1,0:T(8,128)}, bf16[12,64,128]{2,1,0:T(8,128)(2,1)}, f32[18,24,128]...) custom-call(bf16[64,16,128]{2,1,0:T(8,128)(2,1)} %feat.1, f32[336,128]{1,0:T(8,128)} %bitcast.5, ...), custom_call_target="tpu_custom_call" | custom-call | tf_op jit(solution)/shard_map/pack/pallas_call | solution.py:208
  3.7 3.3 %collective-permute-start.3 = (f32[18,24,128]{2,1,0:T(8,128)}, f32[18,24,128]{2,1,0:T(8,128)S(1)}, u32[]{:S(2)}, u32[]{:S(2)}) collective-permute-start(f32[18,24,128]{2,1,0:T(8,128)} %get-tuple-element.26), channel_id=1, source_target_pairs={{4,8},{8,4},{12,16},{16,12},{20,24},{24,20},{28,0},{0,28},{5,9},{9... | collective-permute-start | bytes 663560 | tf_op jit(solution)/shard_map/ppermute | solution.py:690
  7.0 3.5 %collective-permute-start.4 = (f32[2,112,128]{2,1,0:T(8,128)}, f32[2,112,128]{2,1,0:T(8,128)S(1)}, u32[]{:S(2)}, u32[]{:S(2)}) collective-permute-start(f32[2,112,128]{2,1,0:T(8,128)} %get-tuple-element.27), channel_id=1, source_target_pairs={{0,1},{1,2},{2,3},{4,5},{5,6},{6,7},{8,9},{9,10},{10,11},{12,13},{... | collective-permute-start | bytes 344072 | tf_op jit(solution)/shard_map/ppermute | solution.py:691
  10.5 1.3 %collective-permute-start.5 = (f32[2,112,128]{2,1,0:T(8,128)}, f32[2,112,128]{2,1,0:T(8,128)S(1)}, u32[]{:S(2)}, u32[]{:S(2)}) collective-permute-start(f32[2,112,128]{2,1,0:T(8,128)} %get-tuple-element.28), channel_id=1, source_target_pairs={{1,0},{2,1},{3,2},{5,4},{6,5},{7,6},{9,8},{10,9},{11,10},{13,12},{... | collective-permute-start | bytes 344072 | tf_op jit(solution)/shard_map/ppermute | solution.py:692
  11.8 0.1 collective-permute-start
  11.9 0.7 %collective-permute-start.2 = (bf16[12,64,128]{2,1,0:T(8,128)(2,1)}, bf16[12,64,128]{2,1,0:T(8,128)(2,1)S(1)}, u32[]{:S(2)}, u32[]{:S(2)}) collective-permute-start(bf16[12,64,128]{2,1,0:T(8,128)(2,1)} %get-tuple-element.25), channel_id=1, source_target_pairs={{4,8},{8,4},{12,16},{16,12},{20,24},{24,20},{28,0},{0,28},{5,9},{9... | collective-permute-start | bytes 589832 | tf_op jit(solution)/shard_map/ppermute | solution.py:689
  12.6 0.0 copy-done.8
  12.6 0.1 copy.7
  12.7 0.5 collective-permute-done.4.left_in.from_left
  13.2 0.0 copy-start.1
  13.2 0.0 collective-permute-start.1
  13.2 4.2 %collective-permute-done.5.right_in.from_right = f32[2,112,128]{2,1,0:T(8,128)S(1)} collective-permute-done((f32[2,112,128]{2,1,0:T(8,128)}, f32[2,112,128]{2,1,0:T(8,128)S(1)}, u32[]{:S(2)}, u32[]{:S(2)}) %collective-permute-start.5) | collective-permute-done | bytes 114720 | tf_op jit(solution)/shard_map/ppermute | solution.py:692
  17.4 0.0 copy-start.2
  17.4 0.0 collective-permute-done.3._.outer_rest
  17.4 0.0 copy-start
  17.4 0.4 corners.1
  17.8 0.0 copy-done.1
  17.9 0.2 copy-done.2
  18.0 0.1 copy-done
  18.1 0.0 collective-permute-start.6
  18.1 1.3 %collective-permute-start.7 = (f32[312,128]{1,0:T(8,128)S(1)}, f32[312,128]{1,0:T(8,128)S(1)}, u32[]{:S(2)}, u32[]{:S(2)}) collective-permute-start(f32[312,128]{1,0:T(8,128)S(1)} %get-tuple-element.30), channel_id=1, source_target_pairs={{4,8},{8,4},{12,16},{16,12},{20,24},{24,20},{28,0},{0,28},{5,9},{9... | collective-permute-start | bytes 479240 | tf_op jit(solution)/shard_map/ppermute | solution.py:694
  19.4 0.7 %concatenate.12.compat_t = bf16[32,144]{1,0:T(8,128)(2,1)} concatenate(bf16[32,24]{1,0:T(8,128)(2,1)S(1)} %get-tuple-element.43, bf16[32,24]{1,0:T(8,128)(2,1)S(1)} %get-tuple-element.43, bf16[32,24]{1,0:T(8,128)(2,1)S(1)} %get-tuple-element.42, bf16[32,24]{1,0:T(8,128)(2,1)S(1)} %get-tuple-element.43, bf16[32,24]{1,0:T(8,128)(2,1)S(1)} %get-tuple-element.42, ...), dimensions={1} | concatenate | bytes 18432 | tf_op jit(solution)/shard_map/concatenate | solution.py:117
  20.1 0.7 %concatenate.11.compat = bf16[32,144]{1,0:T(8,128)(2,1)} concatenate(bf16[32,24]{1,0:T(8,128)(2,1)S(1)} %get-tuple-element.46, bf16[32,24]{1,0:T(8,128)(2,1)S(1)} %get-tuple-element.46, bf16[32,24]{1,0:T(8,128)(2,1)S(1)} %get-tuple-element.45, bf16[32,24]{1,0:T(8,128)(2,1)S(1)} %get-tuple-element.46, bf16[32,24]{1,0:T(8,128)(2,1)S(1)} %get-tuple-element.45, ...), dimensions={1} | concatenate | bytes 18432 | tf_op jit(solution)/shard_map/concatenate | solution.py:117
  20.8 0.0 collective-permute-done.inner_feat
  20.8 0.0 copy-start.4
  20.8 0.0 collective-permute-done.2.outer_feat
  20.8 0.0 copy-start.5
  20.8 0.0 collective-permute-done.1.inner_rest
  20.8 0.0 copy-start.3
  20.9 0.0 collective-permute-done.6.inner_corner
  20.9 0.0 copy-start.6
  20.9 4.2 %collective-permute-done.7.outer_corner = f32[312,128]{1,0:T(8,128)S(1)} collective-permute-done((f32[312,128]{1,0:T(8,128)S(1)}, f32[312,128]{1,0:T(8,128)S(1)}, u32[]{:S(2)}, u32[]{:S(2)}) %collective-permute-start.7) | collective-permute-done | bytes 159776 | tf_op jit(solution)/shard_map/ppermute | solution.py:694
  25.1 0.0 copy-start.7
  25.1 0.0 copy-done.4
  25.1 0.0 copy-done.5
  25.1 0.0 copy-done.3
  25.1 0.0 copy-done.6
  25.1 0.7 %copy-done.7 = f32[312,128]{1,0:T(8,128)} copy-done((f32[312,128]{1,0:T(8,128)}, f32[312,128]{1,0:T(8,128)S(1)}, u32[]{:S(2)}) %copy-start.7) | copy-done | bytes 159768
  25.8 24.5 %iterate.1 = (bf16[22,64,256]{2,1,0:T(8,128)(2,1)}, f32[22,24,256]{2,1,0:T(8,128)}, f32[22,24,256]{2,1,0:T(8,128)}, f32[22,24,256]{2,1,0:T(8,128)}, f32[22,24,25...) custom-call(bf16[32,144]{1,0:T(8,128)(2,1)} %concatenate.11.compat, ...), custom_call_target="tpu_custom_call" | custom-call | tf_op jit(solution)/shard_map/iterate/pallas_call | solution.py:506
  50.2 4.0 %all-to-all-start = ((f32[32,8,128]{2,1,0:T(8,128)}), f32[32,8,128]{2,1,0:T(8,128)S(1)}, u32[]{:S(2)}, u32[]{:S(2)}) async-start(f32[32,8,128]{2,1,0:T(8,128)} %get-tuple-element.40), calls=%async_computation | async-start | bytes 262144 | tf_op jit(solution)/shard_map/all_to_all | solution.py:705
  54.2 10.8 %finish.1 = (f32[336,128]{1,0:T(8,128)}, f32[1024,128]{1,0:T(8,128)}) custom-call(bf16[22,64,256]{2,1,0:T(8,128)(2,1)} %get-tuple-element.31.feat, f32[22,24,256]{2,1,0:T(8,128)} %get-tuple-element.32.kern, f32[22,24,256]{2,1,0:T(8,128)} %get-tuple-element.33.prob0, f32[22,24,256]{2,1,0:T(8,128)} %get-tuple-element.34.prob1, ...), custom_call_target="tpu_custom_call" | custom-call | flops 200000000 | bytes 8000000 | tf_op jit(solution)/shard_map/finish/pallas_call | solution.py:651
  65.0 0.0 all-to-all-done
  65.0 0.1 fusion.2
  65.1 0.6 pad_maximum_fusion
  (4 shorter events, 0.1 us)
Async XLA Ops:
  0.6 11.9 %copy-start.8 = (f32[21,21]{1,0:T(8,128)S(1)}, f32[21,21]{1,0:T(8,128)}, u32[]{:S(2)}) copy-start(f32[21,21]{1,0:T(8,128)} %param.6) | copy-start | bytes 5296
  3.7 13.7 %collective-permute-start.3 = (f32[18,24,128]{2,1,0:T(8,128)}, f32[18,24,128]{2,1,0:T(8,128)S(1)}, u32[]{:S(2)}, u32[]{:S(2)}) collective-permute-start(f32[18,24,128]{2,1,0:T(8,128)} %get-tuple-element.26), channel_id=1, source_target_pairs={{4,8},{8,4},{12,16},{16,12},{20,24},{24,20},{28,0},{0,28},{5,9},{9... | collective-permute-start | bytes 663560 | tf_op jit(solution)/shard_map/ppermute | solution.py:690
  7.0 6.1 %collective-permute-start.4 = (f32[2,112,128]{2,1,0:T(8,128)}, f32[2,112,128]{2,1,0:T(8,128)S(1)}, u32[]{:S(2)}, u32[]{:S(2)}) collective-permute-start(f32[2,112,128]{2,1,0:T(8,128)} %get-tuple-element.27), channel_id=1, source_target_pairs={{0,1},{1,2},{2,3},{4,5},{5,6},{6,7},{8,9},{9,10},{10,11},{12,13},{... | collective-permute-start | bytes 344072 | tf_op jit(solution)/shard_map/ppermute | solution.py:691
  10.5 6.9 %collective-permute-start.5 = (f32[2,112,128]{2,1,0:T(8,128)}, f32[2,112,128]{2,1,0:T(8,128)S(1)}, u32[]{:S(2)}, u32[]{:S(2)}) collective-permute-start(f32[2,112,128]{2,1,0:T(8,128)} %get-tuple-element.28), channel_id=1, source_target_pairs={{1,0},{2,1},{3,2},{5,4},{6,5},{7,6},{9,8},{10,9},{11,10},{13,12},{... | collective-permute-start | bytes 344072 | tf_op jit(solution)/shard_map/ppermute | solution.py:692
  11.8 9.0 %collective-permute-start = (bf16[12,64,128]{2,1,0:T(8,128)(2,1)}, bf16[12,64,128]{2,1,0:T(8,128)(2,1)S(1)}, u32[]{:S(2)}, u32[]{:S(2)}) collective-permute-start(bf16[12,64,128]{2,1,0:T(8,128)(2,1)} %get-tuple-element.23), channel_id=1, source_target_pairs={{0,4},{4,0},{8,12},{12,8},{16,20},{20,16},{24,28},{28,24},{1,5},{5... | collective-permute-start | bytes 589832 | tf_op jit(solution)/shard_map/ppermute | solution.py:687
  11.9 8.9 %collective-permute-start.2 = (bf16[12,64,128]{2,1,0:T(8,128)(2,1)}, bf16[12,64,128]{2,1,0:T(8,128)(2,1)S(1)}, u32[]{:S(2)}, u32[]{:S(2)}) collective-permute-start(bf16[12,64,128]{2,1,0:T(8,128)(2,1)} %get-tuple-element.25), channel_id=1, source_target_pairs={{4,8},{8,4},{12,16},{16,12},{20,24},{24,20},{28,0},{0,28},{5,9},{9... | collective-permute-start | bytes 589832 | tf_op jit(solution)/shard_map/ppermute | solution.py:689
  13.2 4.7 %copy-start.1 = (f32[2,112,128]{2,1,0:T(8,128)}, f32[2,112,128]{2,1,0:T(8,128)S(1)}, u32[]{:S(2)}) copy-start(f32[2,112,128]{2,1,0:T(8,128)S(1)} %collective-permute-done.4.left_in.from_left) | copy-start | bytes 344068
  13.2 7.7 %collective-permute-start.1 = (f32[18,24,128]{2,1,0:T(8,128)}, f32[18,24,128]{2,1,0:T(8,128)S(1)}, u32[]{:S(2)}, u32[]{:S(2)}) collective-permute-start(f32[18,24,128]{2,1,0:T(8,128)} %get-tuple-element.24), channel_id=1, source_target_pairs={{0,4},{4,0},{8,12},{12,8},{16,20},{20,16},{24,28},{28,24},{1,5},{5... | collective-permute-start | bytes 663560 | tf_op jit(solution)/shard_map/ppermute | solution.py:688
  17.4 0.6 copy-start.2
  17.4 0.7 %copy-start = (f32[18,24,128]{2,1,0:T(8,128)}, f32[18,24,128]{2,1,0:T(8,128)S(1)}, u32[]{:S(2)}) copy-start(f32[18,24,128]{2,1,0:T(8,128)S(1)} %collective-permute-done.3._.outer_rest) | copy-start | bytes 663556
  18.1 2.7 %collective-permute-start.6 = (f32[312,128]{1,0:T(8,128)S(1)}, f32[312,128]{1,0:T(8,128)S(1)}, u32[]{:S(2)}, u32[]{:S(2)}) collective-permute-start(f32[312,128]{1,0:T(8,128)S(1)} %get-tuple-element.29), channel_id=1, source_target_pairs={{0,4},{4,0},{8,12},{12,8},{16,20},{20,16},{24,28},{28,24},{1,5},{5... | collective-permute-start | bytes 479240 | tf_op jit(solution)/shard_map/ppermute | solution.py:695
  18.1 6.9 %collective-permute-start.7 = (f32[312,128]{1,0:T(8,128)S(1)}, f32[312,128]{1,0:T(8,128)S(1)}, u32[]{:S(2)}, u32[]{:S(2)}) collective-permute-start(f32[312,128]{1,0:T(8,128)S(1)} %get-tuple-element.30), channel_id=1, source_target_pairs={{4,8},{8,4},{12,16},{16,12},{20,24},{24,20},{28,0},{0,28},{5,9},{9... | collective-permute-start | bytes 479240 | tf_op jit(solution)/shard_map/ppermute | solution.py:694
  20.8 4.3 %copy-start.4 = (bf16[12,64,128]{2,1,0:T(8,128)(2,1)}, bf16[12,64,128]{2,1,0:T(8,128)(2,1)S(1)}, u32[]{:S(2)}) copy-start(bf16[12,64,128]{2,1,0:T(8,128)(2,1)S(1)} %collective-permute-done.inner_feat) | copy-start | bytes 589828
  20.8 4.3 %copy-start.5 = (bf16[12,64,128]{2,1,0:T(8,128)(2,1)}, bf16[12,64,128]{2,1,0:T(8,128)(2,1)S(1)}, u32[]{:S(2)}) copy-start(bf16[12,64,128]{2,1,0:T(8,128)(2,1)S(1)} %collective-permute-done.2.outer_feat) | copy-start | bytes 589828
  20.8 4.2 %copy-start.3 = (f32[18,24,128]{2,1,0:T(8,128)}, f32[18,24,128]{2,1,0:T(8,128)S(1)}, u32[]{:S(2)}) copy-start(f32[18,24,128]{2,1,0:T(8,128)S(1)} %collective-permute-done.1.inner_rest) | copy-start | bytes 663556
  20.9 4.2 %copy-start.6 = (f32[312,128]{1,0:T(8,128)}, f32[312,128]{1,0:T(8,128)S(1)}, u32[]{:S(2)}) copy-start(f32[312,128]{1,0:T(8,128)S(1)} %collective-permute-done.6.inner_corner) | copy-start | bytes 479236
  25.1 0.7 %copy-start.7 = (f32[312,128]{1,0:T(8,128)}, f32[312,128]{1,0:T(8,128)S(1)}, u32[]{:S(2)}) copy-start(f32[312,128]{1,0:T(8,128)S(1)} %collective-permute-done.7.outer_corner) | copy-start | bytes 479236
  50.2 14.7 %all-to-all-start = ((f32[32,8,128]{2,1,0:T(8,128)}), f32[32,8,128]{2,1,0:T(8,128)S(1)}, u32[]{:S(2)}, u32[]{:S(2)}) async-start(f32[32,8,128]{2,1,0:T(8,128)} %get-tuple-element.40), calls=%async_computation | async-start | bytes 262144 | tf_op jit(solution)/shard_map/all_to_all | solution.py:705

commit v7 on v6

--- a/solution.py
+++ b/solution.py
@@ -11,6 +11,7 @@
 ITERS = 2
 REACH = 3
 HALO = 2 * ITERS * REACH
+GROUPS = 4
 STRIP = 16
 PAD = 24
 DEEP = 32
@@ -30,6 +31,10 @@
     ]
     for copy in copies:
         copy.start()
+    return copies
+
+
+def wait(copies):
     for copy in copies:
         copy.wait()
 
@@ -109,12 +114,17 @@
 
 
 def spread(square):
-    size = square.shape[0]
-    square = jnp.pad(square, ((0, DEEP - size), (0, PAD - size)))
-    high = lax.reduce_precision(square, 8, 7)
-    middle = lax.reduce_precision(square - high, 8, 7)
-    low = square - high - middle
-    return jnp.concatenate([high, high, middle, high, middle, low], axis=1).astype(jnp.bfloat16)
+    high, middle, low = [part.astype(jnp.float32) for part in split(square[0:DEEP])]
+    wide = [jnp.zeros((DEEP, 128), jnp.float32)] * 2
+    for i, part in enumerate((high, high, middle, high, middle, low)):
+        start = PAD * i
+        moved = pltpu.roll(part, start % 128, axis=1)
+        for tile in range(2):
+            low_lane = start - 128 * tile
+            if low_lane < 128 and low_lane + PAD > 0:
+                here = (lane() >= low_lane) & (lane() < low_lane + PAD)
+                wide[tile] = jnp.where(here, moved, wide[tile])
+    return jnp.concatenate(wide, axis=1)[:, 0 : 6 * PAD].astype(jnp.bfloat16)
 
 
 def outer(left, right):
@@ -225,7 +235,7 @@
 
 
 def corner_kernel(left_in, right_in, _, inner, outer, left, right, sems):
-    fetch([(left_in, left), (right_in, right)], sems)
+    wait(fetch([(left_in, left), (right_in, right)], sems))
     depth = left.shape[1]
     short = depth - PAD
     even = position(8 * left.shape[0])[0]
@@ -256,6 +266,147 @@
     )(left, right, earlier)
 
 
+def sizes(here, there, size, size_there):
+    rows = here.shape[0]
+
+    def body(row):
+        value = here[row]
+        size[row] = fold(value * value) * 0.5
+        for group in range(REACH):
+            value = there[group, row]
+            size_there[group, row] = fold(value * value) * 0.5
+
+    each_row(0, rows, rows // 2, body)
+
+
+def affinities(here, there, size, size_there, out):
+    sub = sublane()
+
+    def two(turn):
+        y = 2 * turn
+        mine = [here[y + i + REACH] for i in range(2)]
+        mine_size = [size[y + i + REACH] for i in range(2)]
+        for group in range(REACH):
+            parts = [[], []]
+            for row in range(-REACH, REACH + 2):
+                other = there[group, y + row + REACH]
+                other_size = size_there[group, y + row + REACH]
+                for i in range(2):
+                    if -REACH <= row - i <= REACH:
+                        parts[i].append(fold(mine[i] * other) - (mine_size[i] + other_size))
+            step_a = jnp.where(sub == 7, group + 1, sub - REACH)
+            step_b = jnp.where(sub == 7, 0, group + 1)
+            far = (step_a * step_a + step_b * step_b).astype(jnp.float32)
+            for i in range(2):
+                below = y + i + group + 1 + REACH
+                parts[i].append(fold(mine[i] * here[below]) - (mine_size[i] + size[below]))
+                out[y + i, pl.ds(8 * group, 8), :] = jnp.exp(
+                    merge(parts[i]) - far * (1.0 / (2.0 * REACH * REACH))
+                )
+
+    each_row(0, out.shape[0] // 2, 1, two)
+
+
+def strip_edge(left, left_at, right, right_at):
+    right = pltpu.roll(right, (128 - right_at) % 128, axis=1)
+    left = pltpu.roll(left, (128 - STRIP - left_at) % 128, axis=1)
+    return jnp.where(lane() < 64, right, left)
+
+
+def main_kernel(
+    centre_in, from_left_in, from_right_in, inner_in, outer_in, kern_out,
+    centre, from_left, from_right, inner, outer, feat, short, turned, size, size_turned, turner,
+    sems,
+):
+    coming = fetch(
+        [
+            (inner_in, inner), (outer_in, outer), (centre_in, centre),
+            (from_left_in, from_left), (from_right_in, from_right),
+        ],
+        sems,
+    )
+    height, channels = centre.shape[0], feat.shape[1]
+    tall = feat.shape[0]
+    turner[...] = turns(range(1, REACH + 1), 128)
+    blank = jnp.zeros((REACH, channels, 128), jnp.float32)
+    for at in (0, tall - REACH):
+        feat[pl.ds(at, REACH)] = blank
+        short[pl.ds(at, REACH)] = jnp.zeros((REACH, channels, 256), jnp.bfloat16)
+    even = position(height)[0]
+    wait(coming)
+    above = jnp.where(even, REACH + HALO + height, REACH)
+    for source, base in ((inner, above), (outer, tall - HALO - above)):
+        for i in range(HALO):
+            feat[base + i] = source[i].astype(jnp.float32)
+            short[base + i, :, 0:128] = source[i]
+            short[base + i, :, 128:256] = jnp.zeros((channels, 128), jnp.bfloat16)
+    for y in range(height):
+        at = (y % 8) * STRIP
+        row = y + HALO + REACH
+        feat[row] = centre[y, 0:channels]
+        short[row, :, 0:128] = centre[y, 0:channels].astype(jnp.bfloat16)
+        edge = strip_edge(
+            from_left[y // 8, 0:channels], at, from_right[y // 8, 0:channels], at
+        )
+        short[row, :, 128:256] = edge.astype(jnp.bfloat16)
+    moved = jnp.dot(
+        short[...].reshape(tall * channels, 256), turner[...], preferred_element_type=jnp.float32
+    )
+    for group in range(REACH):
+        turned[group] = moved[:, 128 * group : 128 * group + 128].reshape(tall, channels, 128)
+    sizes(feat, turned, size, size_turned)
+    affinities(feat, turned, size, size_turned, kern_out)
+
+
+def main_affinities(centre, from_left, from_right, inner, outer):
+    height, depth, _ = centre.shape
+    channels = depth - 2 * PAD
+    rows = height + 2 * HALO
+    tall = rows + 2 * REACH
+    inputs = (centre, from_left, from_right, inner, outer)
+
+    def room(*dims, dtype=jnp.float32):
+        return pltpu.VMEM(dims, dtype)
+
+    return pl.pallas_call(
+        main_kernel,
+        out_shape=jax.ShapeDtypeStruct((rows, PAD, 128), jnp.float32),
+        in_specs=[ANY] * 5,
+        out_specs=VMEM,
+        scratch_shapes=[
+            *map(like, inputs),
+            room(tall, channels, 128),
+            room(tall, channels, 256, dtype=jnp.bfloat16),
+            room(REACH, tall, channels, 128),
+            room(tall, 8, 128),
+            room(REACH, tall, 8, 128),
+            room(256, REACH * 128, dtype=jnp.bfloat16),
+            pltpu.SemaphoreType.DMA((5,)),
+        ],
+        compiler_params=params(56),
+        cost_estimate=pl.CostEstimate(
+            flops=200_000_000, bytes_accessed=8_000_000, transcendentals=0
+        ),
+        name="main_affinities",
+    )(*inputs)
+
+
+def side_turns():
+    target = lax.broadcasted_iota(jnp.int32, (256, 128), 1)
+    source = lax.broadcasted_iota(jnp.int32, (256, 128), 0)
+    place = target % 32
+    column = jnp.where(place < 12, place - 12, jnp.where(place < 24, 116 + place, 101 + place))
+    blocks = []
+    for b in range(REACH + 1):
+        hit = source == (column + b + 256) % 256
+        blocks.append(
+            jnp.concatenate(
+                [(hit & (target // 32 == j)).astype(jnp.bfloat16) for j in range(GROUPS)], axis=0
+            )
+        )
+    return jnp.concatenate(blocks, axis=1)
+
+
 def pass_row(y, kern, field, turned):
     def weight(row, at):
         return kern[row, pl.ds(at, 1), :]
@@ -285,36 +436,62 @@
 
 
 def field_kernel(
-    compat, compat_t, centre, inner_feat, inner_rest, outer_feat, outer_rest, inner_corner,
-    outer_corner, from_left, from_right, feat_out, kern_out, prob0_out, prob1_out, grad1_out,
-    grad0_out, unary_out, share,
-    feat, feat_turned, norm, norm_turned, kern, unary, grad, prob0, prob1, grad1, grad0,
-    turned, message0, message1, logit1, logit0, turner,
+    square_in, centre_in, from_left_in, from_right_in, inner_feat_in, inner_rest_in,
+    outer_feat_in, outer_rest_in, inner_corner_in, outer_corner_in, main_in,
+    feat_out, kern_out, prob0_out, prob1_out, grad1_out, grad0_out, unary_out, share,
+    centre, from_left, from_right, inner_feat, inner_rest, outer_feat, outer_rest, inner_corner,
+    outer_corner, main, short, side_feat, side_turned, side_size, side_size_turned, side_kern,
+    kern, unary, grad, prob0,
+    prob1, grad1, grad0, turned, message0, message1, logit1, logit0, side_turner, square, compat, compat_t,
+    in_sems, out_sems,
 ):
+    coming = fetch(
+        [
+            (centre_in, centre), (from_left_in, from_left), (from_right_in, from_right),
+            (inner_feat_in, inner_feat), (inner_rest_in, inner_rest),
+            (outer_feat_in, outer_feat), (outer_rest_in, outer_rest),
+            (inner_corner_in, inner_corner), (outer_corner_in, outer_corner), (main_in, main),
+        ],
+        in_sems,
+    )
+    going = []
+
+    def send(source, target, low):
+        copy = pltpu.make_async_copy(
+            source.at[pl.ds(low, target.shape[0])], target, out_sems.at[len(going)]
+        )
+        copy.start()
+        going.append(copy)
+
     height = centre.shape[0]
     rows = height + 2 * HALO
-    channels = feat.shape[1]
+    channels = short.shape[1]
     side = lane()
-
-    feat[pl.ds(0, REACH)] = jnp.zeros((REACH,) + feat.shape[1:], jnp.float32)
-    feat[pl.ds(rows + REACH, REACH)] = jnp.zeros((REACH,) + feat.shape[1:], jnp.float32)
-
-    def put(row, main, left, left_at, right, right_at):
-        moved_right = pltpu.roll(right, (128 - right_at) % 128, axis=1)
-        moved_left = pltpu.roll(left, (128 - STRIP - left_at) % 128, axis=1)
-        edge = jnp.where(side < 64, moved_right, moved_left)
-        for value, cols in ((main, slice(0, 128)), (edge, slice(128, 256))):
-            feat[row + REACH, :, cols] = value[0:channels]
+    side_turner[...] = side_turns()
+    square[...] = jnp.zeros_like(square)
+    square[0 : square_in.shape[0], 0 : square_in.shape[1]] = square_in[...]
+    compat[...] = spread(square[...])
+    compat_t[...] = spread(square[...].T)
+
+    for at in (0, rows + REACH):
+        short[pl.ds(at, REACH)] = jnp.zeros((REACH, channels, 256), jnp.bfloat16)
+
+    def put(row, own, left, left_at, right, right_at):
+        edge = strip_edge(left, left_at, right, right_at)
+        for value, cols in ((own, slice(0, 128)), (edge, slice(128, 256))):
+            short[row + REACH, :, cols] = value[0:channels].astype(jnp.bfloat16)
             unary[row, :, cols] = value[channels : channels + PAD]
             if value.shape[0] > channels + PAD:
                 grad[row, :, cols] = value[channels + PAD :]
 
+    wait(coming[:3])
     for y in range(height):
         at = (y % 8) * STRIP
         put(HALO + y, centre[y], from_left[y // 8], at, from_right[y // 8], at)
 
+    wait(coming[3:])
     depth = channels + 2 * PAD
-    short = channels + PAD
+    slim = channels + PAD
     near = HALO // 2
 
     def edge_row(feat_in, rest_in, i, top):
@@ -324,7 +501,7 @@
             parts.append(rest_in[HALO + row])
         return jnp.concatenate(parts, axis=0)
 
-    def put_rows(main, corner, top):
+    def put_rows(edge_rows, corner, top):
         base = HALO + height if top else 0
         half = HALO - 8
         for i in range(HALO):
@@ -333,20 +510,20 @@
                 left, right = corner[pl.ds(0, depth)], corner[pl.ds(depth, depth)]
                 left_at = right_at = at
             else:
-                left = right = corner[pl.ds(2 * depth, short)]
+                left = right = corner[pl.ds(2 * depth, slim)]
                 left_at = (i - 8) * STRIP if top else 64 + i * STRIP
                 right_at = (left_at + 64) % 128
-            rows_main = main(i, top)
-            size = min(rows_main.shape[0], left.shape[0])
-            put(base + i, rows_main[0:size], left[0:size], left_at, right[0:size], right_at)
+            own = edge_rows(i, top)
+            size = min(own.shape[0], left.shape[0])
+            put(base + i, own[0:size], left[0:size], left_at, right[0:size], right_at)
 
     even, has_left, has_right, first_row, all_rows = position(height)
-    for main, corner, below in (
+    for edge_rows, corner, below in (
         (functools.partial(edge_row, inner_feat, inner_rest), inner_corner, even),
         (functools.partial(edge_row, outer_feat, outer_rest), outer_corner, jnp.logical_not(even)),
     ):
-        pl.when(below)(functools.partial(put_rows, main, corner, True))
-        pl.when(jnp.logical_not(below))(functools.partial(put_rows, main, corner, False))
+        pl.when(below)(functools.partial(put_rows, edge_rows, corner, True))
+        pl.when(jnp.logical_not(below))(functools.partial(put_rows, edge_rows, corner, False))
 
     wide_lane = lane(256)
     inside_lane = (
@@ -359,58 +536,30 @@
         row = first_row + y
         return inside_lane & (row >= 0) & (row < all_rows)
 
-    turner[...] = turns(range(1, REACH + 1), 256)
-    tall = rows + 2 * REACH
-    moved = jnp.dot(
-        feat[...].reshape(tall * channels, 256).astype(jnp.bfloat16),
-        turner[...],
-        preferred_element_type=jnp.float32,
-    )
+    send(short, feat_out, HALO)
+    slots = rows // GROUPS
+    tall = slots + 2 * REACH
+    stacked = jnp.concatenate(
+        [
+            jnp.concatenate([short[slots * j + k] for j in range(GROUPS)], axis=1)
+            for k in range(tall)
+        ],
+        axis=0,
+    )
+    moved = jnp.dot(stacked, side_turner[...], preferred_element_type=jnp.float32)
+    side_feat[...] = moved[:, 0:128].reshape(tall, channels, 128)
     for group in range(REACH):
-        feat_turned[group] = moved[:, 256 * group : 256 * group + 256].reshape(
-            tall, channels, 256
-        )
-
-    def turn_norm(row):
-        value = feat[row]
-        size = fold(value * value) * 0.5
-        norm[row] = size
-        for group in range(REACH):
-            norm_turned[group, row] = shifted(size, group + 1)
-
-    each_row(0, rows + 2 * REACH, (rows + 2 * REACH) // 2, turn_norm)
-
-    sub = sublane()
-
-    def affinity_rows(y):
-        for tile in range(2):
-            cols = pl.ds(128 * tile, 128)
-            here = [feat[y + i + REACH, :, cols] for i in range(2)]
-            size = [norm[y + i + REACH, :, cols] for i in range(2)]
-            for group in range(REACH):
-                parts = [[], []]
-                for row in range(-REACH, REACH + 2):
-                    there = feat_turned[group, y + row + REACH, :, cols]
-                    other = norm_turned[group, y + row + REACH, :, cols]
-                    for i in range(2):
-                        if -REACH <= row - i <= REACH:
-                            parts[i].append(fold(here[i] * there) - (size[i] + other))
-                step_a = jnp.where(sub == 7, group + 1, sub - REACH)
-                step_b = jnp.where(sub == 7, 0, group + 1)
-                far = (step_a * step_a + step_b * step_b).astype(jnp.float32)
-                for i in range(2):
-                    below = y + i + group + 1 + REACH
-                    parts[i].append(
-                        fold(here[i] * feat[below, :, cols]) - (size[i] + norm[below, :, cols])
-                    )
-                    kern[y + i, pl.ds(8 * group, 8), cols] = jnp.exp(
-                        merge(parts[i]) - far * (1.0 / (2.0 * REACH * REACH))
-                    )
-
-    def affinity_turn(turn):
-        affinity_rows(2 * turn)
-
-    each_row(0, rows // 2, 1, affinity_turn)
+        start = 128 * group + 128
+        side_turned[group] = moved[:, start : start + 128].reshape(tall, channels, 128)
+    sizes(side_feat, side_turned, side_size, side_size_turned)
+    affinities(side_feat, side_turned, side_size, side_size_turned, side_kern)
+    for j in range(GROUPS):
+        for k in range(slots):
+            y, value = slots * j + k, side_kern[k]
+            kern[y, :, 128:256] = pltpu.roll(value, (116 - 32 * j) % 128, axis=1)
+            last = pltpu.roll(value, (101 - 32 * j) % 128, axis=1)
+            kern[y, :, 0:128] = jnp.where(side < 128 - REACH, main[y], last)
+    send(kern, kern_out, HALO - REACH)
 
     def put_field(field, y, value):
         field[y] = value
@@ -421,6 +570,7 @@
         put_field(prob0, y, jnp.where(inside(y), softmax(unary[y]), 0.0))
 
     each_row(0, rows, rows // 2, start)
+    send(prob0, prob0_out, HALO - REACH)
 
     def run_pass(field, out, low, high):
         def body(y):
@@ -435,6 +585,7 @@
         put_field(prob1, y, jnp.where(inside(y), value, 0.0))
 
     each_row(REACH, rows - REACH, rows, mix)
+    send(prob1, prob1_out, HALO - REACH)
     run_pass(prob1, message1, 2 * REACH, rows - 2 * REACH)
 
     def back1(y):
@@ -445,6 +596,7 @@
         put_field(grad1, y, jnp.where(inside(y), -apply(compat_t[...], change), 0.0))
 
     each_row(2 * REACH, rows - 2 * REACH, rows, back1)
+    send(grad1, grad1_out, HALO - REACH)
     def share_of(change, message):
         block = range(HALO, HALO + height)
         left = jnp.concatenate([change[y, :, 0:128] for y in block], axis=1)
@@ -462,6 +614,7 @@
         grad0[y] = jnp.where(inside(y), -apply(compat_t[...], change), 0.0)
 
     each_row(3 * REACH, rows - 3 * REACH, rows, back0)
+    send(grad0, grad0_out, HALO - REACH)
     total = total - share_of(logit0, message0)
 
     total = jnp.concatenate([total, jnp.zeros((PAD, 128 - PAD), jnp.float32)], axis=1)
@@ -473,29 +626,20 @@
     for slot in range(share.shape[0]):
         share[slot] = packed
 
-    def copy(row):
-        at = row + HALO - REACH
-        feat_out[row] = feat[at + REACH].astype(jnp.bfloat16)
-        prob0_out[row] = prob0[at]
-        prob1_out[row] = prob1[at]
-        grad1_out[row] = grad1[at]
-        grad0_out[row] = grad0[at]
-        kern_out[row] = kern[at]
-
-    each_row(0, height + 2 * REACH, 2, copy)
-
     def add_logit(y):
         unary_out[y] = logit0[y + HALO, :, 0:128] + logit1[y + HALO, :, 0:128]
 
-    each_row(0, height, 4, add_logit)
-
-
-def iterate(compat, centre, received, devices):
+    each_row(0, height, height, add_logit)
+    wait(going)
+
+
+def iterate(compat, centre, received, main, devices):
     height, depth, _ = centre.shape
     channels = depth - 2 * PAD
     rows = height + 2 * HALO
     tall = rows + 2 * REACH
     near = height + 2 * REACH
+    slots = rows // GROUPS
 
     def shape(*dims):
         return jax.ShapeDtypeStruct(dims, jnp.float32)
@@ -515,27 +659,45 @@
             shape(height, PAD, 128),
             shape(devices, 8, 128),
         ),
-        in_specs=[VMEM] * (3 + len(received)),
-        out_specs=(VMEM,) * 8,
+        in_specs=[VMEM] + [ANY] * (2 + len(received)),
+        out_specs=(ANY,) * 6 + (VMEM,) * 2,
         scratch_shapes=[
-            room(tall, channels, 256),
-            room(REACH, tall, channels, 256),
-            room(tall, 8, 256),
-            room(REACH, tall, 8, 256),
+            like(centre),
+            *map(like, received),
+            like(main),
+            pltpu.VMEM((tall, channels, 256), jnp.bfloat16),
+            room(slots + 2 * REACH, channels, 128),
+            room(REACH, slots + 2 * REACH, channels, 128),
+            room(slots + 2 * REACH, 8, 128),
+            room(REACH, slots + 2 * REACH, 8, 128),
+            room(slots, PAD, 128),
             *[room(rows, PAD, 256)] * 7,
             room(REACH, rows, PAD, 256),
             *[room(rows, PAD, 256)] * 4,
-            pltpu.VMEM((256, REACH * 256), jnp.bfloat16),
+            pltpu.VMEM((GROUPS * 256, (REACH + 1) * 128), jnp.bfloat16),
+            room(128, 128),
+            pltpu.VMEM((DEEP, 6 * PAD), jnp.bfloat16),
+            pltpu.VMEM((DEEP, 6 * PAD), jnp.bfloat16),
+            pltpu.SemaphoreType.DMA((2 + len(received),)),
+            pltpu.SemaphoreType.DMA((6,)),
         ],
         compiler_params=params(56),
         name="iterate",
-    )(spread(compat), spread(compat.T), centre, *received)
+    )(compat, centre, *received, main)
 
 
 def finish_kernel(
-    feat, kern, prob0, prob1, grad1, grad0, partial, unary_out, feat_out,
-    feat_turned, all_turned, kern_back, weights, turner,
+    feat_in, kern_in, prob0_in, prob1_in, grad1_in, grad0_in, partial_in, unary_out, feat_out,
+    feat, kern, prob0, prob1, grad1, grad0, partial, feat_turned, all_turned, kern_back, weights,
+    turner, unary_rows, in_sems, out_sem,
 ):
+    coming = fetch(
+        [
+            (feat_in, feat), (kern_in, kern), (prob0_in, prob0), (prob1_in, prob1),
+            (grad1_in, grad1), (grad0_in, grad0), (partial_in, partial),
+        ],
+        in_sems,
+    )
     height = partial.shape[0]
     near = height + 2 * REACH
     channels = feat.shape[1]
@@ -551,11 +713,14 @@
         mixed = jnp.where((column < b) if b > 0 else (column >= 128 + b), edge, main)
         return pltpu.roll(mixed, (-b) % 128, axis=1)
 
+    wait(coming[:1])
     full = jnp.dot(
         feat[...].reshape(near * channels, 256), turner[...], preferred_element_type=jnp.float32
     )
     for place in range(len(steps)):
         feat_turned[place] = full[:, 128 * place : 128 * place + 128].reshape(near, channels, 128)
+
+    wait(coming[1:])
 
     def prepare(row):
         for place, field in enumerate((prob0, prob1, grad1, grad0)):
@@ -595,11 +760,13 @@
         value = partial[y] + prob * (cot - jnp.sum(cot * prob, axis=0, keepdims=True))
         for start in range(0, classes, 8):
             size = min(8, classes - start)
-            unary_out[pl.ds(start * height + y, size, stride=height), :] = value[
+            unary_rows[pl.ds(start * height + y, size, stride=height), :] = value[
                 start : start + size
             ]
 
     each_row(0, height, 4, unary_row)
+    leaving = pltpu.make_async_copy(unary_rows, unary_out, out_sem)
+    leaving.start()
     sub = sublane()
 
     def feature_row(y):
@@ -639,6 +806,7 @@
         feat_out[pl.ds(y, channels, stride=height), :] = total * (1.0 / math.sqrt(channels))
 
     each_row(0, height, 1, feature_row)
+    leaving.wait()
 
 
 def finish(feat, kern, prob0, prob1, grad1, grad0, partial, classes):
@@ -654,14 +822,18 @@
             jax.ShapeDtypeStruct((classes * height, 128), jnp.float32),
             jax.ShapeDtypeStruct((channels * height, 128), jnp.float32),
         ),
-        in_specs=[VMEM] * 7,
-        out_specs=(VMEM,) * 2,
+        in_specs=[ANY] * 7,
+        out_specs=(ANY, VMEM),
         scratch_shapes=[
+            *map(like, (feat, kern, prob0, prob1, grad1, grad0, partial)),
             room(2 * REACH + 1, near, channels, 128),
             room(2 * REACH + 1, near, 4 * PAD, 128),
             room(near, PAD, 128),
             room(height, 6 * 8, 128),
             pltpu.VMEM((256, (2 * REACH + 1) * 128), jnp.bfloat16),
+            room(classes * height, 128),
+            pltpu.SemaphoreType.DMA((7,)),
+            pltpu.SemaphoreType.DMA,
         ],
         compiler_params=params(56),
         cost_estimate=pl.CostEstimate(flops=200_000_000, bytes_accessed=8_000_000, transcendentals=0),
@@ -690,17 +862,18 @@
     outer_rest = lax.ppermute(outer_rest, "rows", above)
     from_left = lax.ppermute(right, "cols", forward)
     from_right = lax.ppermute(left, "cols", backward)
-    inner_corner, outer_corner = corners(from_left, from_right, outer_rest)
+    inner_corner, outer_corner = corners(from_left, from_right, outer_feat)
     outer_corner = lax.ppermute(outer_corner, "rows", above)
     inner_corner = lax.ppermute(inner_corner, "rows", below)
+    main = main_affinities(centre, from_left, from_right, inner_feat, outer_feat)
     received = (
-        inner_feat, inner_rest, outer_feat, outer_rest, inner_corner, outer_corner,
-        from_left, from_right,
+        from_left, from_right, inner_feat, inner_rest, outer_feat, outer_rest, inner_corner,
+        outer_corner,
     )
 
     devices = n_rows * n_cols
     *fields, partial, share = iterate(
-        compat, centre, received, devices
+        compat, centre, received, main, devices
     )
     shares = lax.all_to_all(share, ("rows", "cols"), 0, 0)
     unary_grad, feature_grad = finish(*fields, partial, classes)

time: 66 us -> 62.6 us (0.948)
  waiting for transfers between devices: 8.94 us -> 4.85 us
    pallas_call x0 -> x1, Pallas kernels: none -> 6.85 us  [main_affinities(): pl.pallas_call(main_kernel, out_shape=jax.ShapeDtypeStruct((rows, PAD, 12...]
    pallas_call x1, Pallas kernels: 24.5 us -> 18.2 us  [iterate(): pl.pallas_call(field_kernel, out_shape=(jax.ShapeDtypeStruct((near, chann...]
    ppermute x1, waiting for transfers between devices: 4.19 us -> 0.01 us  [on_device(): outer_corner = lax.ppermute(outer_corner, 'rows', above)]
    ppermute x1, starting transfers between devices: 3.33 us -> 0.68 us  [on_device(): outer_rest = lax.ppermute(outer_rest, 'rows', above)]
    ppermute x1, starting transfers between devices: 0.68 us -> 3.33 us  [on_device(): outer_feat = lax.ppermute(outer_feat, 'rows', above)]
    concatenate x2 -> x0, local copies, waits for them, and re-layouts: 1.4 us -> none  [spread(): jnp.concatenate([high, high, middle, high, middle, low], axis=1)]
    unnamed x19 -> x16, local copies, waits for them, and re-layouts: 1.06 us -> 2.39 us
  transfers between devices with their start and end apart: 9 -> 9, of which waited for: 3 -> 2; matrix products, arithmetic and copies ran while one was open for 2% -> 0% of each run, Pallas kernels for 17% -> 29%
where the time goes in v7:
time: 62.6 us; the launch traced here: 62.3 us
  Pallas kernels  39.3 us (63%)
  starting transfers between devices  14.2 us (23%)
  waiting for transfers between devices  4.85 us (8%)
  local copies, waits for them, and re-layouts  2.47 us (4%)
  between operations  0.78 us (1%)
  other arithmetic  0.65 us (1%)
    pallas_call x1, Pallas kernels, iterate(): pl.pallas_call(field_kernel, out_shape=(jax.ShapeDtypeStruct((near, chann...  18.2 us
    pallas_call x1, Pallas kernels, finish(): pl.pallas_call(finish_kernel, out_shape=(jax.ShapeDtypeStruct((classes *...  10.7 us
    pallas_call x1, Pallas kernels, main_affinities(): pl.pallas_call(main_kernel, out_shape=jax.ShapeDtypeStruct((rows, PAD, 12...  6.85 us
    ppermute x1, waiting for transfers between devices, on_device(): from_right = lax.ppermute(left, 'cols', backward)  4.23 us
    all_to_all x1, starting transfers between devices, on_device(): shares = lax.all_to_all(share, ('rows', 'cols'), 0, 0)  4.12 us
    ppermute x1, starting transfers between devices, on_device(): from_left = lax.ppermute(right, 'cols', forward)  3.47 us
    ppermute x1, starting transfers between devices, on_device(): outer_feat = lax.ppermute(outer_feat, 'rows', above)  3.33 us
    pallas_call x1, Pallas kernels, pack(): pl.pallas_call(pack_kernel, out_shape=(shape(height, depth, 128), shape(h...  3.05 us
  transfers between devices with their start and end apart: 9, of which 2 were waited for; matrix products, arithmetic and copies ran while one was open for 0% of the time, Pallas kernels for 29%

profile of v7, /device:TPU:0, one launch (start us, length us, event | category | flops | bytes accessed | tf_op | source)
XLA Modules:
  0.0 62.3 jit_solution(2929316992857847021)
XLA Ops:
  0.6 3.1 %pack.1 = (f32[16,112,128]{2,1,0:T(8,128)}, f32[2,112,128]{2,1,0:T(8,128)}, f32[2,112,128]{2,1,0:T(8,128)}, bf16[12,64,128]{2,1,0:T(8,128)(2,1)}, f32[18,24,128]...) custom-call(bf16[64,16,128]{2,1,0:T(8,128)(2,1)} %feat.1, f32[336,128]{1,0:T(8,128)} %bitcast.4, ...), custom_call_target="tpu_custom_call" | custom-call | tf_op jit(solution)/shard_map/pack/pallas_call | solution.py:218
  3.7 3.3 %collective-permute-start.4 = (bf16[12,64,128]{2,1,0:T(8,128)(2,1)}, bf16[12,64,128]{2,1,0:T(8,128)(2,1)S(1)}, u32[]{:S(2)}, u32[]{:S(2)}) collective-permute-start(bf16[12,64,128]{2,1,0:T(8,128)(2,1)} %get-tuple-element.27), channel_id=1, source_target_pairs={{4,8},{8,4},{12,16},{16,12},{20,24},{24,20},{28,0},{0,28},{5,9},{9... | collective-permute-start | bytes 589832 | tf_op jit(solution)/shard_map/ppermute | solution.py:861
  7.0 3.5 %collective-permute-start = (f32[2,112,128]{2,1,0:T(8,128)}, f32[2,112,128]{2,1,0:T(8,128)S(1)}, u32[]{:S(2)}, u32[]{:S(2)}) collective-permute-start(f32[2,112,128]{2,1,0:T(8,128)} %get-tuple-element.23), channel_id=1, source_target_pairs={{0,1},{1,2},{2,3},{4,5},{5,6},{6,7},{8,9},{9,10},{10,11},{12,13},{... | collective-permute-start | bytes 344072 | tf_op jit(solution)/shard_map/ppermute | solution.py:863
  10.5 1.3 %collective-permute-start.1 = (f32[2,112,128]{2,1,0:T(8,128)}, f32[2,112,128]{2,1,0:T(8,128)S(1)}, u32[]{:S(2)}, u32[]{:S(2)}) collective-permute-start(f32[2,112,128]{2,1,0:T(8,128)} %get-tuple-element.24), channel_id=1, source_target_pairs={{1,0},{2,1},{3,2},{5,4},{6,5},{7,6},{9,8},{10,9},{11,10},{13,12},{... | collective-permute-start | bytes 344072 | tf_op jit(solution)/shard_map/ppermute | solution.py:864
  11.8 0.1 collective-permute-start.3
  11.9 0.7 %collective-permute-start.5 = (f32[18,24,128]{2,1,0:T(8,128)}, f32[18,24,128]{2,1,0:T(8,128)S(1)}, u32[]{:S(2)}, u32[]{:S(2)}) collective-permute-start(f32[18,24,128]{2,1,0:T(8,128)} %get-tuple-element.28), channel_id=1, source_target_pairs={{4,8},{8,4},{12,16},{16,12},{20,24},{24,20},{28,0},{0,28},{5,9},{9... | collective-permute-start | bytes 663560 | tf_op jit(solution)/shard_map/ppermute | solution.py:862
  12.6 0.6 collective-permute-done.left_in.from_left_in
  13.2 0.0 copy-start.1
  13.2 0.0 collective-permute-start.2
  13.2 4.2 %collective-permute-done.1.right_in.from_right_in = f32[2,112,128]{2,1,0:T(8,128)S(1)} collective-permute-done((f32[2,112,128]{2,1,0:T(8,128)}, f32[2,112,128]{2,1,0:T(8,128)S(1)}, u32[]{:S(2)}, u32[]{:S(2)}) %collective-permute-start.1) | collective-permute-done | bytes 114720 | tf_op jit(solution)/shard_map/ppermute | solution.py:864
  17.4 0.0 copy-start.2
  17.4 0.0 collective-permute-done.4._.outer_in.outer_feat_in
  17.4 0.0 copy-start
  17.4 0.4 corners.1
  17.8 0.0 copy-done.1
  17.8 0.2 copy-done.2
  18.0 0.1 copy-done
  18.1 0.0 collective-permute-start.6
  18.1 1.3 %collective-permute-start.7 = (f32[312,128]{1,0:T(8,128)S(1)}, f32[312,128]{1,0:T(8,128)S(1)}, u32[]{:S(2)}, u32[]{:S(2)}) collective-permute-start(f32[312,128]{1,0:T(8,128)S(1)} %get-tuple-element.30), channel_id=1, source_target_pairs={{4,8},{8,4},{12,16},{16,12},{20,24},{24,20},{28,0},{0,28},{5,9},{9... | collective-permute-start | bytes 479240 | tf_op jit(solution)/shard_map/ppermute | solution.py:866
  19.4 0.0 collective-permute-done.2.inner_in.inner_feat_in
  19.4 0.0 copy-start.3
  19.4 0.7 %copy-done.3 = bf16[12,64,128]{2,1,0:T(8,128)(2,1)} copy-done((bf16[12,64,128]{2,1,0:T(8,128)(2,1)}, bf16[12,64,128]{2,1,0:T(8,128)(2,1)S(1)}, u32[]{:S(2)}) %copy-start.3) | copy-done | bytes 196632
  20.1 6.9 %main_affinities.1.main_in = f32[40,24,128]{2,1,0:T(8,128)} custom-call(f32[16,112,128]{2,1,0:T(8,128)} %get-tuple-element.22.centre_in, f32[2,112,128]{2,1,0:T(8,128)} %copy-done.1, f32[2,112,128]{2,1,0:T(8,128)} %copy-done.2, bf16[12,64,128]{2,1,0:T(8,128)(2,1)} %copy-done.3, bf16[12,64,128]{2,1,0:T(8,128)(2,1)} %copy-done), custom_call_target="tpu_custom_call" | custom-call | flops 200000000 | bytes 8000000 | tf_op jit(solution)/shard_map/main_affinities/pallas_call | solution.py:371
  26.9 0.0 collective-permute-done.3.inner_rest_in
  26.9 0.0 copy-start.4
  26.9 0.0 collective-permute-done.5.outer_rest_in
  27.0 0.0 copy-start.5
  27.0 0.0 collective-permute-done.6.inner_corner_in
  27.0 0.0 copy-start.6
  27.0 0.0 collective-permute-done.7.outer_corner_in
  27.0 0.6 %copy-done.4 = f32[18,24,128]{2,1,0:T(8,128)} copy-done((f32[18,24,128]{2,1,0:T(8,128)}, f32[18,24,128]{2,1,0:T(8,128)S(1)}, u32[]{:S(2)}) %copy-start.4) | copy-done | bytes 221208
  27.6 0.1 copy-done.5
  27.7 0.0 copy-done.6
  27.7 0.0 copy-start.7
  27.8 0.7 %copy-done.7 = f32[312,128]{1,0:T(8,128)} copy-done((f32[312,128]{1,0:T(8,128)}, f32[312,128]{1,0:T(8,128)S(1)}, u32[]{:S(2)}) %copy-start.7) | copy-done | bytes 159768
  28.4 18.2 %iterate.1 = (bf16[22,64,256]{2,1,0:T(8,128)(2,1)}, f32[22,24,256]{2,1,0:T(8,128)}, f32[22,24,256]{2,1,0:T(8,128)}, f32[22,24,256]{2,1,0:T(8,128)}, f32[22,24,25...) custom-call(f32[21,21]{1,0:T(8,128)} %square_in.1, ...), custom_call_target="tpu_custom_call" | custom-call | tf_op jit(solution)/shard_map/iterate/pallas_call | solution.py:650
  46.7 4.1 %all-to-all-start = ((f32[32,8,128]{2,1,0:T(8,128)}), f32[32,8,128]{2,1,0:T(8,128)S(1)}, u32[]{:S(2)}, u32[]{:S(2)}) async-start(f32[32,8,128]{2,1,0:T(8,128)} %get-tuple-element.40), calls=%async_computation | async-start | bytes 262144 | tf_op jit(solution)/shard_map/all_to_all | solution.py:878
  50.8 10.7 %finish.1 = (f32[336,128]{1,0:T(8,128)}, f32[1024,128]{1,0:T(8,128)}) custom-call(bf16[22,64,256]{2,1,0:T(8,128)(2,1)} %get-tuple-element.31.feat_in, f32[22,24,256]{2,1,0:T(8,128)} %get-tuple-element.32.kern_in, f32[22,24,256]{2,1,0:T(8,128)} %get-tuple-element.33.prob0_in, f32[22,24,256]{2,1,0:T(8,128)} %get-tuple-element.34.prob1_in, ...), custom_call_target="tpu_custom_call" | custom-call | flops 200000000 | bytes 8000000 | tf_op jit(solution)/shard_map/finish/pallas_call | solution.py:819
  61.5 0.0 all-to-all-done
  61.6 0.1 fusion
  61.6 0.6 pad_maximum_fusion
  (2 shorter events, 0.0 us)
Async XLA Ops:
  3.7 13.7 %collective-permute-start.4 = (bf16[12,64,128]{2,1,0:T(8,128)(2,1)}, bf16[12,64,128]{2,1,0:T(8,128)(2,1)S(1)}, u32[]{:S(2)}, u32[]{:S(2)}) collective-permute-start(bf16[12,64,128]{2,1,0:T(8,128)(2,1)} %get-tuple-element.27), channel_id=1, source_target_pairs={{4,8},{8,4},{12,16},{16,12},{20,24},{24,20},{28,0},{0,28},{5,9},{9... | collective-permute-start | bytes 589832 | tf_op jit(solution)/shard_map/ppermute | solution.py:861
  7.0 6.1 %collective-permute-start = (f32[2,112,128]{2,1,0:T(8,128)}, f32[2,112,128]{2,1,0:T(8,128)S(1)}, u32[]{:S(2)}, u32[]{:S(2)}) collective-permute-start(f32[2,112,128]{2,1,0:T(8,128)} %get-tuple-element.23), channel_id=1, source_target_pairs={{0,1},{1,2},{2,3},{4,5},{5,6},{6,7},{8,9},{9,10},{10,11},{12,13},{... | collective-permute-start | bytes 344072 | tf_op jit(solution)/shard_map/ppermute | solution.py:863
  10.5 6.9 %collective-permute-start.1 = (f32[2,112,128]{2,1,0:T(8,128)}, f32[2,112,128]{2,1,0:T(8,128)S(1)}, u32[]{:S(2)}, u32[]{:S(2)}) collective-permute-start(f32[2,112,128]{2,1,0:T(8,128)} %get-tuple-element.24), channel_id=1, source_target_pairs={{1,0},{2,1},{3,2},{5,4},{6,5},{7,6},{9,8},{10,9},{11,10},{13,12},{... | collective-permute-start | bytes 344072 | tf_op jit(solution)/shard_map/ppermute | solution.py:864
  11.8 15.1 %collective-permute-start.3 = (f32[18,24,128]{2,1,0:T(8,128)}, f32[18,24,128]{2,1,0:T(8,128)S(1)}, u32[]{:S(2)}, u32[]{:S(2)}) collective-permute-start(f32[18,24,128]{2,1,0:T(8,128)} %get-tuple-element.26), channel_id=1, source_target_pairs={{0,4},{4,0},{8,12},{12,8},{16,20},{20,16},{24,28},{28,24},{1,5},{5... | collective-permute-start | bytes 663560 | tf_op jit(solution)/shard_map/ppermute | solution.py:860
  11.9 15.1 %collective-permute-start.5 = (f32[18,24,128]{2,1,0:T(8,128)}, f32[18,24,128]{2,1,0:T(8,128)S(1)}, u32[]{:S(2)}, u32[]{:S(2)}) collective-permute-start(f32[18,24,128]{2,1,0:T(8,128)} %get-tuple-element.28), channel_id=1, source_target_pairs={{4,8},{8,4},{12,16},{16,12},{20,24},{24,20},{28,0},{0,28},{5,9},{9... | collective-permute-start | bytes 663560 | tf_op jit(solution)/shard_map/ppermute | solution.py:862
  13.2 4.7 %copy-start.1 = (f32[2,112,128]{2,1,0:T(8,128)}, f32[2,112,128]{2,1,0:T(8,128)S(1)}, u32[]{:S(2)}) copy-start(f32[2,112,128]{2,1,0:T(8,128)S(1)} %collective-permute-done.left_in.from_left_in) | copy-start | bytes 344068
  13.2 6.2 %collective-permute-start.2 = (bf16[12,64,128]{2,1,0:T(8,128)(2,1)}, bf16[12,64,128]{2,1,0:T(8,128)(2,1)S(1)}, u32[]{:S(2)}, u32[]{:S(2)}) collective-permute-start(bf16[12,64,128]{2,1,0:T(8,128)(2,1)} %get-tuple-element.25), channel_id=1, source_target_pairs={{0,4},{4,0},{8,12},{12,8},{16,20},{20,16},{24,28},{28,24},{1,5},{5... | collective-permute-start | bytes 589832 | tf_op jit(solution)/shard_map/ppermute | solution.py:859
  17.4 0.7 %copy-start.2 = (f32[2,112,128]{2,1,0:T(8,128)}, f32[2,112,128]{2,1,0:T(8,128)S(1)}, u32[]{:S(2)}) copy-start(f32[2,112,128]{2,1,0:T(8,128)S(1)} %collective-permute-done.1.right_in.from_right_in) | copy-start | bytes 344068
  17.4 0.7 %copy-start = (bf16[12,64,128]{2,1,0:T(8,128)(2,1)}, bf16[12,64,128]{2,1,0:T(8,128)(2,1)S(1)}, u32[]{:S(2)}) copy-start(bf16[12,64,128]{2,1,0:T(8,128)(2,1)S(1)} %collective-permute-done.4._.outer_in.outer_feat_in) | copy-start | bytes 589828
  18.1 8.9 %collective-permute-start.6 = (f32[312,128]{1,0:T(8,128)S(1)}, f32[312,128]{1,0:T(8,128)S(1)}, u32[]{:S(2)}, u32[]{:S(2)}) collective-permute-start(f32[312,128]{1,0:T(8,128)S(1)} %get-tuple-element.29), channel_id=1, source_target_pairs={{0,4},{4,0},{8,12},{12,8},{16,20},{20,16},{24,28},{28,24},{1,5},{5... | collective-permute-start | bytes 479240 | tf_op jit(solution)/shard_map/ppermute | solution.py:867
  18.1 8.9 %collective-permute-start.7 = (f32[312,128]{1,0:T(8,128)S(1)}, f32[312,128]{1,0:T(8,128)S(1)}, u32[]{:S(2)}, u32[]{:S(2)}) collective-permute-start(f32[312,128]{1,0:T(8,128)S(1)} %get-tuple-element.30), channel_id=1, source_target_pairs={{4,8},{8,4},{12,16},{16,12},{20,24},{24,20},{28,0},{0,28},{5,9},{9... | collective-permute-start | bytes 479240 | tf_op jit(solution)/shard_map/ppermute | solution.py:866
  19.4 0.7 %copy-start.3 = (bf16[12,64,128]{2,1,0:T(8,128)(2,1)}, bf16[12,64,128]{2,1,0:T(8,128)(2,1)S(1)}, u32[]{:S(2)}) copy-start(bf16[12,64,128]{2,1,0:T(8,128)(2,1)S(1)} %collective-permute-done.2.inner_in.inner_feat_in) | copy-start | bytes 589828
  26.9 0.7 %copy-start.4 = (f32[18,24,128]{2,1,0:T(8,128)}, f32[18,24,128]{2,1,0:T(8,128)S(1)}, u32[]{:S(2)}) copy-start(f32[18,24,128]{2,1,0:T(8,128)S(1)} %collective-permute-done.3.inner_rest_in) | copy-start | bytes 663556
  27.0 0.8 %copy-start.5 = (f32[18,24,128]{2,1,0:T(8,128)}, f32[18,24,128]{2,1,0:T(8,128)S(1)}, u32[]{:S(2)}) copy-start(f32[18,24,128]{2,1,0:T(8,128)S(1)} %collective-permute-done.5.outer_rest_in) | copy-start | bytes 663556
  27.0 0.8 %copy-start.6 = (f32[312,128]{1,0:T(8,128)}, f32[312,128]{1,0:T(8,128)S(1)}, u32[]{:S(2)}) copy-start(f32[312,128]{1,0:T(8,128)S(1)} %collective-permute-done.6.inner_corner_in) | copy-start | bytes 479236
  27.7 0.7 %copy-start.7 = (f32[312,128]{1,0:T(8,128)}, f32[312,128]{1,0:T(8,128)S(1)}, u32[]{:S(2)}) copy-start(f32[312,128]{1,0:T(8,128)S(1)} %collective-permute-done.7.outer_corner_in) | copy-start | bytes 479236
  46.7 14.9 %all-to-all-start = ((f32[32,8,128]{2,1,0:T(8,128)}), f32[32,8,128]{2,1,0:T(8,128)S(1)}, u32[]{:S(2)}, u32[]{:S(2)}) async-start(f32[32,8,128]{2,1,0:T(8,128)} %get-tuple-element.40), calls=%async_computation | async-start | bytes 262144 | tf_op jit(solution)/shard_map/all_to_all | solution.py:878

commit v8 on v7

--- a/solution.py
+++ b/solution.py
@@ -163,14 +163,20 @@
 
 
 def pack_kernel(
-    feat, unary, grad, centre, left, right, inner_feat, inner_rest, outer_feat, outer_rest, wide
+    feat, unary, grad, centre, left, right, inner_feat, inner_rest, outer_feat, outer_rest, wide,
+    wide_unary, wide_grad,
 ):
     channels, height, _ = feat.shape
     classes = unary.shape[0] // height
     wide[...] = feat[...].astype(jnp.float32).reshape(channels * height, 128) * (
         1.0 / math.sqrt(channels)
     )
-    empty = jnp.zeros((PAD - classes, 128), jnp.float32)
+    for source, target, fill in ((unary, wide_unary, LOW), (grad, wide_grad, 0.0)):
+        size = classes * height
+        target[pl.ds(0, size)] = source[...]
+        target[pl.ds(size, PAD * height - size)] = jnp.full(
+            (PAD * height - size, 128), fill, jnp.float32
+        )
     side = lane()
     for slot in range(height // 8):
         ends = [None, None]
@@ -179,10 +185,8 @@
             rows = jnp.concatenate(
                 [
                     wide[pl.ds(y, channels, stride=height), :],
-                    unary[pl.ds(y, classes, stride=height), :],
-                    empty + LOW,
-                    grad[pl.ds(y, classes, stride=height), :],
-                    empty,
+                    wide_unary[pl.ds(y, PAD, stride=height), :],
+                    wide_grad[pl.ds(y, PAD, stride=height), :],
                 ],
                 axis=0,
             )
@@ -228,7 +232,9 @@
         ),
         in_specs=[VMEM] * 3,
         out_specs=(VMEM,) * 7,
-        scratch_shapes=[pltpu.VMEM((channels * height, 128), jnp.float32)],
+        scratch_shapes=[
+            pltpu.VMEM((count * height, 128), jnp.float32) for count in (channels, PAD, PAD)
+        ],
         compiler_params=params(56),
         name="pack",
     )(feat, unary.reshape(-1, 128), grad.reshape(-1, 128))
@@ -314,43 +320,30 @@
 
 
 def main_kernel(
-    centre_in, from_left_in, from_right_in, inner_in, outer_in, kern_out,
-    centre, from_left, from_right, inner, outer, feat, short, turned, size, size_turned, turner,
-    sems,
+    centre_in, inner_in, outer_in, kern_out,
+    centre, inner, outer, feat, short, turned, size, size_turned, turner, sems,
 ):
-    coming = fetch(
-        [
-            (inner_in, inner), (outer_in, outer), (centre_in, centre),
-            (from_left_in, from_left), (from_right_in, from_right),
-        ],
-        sems,
-    )
+    coming = fetch([(inner_in, inner), (outer_in, outer), (centre_in, centre)], sems)
     height, channels = centre.shape[0], feat.shape[1]
     tall = feat.shape[0]
-    turner[...] = turns(range(1, REACH + 1), 128)
-    blank = jnp.zeros((REACH, channels, 128), jnp.float32)
+    turner[...] = turns(range(1, REACH + 1), 128)[0:128]
     for at in (0, tall - REACH):
-        feat[pl.ds(at, REACH)] = blank
-        short[pl.ds(at, REACH)] = jnp.zeros((REACH, channels, 256), jnp.bfloat16)
+        feat[pl.ds(at, REACH)] = jnp.zeros((REACH, channels, 128), jnp.float32)
+        short[pl.ds(at, REACH)] = jnp.zeros((REACH, channels, 128), jnp.bfloat16)
     even = position(height)[0]
     wait(coming)
     above = jnp.where(even, REACH + HALO + height, REACH)
     for source, base in ((inner, above), (outer, tall - HALO - above)):
         for i in range(HALO):
             feat[base + i] = source[i].astype(jnp.float32)
-            short[base + i, :, 0:128] = source[i]
-            short[base + i, :, 128:256] = jnp.zeros((channels, 128), jnp.bfloat16)
+            short[base + i] = source[i]
     for y in range(height):
-        at = (y % 8) * STRIP
         row = y + HALO + REACH
-        feat[row] = centre[y, 0:channels]
-        short[row, :, 0:128] = centre[y, 0:channels].astype(jnp.bfloat16)
-        edge = strip_edge(
-            from_left[y // 8, 0:channels], at, from_right[y // 8, 0:channels], at
-        )
-        short[row, :, 128:256] = edge.astype(jnp.bfloat16)
+        value = centre[y, 0:channels]
+        feat[row] = value
+        short[row] = value.astype(jnp.bfloat16)
     moved = jnp.dot(
-        short[...].reshape(tall * channels, 256), turner[...], preferred_element_type=jnp.float32
+        short[...].reshape(tall * channels, 128), turner[...], preferred_element_type=jnp.float32
     )
     for group in range(REACH):
         turned[group] = moved[:, 128 * group : 128 * group + 128].reshape(tall, channels, 128)
@@ -358,12 +351,12 @@
     affinities(feat, turned, size, size_turned, kern_out)
 
 
-def main_affinities(centre, from_left, from_right, inner, outer):
+def main_affinities(centre, inner, outer):
     height, depth, _ = centre.shape
     channels = depth - 2 * PAD
     rows = height + 2 * HALO
     tall = rows + 2 * REACH
-    inputs = (centre, from_left, from_right, inner, outer)
+    inputs = (centre, inner, outer)
 
     def room(*dims, dtype=jnp.float32):
         return pltpu.VMEM(dims, dtype)
@@ -371,19 +364,19 @@
     return pl.pallas_call(
         main_kernel,
         out_shape=jax.ShapeDtypeStruct((rows, PAD, 128), jnp.float32),
-        in_specs=[ANY] * 5,
+        in_specs=[ANY] * 3,
         out_specs=VMEM,
         scratch_shapes=[
             *map(like, inputs),
             room(tall, channels, 128),
-            room(tall, channels, 256, dtype=jnp.bfloat16),
+            room(tall, channels, 128, dtype=jnp.bfloat16),
             room(REACH, tall, channels, 128),
             room(tall, 8, 128),
             room(REACH, tall, 8, 128),
-            room(256, REACH * 128, dtype=jnp.bfloat16),
-            pltpu.SemaphoreType.DMA((5,)),
+            room(128, REACH * 128, dtype=jnp.bfloat16),
+            pltpu.SemaphoreType.DMA((3,)),
         ],
-        compiler_params=params(56),
+        compiler_params=params(16),
         cost_estimate=pl.CostEstimate(
             flops=200_000_000, bytes_accessed=8_000_000, transcendentals=0
         ),
@@ -438,7 +431,7 @@
 def field_kernel(
     square_in, centre_in, from_left_in, from_right_in, inner_feat_in, inner_rest_in,
     outer_feat_in, outer_rest_in, inner_corner_in, outer_corner_in, main_in,
-    feat_out, kern_out, prob0_out, prob1_out, grad1_out, grad0_out, unary_out, share,
+    feat_out, kern_out, prob0_out, prob1_out, grad1_out, grad0_out, share,
     centre, from_left, from_right, inner_feat, inner_rest, outer_feat, outer_rest, inner_corner,
     outer_corner, main, short, side_feat, side_turned, side_size, side_size_turned, side_kern,
     kern, unary, grad, prob0,
@@ -454,6 +447,7 @@
         ],
         in_sems,
     )
+    height = centre.shape[0]
     going = []
 
     def send(source, target, low):
@@ -463,7 +457,6 @@
         copy.start()
         going.append(copy)
 
-    height = centre.shape[0]
     rows = height + 2 * HALO
     channels = short.shape[1]
     side = lane()
@@ -596,7 +589,6 @@
         put_field(grad1, y, jnp.where(inside(y), -apply(compat_t[...], change), 0.0))
 
     each_row(2 * REACH, rows - 2 * REACH, rows, back1)
-    send(grad1, grad1_out, HALO - REACH)
     def share_of(change, message):
         block = range(HALO, HALO + height)
         left = jnp.concatenate([change[y, :, 0:128] for y in block], axis=1)
@@ -614,7 +606,6 @@
         grad0[y] = jnp.where(inside(y), -apply(compat_t[...], change), 0.0)
 
     each_row(3 * REACH, rows - 3 * REACH, rows, back0)
-    send(grad0, grad0_out, HALO - REACH)
     total = total - share_of(logit0, message0)
 
     total = jnp.concatenate([total, jnp.zeros((PAD, 128 - PAD), jnp.float32)], axis=1)
@@ -626,10 +617,19 @@
     for slot in range(share.shape[0]):
         share[slot] = packed
 
+    middle = (side >= 32) & (side < 96)
+
     def add_logit(y):
-        unary_out[y] = logit0[y + HALO, :, 0:128] + logit1[y + HALO, :, 0:128]
+        at = y + HALO
+        value = logit0[at, :, 0:128] + logit1[at, :, 0:128]
+        for field, shift in ((grad1, 32), (grad0, 96)):
+            field[at, :, 128:256] = jnp.where(
+                middle, pltpu.roll(value, shift, axis=1), field[at, :, 128:256]
+            )
 
     each_row(0, height, height, add_logit)
+    send(grad1, grad1_out, HALO - REACH)
+    send(grad0, grad0_out, HALO - REACH)
     wait(going)
 
 
@@ -656,11 +656,10 @@
             shape(near, PAD, 256),
             shape(near, PAD, 256),
             shape(near, PAD, 256),
-            shape(height, PAD, 128),
             shape(devices, 8, 128),
         ),
         in_specs=[VMEM] + [ANY] * (2 + len(received)),
-        out_specs=(ANY,) * 6 + (VMEM,) * 2,
+        out_specs=(ANY,) * 6 + (VMEM,),
         scratch_shapes=[
             like(centre),
             *map(like, received),
@@ -681,25 +680,25 @@
             pltpu.SemaphoreType.DMA((2 + len(received),)),
             pltpu.SemaphoreType.DMA((6,)),
         ],
-        compiler_params=params(56),
+        compiler_params=params(28),
         name="iterate",
     )(compat, centre, *received, main)
 
 
 def finish_kernel(
-    feat_in, kern_in, prob0_in, prob1_in, grad1_in, grad0_in, partial_in, unary_out, feat_out,
-    feat, kern, prob0, prob1, grad1, grad0, partial, feat_turned, all_turned, kern_back, weights,
+    feat_in, kern_in, prob0_in, prob1_in, grad1_in, grad0_in, unary_out, feat_out,
+    feat, kern, prob0, prob1, grad1, grad0, feat_turned, all_turned, kern_back, weights,
     turner, unary_rows, in_sems, out_sem,
 ):
     coming = fetch(
         [
             (feat_in, feat), (kern_in, kern), (prob0_in, prob0), (prob1_in, prob1),
-            (grad1_in, grad1), (grad0_in, grad0), (partial_in, partial),
+            (grad1_in, grad1), (grad0_in, grad0),
         ],
         in_sems,
     )
-    height = partial.shape[0]
-    near = height + 2 * REACH
+    near = feat.shape[0]
+    height = near - 2 * REACH
     channels = feat.shape[1]
     classes = unary_out.shape[0] // height
     steps = range(-REACH, REACH + 1)
@@ -757,15 +756,19 @@
     def unary_row(y):
         cot = pass_centre(y + REACH)
         prob = prob0[y + REACH, :, 0:128]
-        value = partial[y] + prob * (cot - jnp.sum(cot * prob, axis=0, keepdims=True))
-        for start in range(0, classes, 8):
-            size = min(8, classes - start)
-            unary_rows[pl.ds(start * height + y, size, stride=height), :] = value[
-                start : start + size
-            ]
+        row = y + REACH
+        partial = jnp.where(
+            column < 64,
+            pltpu.roll(grad1[row, :, 128:256], 96, axis=1),
+            pltpu.roll(grad0[row, :, 128:256], 32, axis=1),
+        )
+        value = partial + prob * (cot - jnp.sum(cot * prob, axis=0, keepdims=True))
+        unary_rows[pl.ds(y, PAD, stride=height), :] = value
 
     each_row(0, height, 4, unary_row)
-    leaving = pltpu.make_async_copy(unary_rows, unary_out, out_sem)
+    leaving = pltpu.make_async_copy(
+        unary_rows.at[pl.ds(0, classes * height)], unary_out, out_sem
+    )
     leaving.start()
     sub = sublane()
 
@@ -809,9 +812,9 @@
     leaving.wait()
 
 
-def finish(feat, kern, prob0, prob1, grad1, grad0, partial, classes):
+def finish(feat, kern, prob0, prob1, grad1, grad0, classes):
     near, channels, _ = feat.shape
-    height = partial.shape[0]
+    height = near - 2 * REACH
 
     def room(*dims):
         return pltpu.VMEM(dims, jnp.float32)
@@ -822,23 +825,23 @@
             jax.ShapeDtypeStruct((classes * height, 128), jnp.float32),
             jax.ShapeDtypeStruct((channels * height, 128), jnp.float32),
         ),
-        in_specs=[ANY] * 7,
+        in_specs=[ANY] * 6,
         out_specs=(ANY, VMEM),
         scratch_shapes=[
-            *map(like, (feat, kern, prob0, prob1, grad1, grad0, partial)),
+            *map(like, (feat, kern, prob0, prob1, grad1, grad0)),
             room(2 * REACH + 1, near, channels, 128),
             room(2 * REACH + 1, near, 4 * PAD, 128),
             room(near, PAD, 128),
             room(height, 6 * 8, 128),
             pltpu.VMEM((256, (2 * REACH + 1) * 128), jnp.bfloat16),
-            room(classes * height, 128),
-            pltpu.SemaphoreType.DMA((7,)),
+            room(PAD * height, 128),
+            pltpu.SemaphoreType.DMA((6,)),
             pltpu.SemaphoreType.DMA,
         ],
-        compiler_params=params(56),
+        compiler_params=params(24),
         cost_estimate=pl.CostEstimate(flops=200_000_000, bytes_accessed=8_000_000, transcendentals=0),
         name="finish",
-    )(feat, kern, prob0, prob1, grad1, grad0, partial)
+    )(feat, kern, prob0, prob1, grad1, grad0)
 
 
 def on_device(unary, features, compat, grad_output):
@@ -865,18 +868,18 @@
     inner_corner, outer_corner = corners(from_left, from_right, outer_feat)
     outer_corner = lax.ppermute(outer_corner, "rows", above)
     inner_corner = lax.ppermute(inner_corner, "rows", below)
-    main = main_affinities(centre, from_left, from_right, inner_feat, outer_feat)
+    main = main_affinities(centre, inner_feat, outer_feat)
     received = (
         from_left, from_right, inner_feat, inner_rest, outer_feat, outer_rest, inner_corner,
         outer_corner,
     )
 
     devices = n_rows * n_cols
-    *fields, partial, share = iterate(
+    *fields, share = iterate(
         compat, centre, received, main, devices
     )
     shares = lax.all_to_all(share, ("rows", "cols"), 0, 0)
-    unary_grad, feature_grad = finish(*fields, partial, classes)
+    unary_grad, feature_grad = finish(*fields, classes)
     summed = jnp.sum(shares, axis=0) / math.sqrt(n_rows * height * n_cols * width)
     compat_grad = jnp.concatenate(
         [summed[:, 0:PAD], summed[:, 32 : 32 + PAD], summed[:, 64 : 64 + PAD]], axis=0

time: 62.6 us -> 59.6 us (0.952)
  Pallas kernels: 39.3 us -> 37.5 us
  local copies, waits for them, and re-layouts: 2.47 us -> 1.26 us
    pallas_call x1, Pallas kernels: 6.85 us -> 5.15 us  [main_affinities(): pl.pallas_call(main_kernel, out_shape=jax.ShapeDtypeStruct((rows, PAD, 12...]
    unnamed x16 -> x6, local copies, waits for them, and re-layouts: 2.39 us -> 1.19 us
  transfers between devices with their start and end apart: 9 -> 9, of which waited for: 2 -> 2; matrix products, arithmetic and copies ran while one was open for 0% -> 0% of each run, Pallas kernels for 29% -> 27%
where the time goes in v8:
time: 59.6 us; the launch traced here: 59.4 us
  Pallas kernels  37.5 us (63%)
  starting transfers between devices  14.3 us (24%)
  waiting for transfers between devices  4.85 us (8%)
  local copies, waits for them, and re-layouts  1.26 us (2%)
  between operations  0.77 us (1%)
  other arithmetic  0.65 us (1%)
    pallas_call x1, Pallas kernels, iterate(): pl.pallas_call(field_kernel, out_shape=(jax.ShapeDtypeStruct((near, chann...  18.7 us
    pallas_call x1, Pallas kernels, finish(): pl.pallas_call(finish_kernel, out_shape=(jax.ShapeDtypeStruct((classes *...  10.2 us
    pallas_call x1, Pallas kernels, main_affinities(): pl.pallas_call(main_kernel, out_shape=jax.ShapeDtypeStruct((rows, PAD, 12...  5.15 us
    ppermute x1, waiting for transfers between devices, on_device(): from_right = lax.ppermute(left, 'cols', backward)  4.23 us
    all_to_all x1, starting transfers between devices, on_device(): shares = lax.all_to_all(share, ('rows', 'cols'), 0, 0)  4.13 us
    ppermute x1, starting transfers between devices, on_device(): from_left = lax.ppermute(right, 'cols', forward)  3.47 us
    ppermute x1, starting transfers between devices, on_device(): outer_feat = lax.ppermute(outer_feat, 'rows', above)  3.33 us
    pallas_call x1, Pallas kernels, pack(): pl.pallas_call(pack_kernel, out_shape=(shape(height, depth, 128), shape(h...  3.07 us
  transfers between devices with their start and end apart: 9, of which 2 were waited for; matrix products, arithmetic and copies ran while one was open for 0% of the time, Pallas kernels for 27%

profile of v8, /device:TPU:0, one launch (start us, length us, event | category | flops | bytes accessed | tf_op | source)
XLA Modules:
  0.0 59.4 jit_solution(13353499102841356831)
XLA Ops:
  0.6 3.1 %pack.1 = (f32[16,112,128]{2,1,0:T(8,128)}, f32[2,112,128]{2,1,0:T(8,128)}, f32[2,112,128]{2,1,0:T(8,128)}, bf16[12,64,128]{2,1,0:T(8,128)(2,1)}, f32[18,24,128]...) custom-call(bf16[64,16,128]{2,1,0:T(8,128)(2,1)} %feat.1, f32[336,128]{1,0:T(8,128)} %bitcast.4, ...), custom_call_target="tpu_custom_call" | custom-call | tf_op jit(solution)/shard_map/pack/pallas_call | solution.py:222
  3.7 3.3 %collective-permute-start.4 = (bf16[12,64,128]{2,1,0:T(8,128)(2,1)}, bf16[12,64,128]{2,1,0:T(8,128)(2,1)S(1)}, u32[]{:S(2)}, u32[]{:S(2)}) collective-permute-start(bf16[12,64,128]{2,1,0:T(8,128)(2,1)} %get-tuple-element.26), channel_id=1, source_target_pairs={{4,8},{8,4},{12,16},{16,12},{20,24},{24,20},{28,0},{0,28},{5,9},{9... | collective-permute-start | bytes 589832 | tf_op jit(solution)/shard_map/ppermute | solution.py:864
  7.0 3.5 %collective-permute-start = (f32[2,112,128]{2,1,0:T(8,128)}, f32[2,112,128]{2,1,0:T(8,128)S(1)}, u32[]{:S(2)}, u32[]{:S(2)}) collective-permute-start(f32[2,112,128]{2,1,0:T(8,128)} %get-tuple-element.22), channel_id=1, source_target_pairs={{0,1},{1,2},{2,3},{4,5},{5,6},{6,7},{8,9},{9,10},{10,11},{12,13},{... | collective-permute-start | bytes 344072 | tf_op jit(solution)/shard_map/ppermute | solution.py:866
  10.5 1.3 %collective-permute-start.1 = (f32[2,112,128]{2,1,0:T(8,128)}, f32[2,112,128]{2,1,0:T(8,128)S(1)}, u32[]{:S(2)}, u32[]{:S(2)}) collective-permute-start(f32[2,112,128]{2,1,0:T(8,128)} %get-tuple-element.23), channel_id=1, source_target_pairs={{1,0},{2,1},{3,2},{5,4},{6,5},{7,6},{9,8},{10,9},{11,10},{13,12},{... | collective-permute-start | bytes 344072 | tf_op jit(solution)/shard_map/ppermute | solution.py:867
  11.8 0.1 collective-permute-start.3
  11.9 0.7 %collective-permute-start.5 = (f32[18,24,128]{2,1,0:T(8,128)}, f32[18,24,128]{2,1,0:T(8,128)S(1)}, u32[]{:S(2)}, u32[]{:S(2)}) collective-permute-start(f32[18,24,128]{2,1,0:T(8,128)} %get-tuple-element.27), channel_id=1, source_target_pairs={{4,8},{8,4},{12,16},{16,12},{20,24},{24,20},{28,0},{0,28},{5,9},{9... | collective-permute-start | bytes 663560 | tf_op jit(solution)/shard_map/ppermute | solution.py:865
  12.6 0.6 %collective-permute-done.left_in.from_left_in = f32[2,112,128]{2,1,0:T(8,128)S(1)} collective-permute-done((f32[2,112,128]{2,1,0:T(8,128)}, f32[2,112,128]{2,1,0:T(8,128)S(1)}, u32[]{:S(2)}, u32[]{:S(2)}) %collective-permute-start) | collective-permute-done | bytes 114720 | tf_op jit(solution)/shard_map/ppermute | solution.py:866
  13.2 0.0 collective-permute-start.2
  13.2 4.2 %collective-permute-done.1.right_in.from_right_in = f32[2,112,128]{2,1,0:T(8,128)S(1)} collective-permute-done((f32[2,112,128]{2,1,0:T(8,128)}, f32[2,112,128]{2,1,0:T(8,128)S(1)}, u32[]{:S(2)}, u32[]{:S(2)}) %collective-permute-start.1) | collective-permute-done | bytes 114720 | tf_op jit(solution)/shard_map/ppermute | solution.py:867
  17.4 0.0 collective-permute-done.4._.outer_in.outer_feat_in
  17.4 0.4 corners.1
  17.8 0.1 collective-permute-start.6
  17.9 1.2 %collective-permute-start.7 = (f32[312,128]{1,0:T(8,128)S(1)}, f32[312,128]{1,0:T(8,128)S(1)}, u32[]{:S(2)}, u32[]{:S(2)}) collective-permute-start(f32[312,128]{1,0:T(8,128)S(1)} %get-tuple-element.29), channel_id=1, source_target_pairs={{4,8},{8,4},{12,16},{16,12},{20,24},{24,20},{28,0},{0,28},{5,9},{9... | collective-permute-start | bytes 479240 | tf_op jit(solution)/shard_map/ppermute | solution.py:869
  19.2 0.0 collective-permute-done.2.inner_in.inner_feat_in
  19.2 0.0 copy-start
  19.2 1.2 %copy-done = f32[16,112,128]{2,1,0:T(8,128)S(1)} copy-done((f32[16,112,128]{2,1,0:T(8,128)S(1)}, f32[16,112,128]{2,1,0:T(8,128)}, u32[]{:S(2)}) %copy-start) | copy-done | bytes 917528
  20.3 0.0 copy-start.1
  20.3 0.0 copy-start.2
  20.3 5.2 %main_affinities.1.main_in = f32[40,24,128]{2,1,0:T(8,128)S(1)} custom-call(f32[16,112,128]{2,1,0:T(8,128)S(1)} %copy-done, bf16[12,64,128]{2,1,0:T(8,128)(2,1)S(1)} %collective-permute-done.2.inner_in.inner_feat_in, bf16[12,64,128]{2,1,0:T(8,128)(2,1)S(1)} %collective-permute-done.4._.outer_in.outer_feat_in), custom_call_target="tpu_custom_call" | custom-call | flops 200000000 | bytes 8000000 | tf_op jit(solution)/shard_map/main_affinities/pallas_call | solution.py:364
  25.5 0.0 collective-permute-done.3.inner_rest_in
  25.5 0.0 collective-permute-done.5.outer_rest_in
  25.5 0.0 collective-permute-done.6.inner_corner_in
  25.5 0.0 collective-permute-done.7.outer_corner_in
  25.5 0.0 copy-done.1
  25.6 0.0 copy-done.2
  25.6 18.7 %iterate.1 = (bf16[22,64,256]{2,1,0:T(8,128)(2,1)S(1)}, f32[22,24,256]{2,1,0:T(8,128)S(1)}, f32[22,24,256]{2,1,0:T(8,128)S(1)}, f32[22,24,256]{2,1,0:T(8,128)S(1...) custom-call(f32[21,21]{1,0:T(8,128)S(1)} %copy-done.2, ...), custom_call_target="tpu_custom_call" | custom-call | tf_op jit(solution)/shard_map/iterate/pallas_call | solution.py:650
  44.2 4.1 %all-to-all-start = ((f32[32,8,128]{2,1,0:T(8,128)}), f32[32,8,128]{2,1,0:T(8,128)S(1)}, u32[]{:S(2)}, u32[]{:S(2)}) async-start(f32[32,8,128]{2,1,0:T(8,128)} %get-tuple-element.38), calls=%async_computation | async-start | bytes 262144 | tf_op jit(solution)/shard_map/all_to_all | solution.py:881
  48.4 10.2 %finish.1 = (f32[336,128]{1,0:T(8,128)}, f32[1024,128]{1,0:T(8,128)}) custom-call(bf16[22,64,256]{2,1,0:T(8,128)(2,1)S(1)} %get-tuple-element.30.feat_in, f32[22,24,256]{2,1,0:T(8,128)S(1)} %get-tuple-element.31.kern_in, f32[22,24,256]{2,1,0:T(8,128)S(1)} %get-tuple-element.32.prob0_in, f32[22,24,256]{2,1,0:T(8,128)S(1)} %get-tuple-element.33.prob1_in, ...), custom_call_target="tpu_custom_call" | custom-call | flops 200000000 | bytes 8000000 | tf_op jit(solution)/shard_map/finish/pallas_call | solution.py:822
  58.6 0.0 all-to-all-done
  58.7 0.1 fusion
  58.8 0.6 %pad_maximum_fusion = f32[21,21]{1,0:T(8,128)} fusion(f32[8,24]{1,0:T(8,128)S(1)} %get-tuple-element.40, f32[8,24]{1,0:T(8,128)S(1)} %get-tuple-element.41, f32[8,24]{1,0:T(8,128)S(1)} %get-tuple-element.39), kind=kLoop, calls=%fused_computation | loop fusion | flops 882 | bytes 4068 | tf_op jit(solution)/shard_map/concatenate | solution.py:884
  (2 shorter events, 0.0 us)
Async XLA Ops:
  3.7 13.7 %collective-permute-start.4 = (bf16[12,64,128]{2,1,0:T(8,128)(2,1)}, bf16[12,64,128]{2,1,0:T(8,128)(2,1)S(1)}, u32[]{:S(2)}, u32[]{:S(2)}) collective-permute-start(bf16[12,64,128]{2,1,0:T(8,128)(2,1)} %get-tuple-element.26), channel_id=1, source_target_pairs={{4,8},{8,4},{12,16},{16,12},{20,24},{24,20},{28,0},{0,28},{5,9},{9... | collective-permute-start | bytes 589832 | tf_op jit(solution)/shard_map/ppermute | solution.py:864
  7.0 6.1 %collective-permute-start = (f32[2,112,128]{2,1,0:T(8,128)}, f32[2,112,128]{2,1,0:T(8,128)S(1)}, u32[]{:S(2)}, u32[]{:S(2)}) collective-permute-start(f32[2,112,128]{2,1,0:T(8,128)} %get-tuple-element.22), channel_id=1, source_target_pairs={{0,1},{1,2},{2,3},{4,5},{5,6},{6,7},{8,9},{9,10},{10,11},{12,13},{... | collective-permute-start | bytes 344072 | tf_op jit(solution)/shard_map/ppermute | solution.py:866
  10.5 6.9 %collective-permute-start.1 = (f32[2,112,128]{2,1,0:T(8,128)}, f32[2,112,128]{2,1,0:T(8,128)S(1)}, u32[]{:S(2)}, u32[]{:S(2)}) collective-permute-start(f32[2,112,128]{2,1,0:T(8,128)} %get-tuple-element.23), channel_id=1, source_target_pairs={{1,0},{2,1},{3,2},{5,4},{6,5},{7,6},{9,8},{10,9},{11,10},{13,12},{... | collective-permute-start | bytes 344072 | tf_op jit(solution)/shard_map/ppermute | solution.py:867
  11.8 13.7 %collective-permute-start.3 = (f32[18,24,128]{2,1,0:T(8,128)}, f32[18,24,128]{2,1,0:T(8,128)S(1)}, u32[]{:S(2)}, u32[]{:S(2)}) collective-permute-start(f32[18,24,128]{2,1,0:T(8,128)} %get-tuple-element.25), channel_id=1, source_target_pairs={{0,4},{4,0},{8,12},{12,8},{16,20},{20,16},{24,28},{28,24},{1,5},{5... | collective-permute-start | bytes 663560 | tf_op jit(solution)/shard_map/ppermute | solution.py:863
  11.9 13.6 %collective-permute-start.5 = (f32[18,24,128]{2,1,0:T(8,128)}, f32[18,24,128]{2,1,0:T(8,128)S(1)}, u32[]{:S(2)}, u32[]{:S(2)}) collective-permute-start(f32[18,24,128]{2,1,0:T(8,128)} %get-tuple-element.27), channel_id=1, source_target_pairs={{4,8},{8,4},{12,16},{16,12},{20,24},{24,20},{28,0},{0,28},{5,9},{9... | collective-permute-start | bytes 663560 | tf_op jit(solution)/shard_map/ppermute | solution.py:865
  13.2 6.0 %collective-permute-start.2 = (bf16[12,64,128]{2,1,0:T(8,128)(2,1)}, bf16[12,64,128]{2,1,0:T(8,128)(2,1)S(1)}, u32[]{:S(2)}, u32[]{:S(2)}) collective-permute-start(bf16[12,64,128]{2,1,0:T(8,128)(2,1)} %get-tuple-element.24), channel_id=1, source_target_pairs={{0,4},{4,0},{8,12},{12,8},{16,20},{20,16},{24,28},{28,24},{1,5},{5... | collective-permute-start | bytes 589832 | tf_op jit(solution)/shard_map/ppermute | solution.py:862
  17.8 7.7 %collective-permute-start.6 = (f32[312,128]{1,0:T(8,128)S(1)}, f32[312,128]{1,0:T(8,128)S(1)}, u32[]{:S(2)}, u32[]{:S(2)}) collective-permute-start(f32[312,128]{1,0:T(8,128)S(1)} %get-tuple-element.28), channel_id=1, source_target_pairs={{0,4},{4,0},{8,12},{12,8},{16,20},{20,16},{24,28},{28,24},{1,5},{5... | collective-permute-start | bytes 479240 | tf_op jit(solution)/shard_map/ppermute | solution.py:870
  17.9 7.6 %collective-permute-start.7 = (f32[312,128]{1,0:T(8,128)S(1)}, f32[312,128]{1,0:T(8,128)S(1)}, u32[]{:S(2)}, u32[]{:S(2)}) collective-permute-start(f32[312,128]{1,0:T(8,128)S(1)} %get-tuple-element.29), channel_id=1, source_target_pairs={{4,8},{8,4},{12,16},{16,12},{20,24},{24,20},{28,0},{0,28},{5,9},{9... | collective-permute-start | bytes 479240 | tf_op jit(solution)/shard_map/ppermute | solution.py:869
  19.2 1.2 %copy-start = (f32[16,112,128]{2,1,0:T(8,128)S(1)}, f32[16,112,128]{2,1,0:T(8,128)}, u32[]{:S(2)}) copy-start(f32[16,112,128]{2,1,0:T(8,128)} %get-tuple-element.21.centre_in) | copy-start | bytes 2752516
  20.3 5.2 %copy-start.1 = (f32[16,112,128]{2,1,0:T(8,128)S(1)}, f32[16,112,128]{2,1,0:T(8,128)}, u32[]{:S(2)}) copy-start(f32[16,112,128]{2,1,0:T(8,128)} %get-tuple-element.21.centre_in) | copy-start | bytes 2752516
  20.3 5.2 %copy-start.2 = (f32[21,21]{1,0:T(8,128)S(1)}, f32[21,21]{1,0:T(8,128)}, u32[]{:S(2)}) copy-start(f32[21,21]{1,0:T(8,128)} %square_in.1) | copy-start | bytes 5296
  44.2 14.4 %all-to-all-start = ((f32[32,8,128]{2,1,0:T(8,128)}), f32[32,8,128]{2,1,0:T(8,128)S(1)}, u32[]{:S(2)}, u32[]{:S(2)}) async-start(f32[32,8,128]{2,1,0:T(8,128)} %get-tuple-element.38), calls=%async_computation | async-start | bytes 262144 | tf_op jit(solution)/shard_map/all_to_all | solution.py:881

commit v9 on v8

--- a/solution.py
+++ b/solution.py
@@ -320,10 +320,8 @@
 
 
 def main_kernel(
-    centre_in, inner_in, outer_in, kern_out,
-    centre, inner, outer, feat, short, turned, size, size_turned, turner, sems,
+    centre, inner, outer, kern_out, feat, short, turned, size, size_turned, turner,
 ):
-    coming = fetch([(inner_in, inner), (outer_in, outer), (centre_in, centre)], sems)
     height, channels = centre.shape[0], feat.shape[1]
     tall = feat.shape[0]
     turner[...] = turns(range(1, REACH + 1), 128)[0:128]
@@ -331,7 +329,6 @@
         feat[pl.ds(at, REACH)] = jnp.zeros((REACH, channels, 128), jnp.float32)
         short[pl.ds(at, REACH)] = jnp.zeros((REACH, channels, 128), jnp.bfloat16)
     even = position(height)[0]
-    wait(coming)
     above = jnp.where(even, REACH + HALO + height, REACH)
     for source, base in ((inner, above), (outer, tall - HALO - above)):
         for i in range(HALO):
@@ -364,17 +361,15 @@
     return pl.pallas_call(
         main_kernel,
         out_shape=jax.ShapeDtypeStruct((rows, PAD, 128), jnp.float32),
-        in_specs=[ANY] * 3,
+        in_specs=[VMEM] * 3,
         out_specs=VMEM,
         scratch_shapes=[
-            *map(like, inputs),
             room(tall, channels, 128),
             room(tall, channels, 128, dtype=jnp.bfloat16),
             room(REACH, tall, channels, 128),
             room(tall, 8, 128),
             room(REACH, tall, 8, 128),
             room(128, REACH * 128, dtype=jnp.bfloat16),
-            pltpu.SemaphoreType.DMA((3,)),
         ],
         compiler_params=params(16),
         cost_estimate=pl.CostEstimate(
@@ -429,24 +424,13 @@
 
 
 def field_kernel(
-    square_in, centre_in, from_left_in, from_right_in, inner_feat_in, inner_rest_in,
-    outer_feat_in, outer_rest_in, inner_corner_in, outer_corner_in, main_in,
+    square_in, centre, from_left, from_right, inner_feat, inner_rest, outer_feat, outer_rest,
+    inner_corner, outer_corner, main,
     feat_out, kern_out, prob0_out, prob1_out, grad1_out, grad0_out, share,
-    centre, from_left, from_right, inner_feat, inner_rest, outer_feat, outer_rest, inner_corner,
-    outer_corner, main, short, side_feat, side_turned, side_size, side_size_turned, side_kern,
-    kern, unary, grad, prob0,
-    prob1, grad1, grad0, turned, message0, message1, logit1, logit0, side_turner, square, compat, compat_t,
-    in_sems, out_sems,
+    short, side_feat, side_turned, side_size, side_size_turned, side_kern,
+    kern, unary, grad, prob0, prob1, grad1, grad0, turned, message0, message1, logit1, logit0,
+    side_turner, square, compat, compat_t, out_sems,
 ):
-    coming = fetch(
-        [
-            (centre_in, centre), (from_left_in, from_left), (from_right_in, from_right),
-            (inner_feat_in, inner_feat), (inner_rest_in, inner_rest),
-            (outer_feat_in, outer_feat), (outer_rest_in, outer_rest),
-            (inner_corner_in, inner_corner), (outer_corner_in, outer_corner), (main_in, main),
-        ],
-        in_sems,
-    )
     height = centre.shape[0]
     going = []
 
@@ -477,12 +461,10 @@
             if value.shape[0] > channels + PAD:
                 grad[row, :, cols] = value[channels + PAD :]
 
-    wait(coming[:3])
     for y in range(height):
         at = (y % 8) * STRIP
         put(HALO + y, centre[y], from_left[y // 8], at, from_right[y // 8], at)
 
-    wait(coming[3:])
     depth = channels + 2 * PAD
     slim = channels + PAD
     near = HALO // 2
@@ -658,12 +640,9 @@
             shape(near, PAD, 256),
             shape(devices, 8, 128),
         ),
-        in_specs=[VMEM] + [ANY] * (2 + len(received)),
+        in_specs=[VMEM] * (3 + len(received)),
         out_specs=(ANY,) * 6 + (VMEM,),
         scratch_shapes=[
-            like(centre),
-            *map(like, received),
-            like(main),
             pltpu.VMEM((tall, channels, 256), jnp.bfloat16),
             room(slots + 2 * REACH, channels, 128),
             room(REACH, slots + 2 * REACH, channels, 128),
@@ -677,7 +656,6 @@
             room(128, 128),
             pltpu.VMEM((DEEP, 6 * PAD), jnp.bfloat16),
             pltpu.VMEM((DEEP, 6 * PAD), jnp.bfloat16),
-            pltpu.SemaphoreType.DMA((2 + len(received),)),
             pltpu.SemaphoreType.DMA((6,)),
         ],
         compiler_params=params(28),
@@ -686,17 +664,9 @@
 
 
 def finish_kernel(
-    feat_in, kern_in, prob0_in, prob1_in, grad1_in, grad0_in, unary_out, feat_out,
-    feat, kern, prob0, prob1, grad1, grad0, feat_turned, all_turned, kern_back, weights,
-    turner, unary_rows, in_sems, out_sem,
+    feat, kern, prob0, prob1, grad1, grad0, unary_out, feat_out, feat_turned, all_turned, kern_back, weights,
+    turner, unary_rows, out_sem,
 ):
-    coming = fetch(
-        [
-            (feat_in, feat), (kern_in, kern), (prob0_in, prob0), (prob1_in, prob1),
-            (grad1_in, grad1), (grad0_in, grad0),
-        ],
-        in_sems,
-    )
     near = feat.shape[0]
     height = near - 2 * REACH
     channels = feat.shape[1]
@@ -712,14 +682,11 @@
         mixed = jnp.where((column < b) if b > 0 else (column >= 128 + b), edge, main)
         return pltpu.roll(mixed, (-b) % 128, axis=1)
 
-    wait(coming[:1])
     full = jnp.dot(
         feat[...].reshape(near * channels, 256), turner[...], preferred_element_type=jnp.float32
     )
     for place in range(len(steps)):
         feat_turned[place] = full[:, 128 * place : 128 * place + 128].reshape(near, channels, 128)
-
-    wait(coming[1:])
 
     def prepare(row):
         for place, field in enumerate((prob0, prob1, grad1, grad0)):
@@ -825,17 +792,15 @@
             jax.ShapeDtypeStruct((classes * height, 128), jnp.float32),
             jax.ShapeDtypeStruct((channels * height, 128), jnp.float32),
         ),
-        in_specs=[ANY] * 6,
+        in_specs=[VMEM] * 6,
         out_specs=(ANY, VMEM),
         scratch_shapes=[
-            *map(like, (feat, kern, prob0, prob1, grad1, grad0)),
             room(2 * REACH + 1, near, channels, 128),
             room(2 * REACH + 1, near, 4 * PAD, 128),
             room(near, PAD, 128),
             room(height, 6 * 8, 128),
             pltpu.VMEM((256, (2 * REACH + 1) * 128), jnp.bfloat16),
             room(PAD * height, 128),
-            pltpu.SemaphoreType.DMA((6,)),
             pltpu.SemaphoreType.DMA,
         ],
         compiler_params=params(24),

time: 59.6 us -> 55.2 us (0.926)
  Pallas kernels: 37.5 us -> 33.1 us
    pallas_call x1, Pallas kernels: 18.7 us -> 16.5 us  [iterate(): pl.pallas_call(field_kernel, out_shape=(jax.ShapeDtypeStruct((near, chann...]
    pallas_call x1, Pallas kernels: 10.2 us -> 8.73 us  [finish(): pl.pallas_call(finish_kernel, out_shape=(jax.ShapeDtypeStruct((classes *...]
    pallas_call x1, Pallas kernels: 5.15 us -> 4.41 us  [main_affinities(): pl.pallas_call(main_kernel, out_shape=jax.ShapeDtypeStruct((rows, PAD, 12...]
  transfers between devices with their start and end apart: 9 -> 9, of which waited for: 2 -> 3; matrix products, arithmetic and copies ran while one was open for 0% -> 0% of each run, Pallas kernels for 27% -> 25%
where the time goes in v9:
time: 55.2 us; the launch traced here: 54.9 us
  Pallas kernels  33.1 us (60%)
  starting transfers between devices  14.1 us (26%)
  waiting for transfers between devices  5.07 us (9%)
  local copies, waits for them, and re-layouts  1.26 us (2%)
  between operations  0.74 us (1%)
  other arithmetic  0.65 us (1%)
    pallas_call x1, Pallas kernels, iterate(): pl.pallas_call(field_kernel, out_shape=(jax.ShapeDtypeStruct((near, chann...  16.5 us
    pallas_call x1, Pallas kernels, finish(): pl.pallas_call(finish_kernel, out_shape=(jax.ShapeDtypeStruct((classes *...  8.73 us
    pallas_call x1, Pallas kernels, main_affinities(): pl.pallas_call(main_kernel, out_shape=jax.ShapeDtypeStruct((rows, PAD, 12...  4.41 us
    ppermute x1, waiting for transfers between devices, on_device(): from_right = lax.ppermute(left, 'cols', backward)  4.23 us
    all_to_all x1, starting transfers between devices, on_device(): shares = lax.all_to_all(share, ('rows', 'cols'), 0, 0)  3.91 us
    ppermute x1, starting transfers between devices, on_device(): from_left = lax.ppermute(right, 'cols', forward)  3.47 us
    ppermute x1, starting transfers between devices, on_device(): outer_feat = lax.ppermute(outer_feat, 'rows', above)  3.33 us
    pallas_call x1, Pallas kernels, pack(): pl.pallas_call(pack_kernel, out_shape=(shape(height, depth, 128), shape(h...  3.07 us
  transfers between devices with their start and end apart: 9, of which 3 were waited for; matrix products, arithmetic and copies ran while one was open for 0% of the time, Pallas kernels for 25%

profile of v9, /device:TPU:0, one launch (start us, length us, event | category | flops | bytes accessed | tf_op | source)
XLA Modules:
  0.0 54.9 jit_solution(18352872373087489960)
XLA Ops:
  0.6 3.1 %pack.1 = (f32[16,112,128]{2,1,0:T(8,128)}, f32[2,112,128]{2,1,0:T(8,128)}, f32[2,112,128]{2,1,0:T(8,128)}, bf16[12,64,128]{2,1,0:T(8,128)(2,1)}, f32[18,24,128]...) custom-call(bf16[64,16,128]{2,1,0:T(8,128)(2,1)} %feat.1, f32[336,128]{1,0:T(8,128)} %bitcast.4, ...), custom_call_target="tpu_custom_call" | custom-call | tf_op jit(solution)/shard_map/pack/pallas_call | solution.py:222
  3.7 3.3 %collective-permute-start.4 = (bf16[12,64,128]{2,1,0:T(8,128)(2,1)}, bf16[12,64,128]{2,1,0:T(8,128)(2,1)S(1)}, u32[]{:S(2)}, u32[]{:S(2)}) collective-permute-start(bf16[12,64,128]{2,1,0:T(8,128)(2,1)} %get-tuple-element.26), channel_id=1, source_target_pairs={{4,8},{8,4},{12,16},{16,12},{20,24},{24,20},{28,0},{0,28},{5,9},{9... | collective-permute-start | bytes 589832 | tf_op jit(solution)/shard_map/ppermute | solution.py:829
  7.0 3.5 %collective-permute-start = (f32[2,112,128]{2,1,0:T(8,128)}, f32[2,112,128]{2,1,0:T(8,128)S(1)}, u32[]{:S(2)}, u32[]{:S(2)}) collective-permute-start(f32[2,112,128]{2,1,0:T(8,128)} %get-tuple-element.22), channel_id=1, source_target_pairs={{0,1},{1,2},{2,3},{4,5},{5,6},{6,7},{8,9},{9,10},{10,11},{12,13},{... | collective-permute-start | bytes 344072 | tf_op jit(solution)/shard_map/ppermute | solution.py:831
  10.5 1.3 %collective-permute-start.1 = (f32[2,112,128]{2,1,0:T(8,128)}, f32[2,112,128]{2,1,0:T(8,128)S(1)}, u32[]{:S(2)}, u32[]{:S(2)}) collective-permute-start(f32[2,112,128]{2,1,0:T(8,128)} %get-tuple-element.23), channel_id=1, source_target_pairs={{1,0},{2,1},{3,2},{5,4},{6,5},{7,6},{9,8},{10,9},{11,10},{13,12},{... | collective-permute-start | bytes 344072 | tf_op jit(solution)/shard_map/ppermute | solution.py:832
  11.8 0.1 collective-permute-start.3
  11.9 0.7 %collective-permute-start.5 = (f32[18,24,128]{2,1,0:T(8,128)}, f32[18,24,128]{2,1,0:T(8,128)S(1)}, u32[]{:S(2)}, u32[]{:S(2)}) collective-permute-start(f32[18,24,128]{2,1,0:T(8,128)} %get-tuple-element.27), channel_id=1, source_target_pairs={{4,8},{8,4},{12,16},{16,12},{20,24},{24,20},{28,0},{0,28},{5,9},{9... | collective-permute-start | bytes 663560 | tf_op jit(solution)/shard_map/ppermute | solution.py:830
  12.6 0.6 %collective-permute-done.left_in.from_left = f32[2,112,128]{2,1,0:T(8,128)S(1)} collective-permute-done((f32[2,112,128]{2,1,0:T(8,128)}, f32[2,112,128]{2,1,0:T(8,128)S(1)}, u32[]{:S(2)}, u32[]{:S(2)}) %collective-permute-start) | collective-permute-done | bytes 114720 | tf_op jit(solution)/shard_map/ppermute | solution.py:831
  13.2 0.0 collective-permute-start.2
  13.2 4.2 %collective-permute-done.1.right_in.from_right = f32[2,112,128]{2,1,0:T(8,128)S(1)} collective-permute-done((f32[2,112,128]{2,1,0:T(8,128)}, f32[2,112,128]{2,1,0:T(8,128)S(1)}, u32[]{:S(2)}, u32[]{:S(2)}) %collective-permute-start.1) | collective-permute-done | bytes 114720 | tf_op jit(solution)/shard_map/ppermute | solution.py:832
  17.4 0.0 collective-permute-done.4._.outer.outer_feat
  17.4 0.4 corners.1
  17.8 0.1 collective-permute-start.6
  17.9 1.2 %collective-permute-start.7 = (f32[312,128]{1,0:T(8,128)S(1)}, f32[312,128]{1,0:T(8,128)S(1)}, u32[]{:S(2)}, u32[]{:S(2)}) collective-permute-start(f32[312,128]{1,0:T(8,128)S(1)} %get-tuple-element.29), channel_id=1, source_target_pairs={{4,8},{8,4},{12,16},{16,12},{20,24},{24,20},{28,0},{0,28},{5,9},{9... | collective-permute-start | bytes 479240 | tf_op jit(solution)/shard_map/ppermute | solution.py:834
  19.2 0.0 collective-permute-done.2.inner.inner_feat
  19.2 0.0 copy-start
  19.2 1.2 %copy-done = f32[16,112,128]{2,1,0:T(8,128)S(1)} copy-done((f32[16,112,128]{2,1,0:T(8,128)S(1)}, f32[16,112,128]{2,1,0:T(8,128)}, u32[]{:S(2)}) %copy-start) | copy-done | bytes 917528
  20.3 0.0 copy-start.1
  20.3 0.0 copy-start.2
  20.3 4.4 %main_affinities.1.main = f32[40,24,128]{2,1,0:T(8,128)S(1)} custom-call(f32[16,112,128]{2,1,0:T(8,128)S(1)} %copy-done, bf16[12,64,128]{2,1,0:T(8,128)(2,1)S(1)} %collective-permute-done.2.inner.inner_feat, bf16[12,64,128]{2,1,0:T(8,128)(2,1)S(1)} %collective-permute-done.4._.outer.outer_feat), custom_call_target="tpu_custom_call" | custom-call | flops 200000000 | bytes 8000000 | tf_op jit(solution)/shard_map/main_affinities/pallas_call | solution.py:361
  24.8 0.0 collective-permute-done.3.inner_rest
  24.8 0.0 collective-permute-done.5.outer_rest
  24.8 0.0 collective-permute-done.6.inner_corner
  24.8 0.2 collective-permute-done.7.outer_corner
  25.0 0.0 copy-done.1
  25.0 0.0 copy-done.2
  25.0 16.5 %iterate.1 = (bf16[22,64,256]{2,1,0:T(8,128)(2,1)S(1)}, f32[22,24,256]{2,1,0:T(8,128)S(1)}, f32[22,24,256]{2,1,0:T(8,128)S(1)}, f32[22,24,256]{2,1,0:T(8,128)S(1...) custom-call(f32[21,21]{1,0:T(8,128)S(1)} %copy-done.2, ...), custom_call_target="tpu_custom_call" | custom-call | tf_op jit(solution)/shard_map/iterate/pallas_call | solution.py:632
  41.5 3.9 %all-to-all-start = ((f32[32,8,128]{2,1,0:T(8,128)}), f32[32,8,128]{2,1,0:T(8,128)S(1)}, u32[]{:S(2)}, u32[]{:S(2)}) async-start(f32[32,8,128]{2,1,0:T(8,128)} %get-tuple-element.38), calls=%async_computation | async-start | bytes 262144 | tf_op jit(solution)/shard_map/all_to_all | solution.py:846
  45.4 8.7 %finish.1 = (f32[336,128]{1,0:T(8,128)}, f32[1024,128]{1,0:T(8,128)}) custom-call(bf16[22,64,256]{2,1,0:T(8,128)(2,1)S(1)} %get-tuple-element.30.feat, f32[22,24,256]{2,1,0:T(8,128)S(1)} %get-tuple-element.31.kern, f32[22,24,256]{2,1,0:T(8,128)S(1)} %get-tuple-element.32.prob0, f32[22,24,256]{2,1,0:T(8,128)S(1)} %get-tuple-element.33.prob1, ...), custom_call_target="tpu_custom_call" | custom-call | flops 200000000 | bytes 8000000 | tf_op jit(solution)/shard_map/finish/pallas_call | solution.py:789
  54.2 0.0 all-to-all-done
  54.2 0.1 fusion
  54.3 0.6 %pad_maximum_fusion = f32[21,21]{1,0:T(8,128)} fusion(f32[8,24]{1,0:T(8,128)S(1)} %get-tuple-element.40, f32[8,24]{1,0:T(8,128)S(1)} %get-tuple-element.41, f32[8,24]{1,0:T(8,128)S(1)} %get-tuple-element.39), kind=kLoop, calls=%fused_computation | loop fusion | flops 882 | bytes 4068 | tf_op jit(solution)/shard_map/concatenate | solution.py:849
  (2 shorter events, 0.0 us)
Async XLA Ops:
  3.7 13.7 %collective-permute-start.4 = (bf16[12,64,128]{2,1,0:T(8,128)(2,1)}, bf16[12,64,128]{2,1,0:T(8,128)(2,1)S(1)}, u32[]{:S(2)}, u32[]{:S(2)}) collective-permute-start(bf16[12,64,128]{2,1,0:T(8,128)(2,1)} %get-tuple-element.26), channel_id=1, source_target_pairs={{4,8},{8,4},{12,16},{16,12},{20,24},{24,20},{28,0},{0,28},{5,9},{9... | collective-permute-start | bytes 589832 | tf_op jit(solution)/shard_map/ppermute | solution.py:829
  7.0 6.1 %collective-permute-start = (f32[2,112,128]{2,1,0:T(8,128)}, f32[2,112,128]{2,1,0:T(8,128)S(1)}, u32[]{:S(2)}, u32[]{:S(2)}) collective-permute-start(f32[2,112,128]{2,1,0:T(8,128)} %get-tuple-element.22), channel_id=1, source_target_pairs={{0,1},{1,2},{2,3},{4,5},{5,6},{6,7},{8,9},{9,10},{10,11},{12,13},{... | collective-permute-start | bytes 344072 | tf_op jit(solution)/shard_map/ppermute | solution.py:831
  10.5 6.9 %collective-permute-start.1 = (f32[2,112,128]{2,1,0:T(8,128)}, f32[2,112,128]{2,1,0:T(8,128)S(1)}, u32[]{:S(2)}, u32[]{:S(2)}) collective-permute-start(f32[2,112,128]{2,1,0:T(8,128)} %get-tuple-element.23), channel_id=1, source_target_pairs={{1,0},{2,1},{3,2},{5,4},{6,5},{7,6},{9,8},{10,9},{11,10},{13,12},{... | collective-permute-start | bytes 344072 | tf_op jit(solution)/shard_map/ppermute | solution.py:832
  11.8 12.9 %collective-permute-start.3 = (f32[18,24,128]{2,1,0:T(8,128)}, f32[18,24,128]{2,1,0:T(8,128)S(1)}, u32[]{:S(2)}, u32[]{:S(2)}) collective-permute-start(f32[18,24,128]{2,1,0:T(8,128)} %get-tuple-element.25), channel_id=1, source_target_pairs={{0,4},{4,0},{8,12},{12,8},{16,20},{20,16},{24,28},{28,24},{1,5},{5... | collective-permute-start | bytes 663560 | tf_op jit(solution)/shard_map/ppermute | solution.py:828
  11.9 12.9 %collective-permute-start.5 = (f32[18,24,128]{2,1,0:T(8,128)}, f32[18,24,128]{2,1,0:T(8,128)S(1)}, u32[]{:S(2)}, u32[]{:S(2)}) collective-permute-start(f32[18,24,128]{2,1,0:T(8,128)} %get-tuple-element.27), channel_id=1, source_target_pairs={{4,8},{8,4},{12,16},{16,12},{20,24},{24,20},{28,0},{0,28},{5,9},{9... | collective-permute-start | bytes 663560 | tf_op jit(solution)/shard_map/ppermute | solution.py:830
  13.2 6.0 %collective-permute-start.2 = (bf16[12,64,128]{2,1,0:T(8,128)(2,1)}, bf16[12,64,128]{2,1,0:T(8,128)(2,1)S(1)}, u32[]{:S(2)}, u32[]{:S(2)}) collective-permute-start(bf16[12,64,128]{2,1,0:T(8,128)(2,1)} %get-tuple-element.24), channel_id=1, source_target_pairs={{0,4},{4,0},{8,12},{12,8},{16,20},{20,16},{24,28},{28,24},{1,5},{5... | collective-permute-start | bytes 589832 | tf_op jit(solution)/shard_map/ppermute | solution.py:827
  17.8 6.9 %collective-permute-start.6 = (f32[312,128]{1,0:T(8,128)S(1)}, f32[312,128]{1,0:T(8,128)S(1)}, u32[]{:S(2)}, u32[]{:S(2)}) collective-permute-start(f32[312,128]{1,0:T(8,128)S(1)} %get-tuple-element.28), channel_id=1, source_target_pairs={{0,4},{4,0},{8,12},{12,8},{16,20},{20,16},{24,28},{28,24},{1,5},{5... | collective-permute-start | bytes 479240 | tf_op jit(solution)/shard_map/ppermute | solution.py:835
  17.9 7.1 %collective-permute-start.7 = (f32[312,128]{1,0:T(8,128)S(1)}, f32[312,128]{1,0:T(8,128)S(1)}, u32[]{:S(2)}, u32[]{:S(2)}) collective-permute-start(f32[312,128]{1,0:T(8,128)S(1)} %get-tuple-element.29), channel_id=1, source_target_pairs={{4,8},{8,4},{12,16},{16,12},{20,24},{24,20},{28,0},{0,28},{5,9},{9... | collective-permute-start | bytes 479240 | tf_op jit(solution)/shard_map/ppermute | solution.py:834
  19.2 1.2 %copy-start = (f32[16,112,128]{2,1,0:T(8,128)S(1)}, f32[16,112,128]{2,1,0:T(8,128)}, u32[]{:S(2)}) copy-start(f32[16,112,128]{2,1,0:T(8,128)} %get-tuple-element.21.centre) | copy-start | bytes 2752516
  20.3 4.7 %copy-start.1 = (f32[16,112,128]{2,1,0:T(8,128)S(1)}, f32[16,112,128]{2,1,0:T(8,128)}, u32[]{:S(2)}) copy-start(f32[16,112,128]{2,1,0:T(8,128)} %get-tuple-element.21.centre) | copy-start | bytes 2752516
  20.3 4.7 %copy-start.2 = (f32[21,21]{1,0:T(8,128)S(1)}, f32[21,21]{1,0:T(8,128)}, u32[]{:S(2)}) copy-start(f32[21,21]{1,0:T(8,128)} %square_in.1) | copy-start | bytes 5296
  41.5 12.7 %all-to-all-start = ((f32[32,8,128]{2,1,0:T(8,128)}), f32[32,8,128]{2,1,0:T(8,128)S(1)}, u32[]{:S(2)}, u32[]{:S(2)}) async-start(f32[32,8,128]{2,1,0:T(8,128)} %get-tuple-element.38), calls=%async_computation | async-start | bytes 262144 | tf_op jit(solution)/shard_map/all_to_all | solution.py:846

commit v10 on v9

--- a/solution.py
+++ b/solution.py
@@ -248,10 +248,13 @@
     side = lane()
     for out, top in ((inner, jnp.logical_not(even)), (outer, even)):
         whole = jnp.where(top, 0, 1)
-        out[pl.ds(0, depth)] = left[whole]
-        out[pl.ds(depth, depth)] = right[whole]
+        out[pl.ds(0, short)] = left[whole, 0:short]
+        out[pl.ds(short, short)] = right[whole, 0:short]
+        out[pl.ds(3 * short, PAD)] = jnp.where(
+            side % STRIP < STRIP // 2, right[whole, short:], left[whole, short:]
+        )
         mine = (side < 64) == top
-        out[pl.ds(2 * depth, short)] = jnp.where(
+        out[pl.ds(2 * short, short)] = jnp.where(
             mine,
             left[1 - whole, 0:short],
             pltpu.roll(right[1 - whole, 0:short], 64, axis=1),
@@ -260,7 +263,7 @@
 
 def corners(left, right, earlier):
     depth = left.shape[1]
-    out = jax.ShapeDtypeStruct((3 * depth - PAD, 128), jnp.float32)
+    out = jax.ShapeDtypeStruct((3 * depth - 2 * PAD, 128), jnp.float32)
     return pl.pallas_call(
         corner_kernel,
         out_shape=(out, out),
@@ -429,17 +432,14 @@
     feat_out, kern_out, prob0_out, prob1_out, grad1_out, grad0_out, share,
     short, side_feat, side_turned, side_size, side_size_turned, side_kern,
     kern, unary, grad, prob0, prob1, grad1, grad0, turned, message0, message1, logit1, logit0,
-    side_turner, square, compat, compat_t, out_sems,
+    side_turner, square, compat, compat_t,
 ):
     height = centre.shape[0]
-    going = []
-
     def send(source, target, low):
-        copy = pltpu.make_async_copy(
-            source.at[pl.ds(low, target.shape[0])], target, out_sems.at[len(going)]
-        )
-        copy.start()
-        going.append(copy)
+        def body(row):
+            target[row] = source[row + low]
+
+        each_row(0, target.shape[0], target.shape[0], body)
 
     rows = height + 2 * HALO
     channels = short.shape[1]
@@ -465,7 +465,6 @@
         at = (y % 8) * STRIP
         put(HALO + y, centre[y], from_left[y // 8], at, from_right[y // 8], at)
 
-    depth = channels + 2 * PAD
     slim = channels + PAD
     near = HALO // 2
 
@@ -482,10 +481,12 @@
         for i in range(HALO):
             at = (i if top else i - half) * STRIP
             if 0 <= at < 128:
-                left, right = corner[pl.ds(0, depth)], corner[pl.ds(depth, depth)]
+                shared = corner[pl.ds(3 * slim, PAD)]
+                left = jnp.concatenate([corner[pl.ds(0, slim)], shared], axis=0)
+                right = jnp.concatenate([corner[pl.ds(slim, slim)], shared], axis=0)
                 left_at = right_at = at
             else:
-                left = right = corner[pl.ds(2 * depth, slim)]
+                left = right = corner[pl.ds(2 * slim, slim)]
                 left_at = (i - 8) * STRIP if top else 64 + i * STRIP
                 right_at = (left_at + 64) % 128
             own = edge_rows(i, top)
@@ -612,7 +613,6 @@
     each_row(0, height, height, add_logit)
     send(grad1, grad1_out, HALO - REACH)
     send(grad0, grad0_out, HALO - REACH)
-    wait(going)
 
 
 def iterate(compat, centre, received, main, devices):
@@ -641,7 +641,7 @@
             shape(devices, 8, 128),
         ),
         in_specs=[VMEM] * (3 + len(received)),
-        out_specs=(ANY,) * 6 + (VMEM,),
+        out_specs=(VMEM,) * 7,
         scratch_shapes=[
             pltpu.VMEM((tall, channels, 256), jnp.bfloat16),
             room(slots + 2 * REACH, channels, 128),
@@ -656,7 +656,6 @@
             room(128, 128),
             pltpu.VMEM((DEEP, 6 * PAD), jnp.bfloat16),
             pltpu.VMEM((DEEP, 6 * PAD), jnp.bfloat16),
-            pltpu.SemaphoreType.DMA((6,)),
         ],
         compiler_params=params(28),
         name="iterate",

time: 55.2 us -> 54.4 us (0.986)
    pallas_call x1, Pallas kernels: 16.5 us -> 15.9 us  [iterate(): pl.pallas_call(field_kernel, out_shape=(jax.ShapeDtypeStruct((near, chann...]
  transfers between devices with their start and end apart: 9 -> 9, of which waited for: 3 -> 2; matrix products, arithmetic and copies ran while one was open for 0% -> 0% of each run, Pallas kernels for 25% -> 25%
where the time goes in v10:
time: 54.4 us; the launch traced here: 54.2 us
  Pallas kernels  32.6 us (60%)
  starting transfers between devices  14.1 us (26%)
  waiting for transfers between devices  4.85 us (9%)
  local copies, waits for them, and re-layouts  1.26 us (2%)
  between operations  0.76 us (1%)
  other arithmetic  0.65 us (1%)
    pallas_call x1, Pallas kernels, iterate(): pl.pallas_call(field_kernel, out_shape=(jax.ShapeDtypeStruct((near, chann...  15.9 us
    pallas_call x1, Pallas kernels, finish(): pl.pallas_call(finish_kernel, out_shape=(jax.ShapeDtypeStruct((classes *...  8.73 us
    pallas_call x1, Pallas kernels, main_affinities(): pl.pallas_call(main_kernel, out_shape=jax.ShapeDtypeStruct((rows, PAD, 12...  4.41 us
    ppermute x1, waiting for transfers between devices, on_device(): from_right = lax.ppermute(left, 'cols', backward)  4.23 us
    all_to_all x1, starting transfers between devices, on_device(): shares = lax.all_to_all(share, ('rows', 'cols'), 0, 0)  3.94 us
    ppermute x1, starting transfers between devices, on_device(): from_left = lax.ppermute(right, 'cols', forward)  3.47 us
    ppermute x1, starting transfers between devices, on_device(): outer_feat = lax.ppermute(outer_feat, 'rows', above)  3.33 us
    pallas_call x1, Pallas kernels, pack(): pl.pallas_call(pack_kernel, out_shape=(shape(height, depth, 128), shape(h...  3.07 us
  transfers between devices with their start and end apart: 9, of which 2 were waited for; matrix products, arithmetic and copies ran while one was open for 0% of the time, Pallas kernels for 25%

profile of v10, /device:TPU:0, one launch (start us, length us, event | category | flops | bytes accessed | tf_op | source)
XLA Modules:
  0.0 54.2 jit_solution(6283414276534064557)
XLA Ops:
  0.6 3.1 %pack.1 = (f32[16,112,128]{2,1,0:T(8,128)}, f32[2,112,128]{2,1,0:T(8,128)}, f32[2,112,128]{2,1,0:T(8,128)}, bf16[12,64,128]{2,1,0:T(8,128)(2,1)}, f32[18,24,128]...) custom-call(bf16[64,16,128]{2,1,0:T(8,128)(2,1)} %feat.1, f32[336,128]{1,0:T(8,128)} %bitcast.4, ...), custom_call_target="tpu_custom_call" | custom-call | tf_op jit(solution)/shard_map/pack/pallas_call | solution.py:222
  3.7 3.3 %collective-permute-start.4 = (bf16[12,64,128]{2,1,0:T(8,128)(2,1)}, bf16[12,64,128]{2,1,0:T(8,128)(2,1)S(1)}, u32[]{:S(2)}, u32[]{:S(2)}) collective-permute-start(bf16[12,64,128]{2,1,0:T(8,128)(2,1)} %get-tuple-element.26), channel_id=1, source_target_pairs={{4,8},{8,4},{12,16},{16,12},{20,24},{24,20},{28,0},{0,28},{5,9},{9... | collective-permute-start | bytes 589832 | tf_op jit(solution)/shard_map/ppermute | solution.py:828
  7.0 3.5 %collective-permute-start = (f32[2,112,128]{2,1,0:T(8,128)}, f32[2,112,128]{2,1,0:T(8,128)S(1)}, u32[]{:S(2)}, u32[]{:S(2)}) collective-permute-start(f32[2,112,128]{2,1,0:T(8,128)} %get-tuple-element.22), channel_id=1, source_target_pairs={{0,1},{1,2},{2,3},{4,5},{5,6},{6,7},{8,9},{9,10},{10,11},{12,13},{... | collective-permute-start | bytes 344072 | tf_op jit(solution)/shard_map/ppermute | solution.py:830
  10.5 1.3 %collective-permute-start.1 = (f32[2,112,128]{2,1,0:T(8,128)}, f32[2,112,128]{2,1,0:T(8,128)S(1)}, u32[]{:S(2)}, u32[]{:S(2)}) collective-permute-start(f32[2,112,128]{2,1,0:T(8,128)} %get-tuple-element.23), channel_id=1, source_target_pairs={{1,0},{2,1},{3,2},{5,4},{6,5},{7,6},{9,8},{10,9},{11,10},{13,12},{... | collective-permute-start | bytes 344072 | tf_op jit(solution)/shard_map/ppermute | solution.py:831
  11.8 0.1 collective-permute-start.3
  11.9 0.7 %collective-permute-start.5 = (f32[18,24,128]{2,1,0:T(8,128)}, f32[18,24,128]{2,1,0:T(8,128)S(1)}, u32[]{:S(2)}, u32[]{:S(2)}) collective-permute-start(f32[18,24,128]{2,1,0:T(8,128)} %get-tuple-element.27), channel_id=1, source_target_pairs={{4,8},{8,4},{12,16},{16,12},{20,24},{24,20},{28,0},{0,28},{5,9},{9... | collective-permute-start | bytes 663560 | tf_op jit(solution)/shard_map/ppermute | solution.py:829
  12.6 0.6 %collective-permute-done.left_in.from_left = f32[2,112,128]{2,1,0:T(8,128)S(1)} collective-permute-done((f32[2,112,128]{2,1,0:T(8,128)}, f32[2,112,128]{2,1,0:T(8,128)S(1)}, u32[]{:S(2)}, u32[]{:S(2)}) %collective-permute-start) | collective-permute-done | bytes 114720 | tf_op jit(solution)/shard_map/ppermute | solution.py:830
  13.2 0.0 collective-permute-start.2
  13.2 4.2 %collective-permute-done.1.right_in.from_right = f32[2,112,128]{2,1,0:T(8,128)S(1)} collective-permute-done((f32[2,112,128]{2,1,0:T(8,128)}, f32[2,112,128]{2,1,0:T(8,128)S(1)}, u32[]{:S(2)}, u32[]{:S(2)}) %collective-permute-start.1) | collective-permute-done | bytes 114720 | tf_op jit(solution)/shard_map/ppermute | solution.py:831
  17.4 0.0 collective-permute-done.4._.outer.outer_feat
  17.4 0.4 corners.1
  17.8 0.1 collective-permute-start.6
  17.9 1.2 %collective-permute-start.7 = (f32[288,128]{1,0:T(8,128)S(1)}, f32[288,128]{1,0:T(8,128)S(1)}, u32[]{:S(2)}, u32[]{:S(2)}) collective-permute-start(f32[288,128]{1,0:T(8,128)S(1)} %get-tuple-element.29), channel_id=1, source_target_pairs={{4,8},{8,4},{12,16},{16,12},{20,24},{24,20},{28,0},{0,28},{5,9},{9... | collective-permute-start | bytes 442376 | tf_op jit(solution)/shard_map/ppermute | solution.py:833
  19.2 0.0 collective-permute-done.2.inner.inner_feat
  19.2 0.0 copy-start
  19.2 1.2 %copy-done = f32[16,112,128]{2,1,0:T(8,128)S(1)} copy-done((f32[16,112,128]{2,1,0:T(8,128)S(1)}, f32[16,112,128]{2,1,0:T(8,128)}, u32[]{:S(2)}) %copy-start) | copy-done | bytes 917528
  20.3 0.0 copy-start.1
  20.3 0.0 copy-start.2
  20.3 4.4 %main_affinities.1.main = f32[40,24,128]{2,1,0:T(8,128)S(1)} custom-call(f32[16,112,128]{2,1,0:T(8,128)S(1)} %copy-done, bf16[12,64,128]{2,1,0:T(8,128)(2,1)S(1)} %collective-permute-done.2.inner.inner_feat, bf16[12,64,128]{2,1,0:T(8,128)(2,1)S(1)} %collective-permute-done.4._.outer.outer_feat), custom_call_target="tpu_custom_call" | custom-call | flops 200000000 | bytes 8000000 | tf_op jit(solution)/shard_map/main_affinities/pallas_call | solution.py:364
  24.8 0.0 collective-permute-done.3.inner_rest
  24.8 0.0 collective-permute-done.5.outer_rest
  24.8 0.0 collective-permute-done.6.inner_corner
  24.8 0.0 collective-permute-done.7.outer_corner
  24.8 0.0 copy-done.1
  24.8 0.0 copy-done.2
  24.8 15.9 %iterate.1 = (bf16[22,64,256]{2,1,0:T(8,128)(2,1)S(1)}, f32[22,24,256]{2,1,0:T(8,128)S(1)}, f32[22,24,256]{2,1,0:T(8,128)S(1)}, f32[22,24,256]{2,1,0:T(8,128)S(1...) custom-call(f32[21,21]{1,0:T(8,128)S(1)} %copy-done.2, ...), custom_call_target="tpu_custom_call" | custom-call | tf_op jit(solution)/shard_map/iterate/pallas_call | solution.py:632
  40.8 3.9 %all-to-all-start = ((f32[32,8,128]{2,1,0:T(8,128)}), f32[32,8,128]{2,1,0:T(8,128)S(1)}, u32[]{:S(2)}, u32[]{:S(2)}) async-start(f32[32,8,128]{2,1,0:T(8,128)} %get-tuple-element.38), calls=%async_computation | async-start | bytes 262144 | tf_op jit(solution)/shard_map/all_to_all | solution.py:845
  44.7 8.7 %finish.1 = (f32[336,128]{1,0:T(8,128)}, f32[1024,128]{1,0:T(8,128)}) custom-call(bf16[22,64,256]{2,1,0:T(8,128)(2,1)S(1)} %get-tuple-element.30.feat, f32[22,24,256]{2,1,0:T(8,128)S(1)} %get-tuple-element.31.kern, f32[22,24,256]{2,1,0:T(8,128)S(1)} %get-tuple-element.32.prob0, f32[22,24,256]{2,1,0:T(8,128)S(1)} %get-tuple-element.33.prob1, ...), custom_call_target="tpu_custom_call" | custom-call | flops 200000000 | bytes 8000000 | tf_op jit(solution)/shard_map/finish/pallas_call | solution.py:788
  53.4 0.0 all-to-all-done
  53.5 0.1 fusion
  53.6 0.6 %pad_maximum_fusion = f32[21,21]{1,0:T(8,128)} fusion(f32[8,24]{1,0:T(8,128)S(1)} %get-tuple-element.40, f32[8,24]{1,0:T(8,128)S(1)} %get-tuple-element.41, f32[8,24]{1,0:T(8,128)S(1)} %get-tuple-element.39), kind=kLoop, calls=%fused_computation | loop fusion | flops 882 | bytes 4068 | tf_op jit(solution)/shard_map/concatenate | solution.py:848
  (2 shorter events, 0.0 us)
Async XLA Ops:
  3.7 13.7 %collective-permute-start.4 = (bf16[12,64,128]{2,1,0:T(8,128)(2,1)}, bf16[12,64,128]{2,1,0:T(8,128)(2,1)S(1)}, u32[]{:S(2)}, u32[]{:S(2)}) collective-permute-start(bf16[12,64,128]{2,1,0:T(8,128)(2,1)} %get-tuple-element.26), channel_id=1, source_target_pairs={{4,8},{8,4},{12,16},{16,12},{20,24},{24,20},{28,0},{0,28},{5,9},{9... | collective-permute-start | bytes 589832 | tf_op jit(solution)/shard_map/ppermute | solution.py:828
  7.0 6.1 %collective-permute-start = (f32[2,112,128]{2,1,0:T(8,128)}, f32[2,112,128]{2,1,0:T(8,128)S(1)}, u32[]{:S(2)}, u32[]{:S(2)}) collective-permute-start(f32[2,112,128]{2,1,0:T(8,128)} %get-tuple-element.22), channel_id=1, source_target_pairs={{0,1},{1,2},{2,3},{4,5},{5,6},{6,7},{8,9},{9,10},{10,11},{12,13},{... | collective-permute-start | bytes 344072 | tf_op jit(solution)/shard_map/ppermute | solution.py:830
  10.5 6.9 %collective-permute-start.1 = (f32[2,112,128]{2,1,0:T(8,128)}, f32[2,112,128]{2,1,0:T(8,128)S(1)}, u32[]{:S(2)}, u32[]{:S(2)}) collective-permute-start(f32[2,112,128]{2,1,0:T(8,128)} %get-tuple-element.23), channel_id=1, source_target_pairs={{1,0},{2,1},{3,2},{5,4},{6,5},{7,6},{9,8},{10,9},{11,10},{13,12},{... | collective-permute-start | bytes 344072 | tf_op jit(solution)/shard_map/ppermute | solution.py:831
  11.8 12.9 %collective-permute-start.3 = (f32[18,24,128]{2,1,0:T(8,128)}, f32[18,24,128]{2,1,0:T(8,128)S(1)}, u32[]{:S(2)}, u32[]{:S(2)}) collective-permute-start(f32[18,24,128]{2,1,0:T(8,128)} %get-tuple-element.25), channel_id=1, source_target_pairs={{0,4},{4,0},{8,12},{12,8},{16,20},{20,16},{24,28},{28,24},{1,5},{5... | collective-permute-start | bytes 663560 | tf_op jit(solution)/shard_map/ppermute | solution.py:827
  11.9 12.9 %collective-permute-start.5 = (f32[18,24,128]{2,1,0:T(8,128)}, f32[18,24,128]{2,1,0:T(8,128)S(1)}, u32[]{:S(2)}, u32[]{:S(2)}) collective-permute-start(f32[18,24,128]{2,1,0:T(8,128)} %get-tuple-element.27), channel_id=1, source_target_pairs={{4,8},{8,4},{12,16},{16,12},{20,24},{24,20},{28,0},{0,28},{5,9},{9... | collective-permute-start | bytes 663560 | tf_op jit(solution)/shard_map/ppermute | solution.py:829
  13.2 6.0 %collective-permute-start.2 = (bf16[12,64,128]{2,1,0:T(8,128)(2,1)}, bf16[12,64,128]{2,1,0:T(8,128)(2,1)S(1)}, u32[]{:S(2)}, u32[]{:S(2)}) collective-permute-start(bf16[12,64,128]{2,1,0:T(8,128)(2,1)} %get-tuple-element.24), channel_id=1, source_target_pairs={{0,4},{4,0},{8,12},{12,8},{16,20},{20,16},{24,28},{28,24},{1,5},{5... | collective-permute-start | bytes 589832 | tf_op jit(solution)/shard_map/ppermute | solution.py:826
  17.8 6.9 %collective-permute-start.6 = (f32[288,128]{1,0:T(8,128)S(1)}, f32[288,128]{1,0:T(8,128)S(1)}, u32[]{:S(2)}, u32[]{:S(2)}) collective-permute-start(f32[288,128]{1,0:T(8,128)S(1)} %get-tuple-element.28), channel_id=1, source_target_pairs={{0,4},{4,0},{8,12},{12,8},{16,20},{20,16},{24,28},{28,24},{1,5},{5... | collective-permute-start | bytes 442376 | tf_op jit(solution)/shard_map/ppermute | solution.py:834
  17.9 6.9 %collective-permute-start.7 = (f32[288,128]{1,0:T(8,128)S(1)}, f32[288,128]{1,0:T(8,128)S(1)}, u32[]{:S(2)}, u32[]{:S(2)}) collective-permute-start(f32[288,128]{1,0:T(8,128)S(1)} %get-tuple-element.29), channel_id=1, source_target_pairs={{4,8},{8,4},{12,16},{16,12},{20,24},{24,20},{28,0},{0,28},{5,9},{9... | collective-permute-start | bytes 442376 | tf_op jit(solution)/shard_map/ppermute | solution.py:833
  19.2 1.2 %copy-start = (f32[16,112,128]{2,1,0:T(8,128)S(1)}, f32[16,112,128]{2,1,0:T(8,128)}, u32[]{:S(2)}) copy-start(f32[16,112,128]{2,1,0:T(8,128)} %get-tuple-element.21.centre) | copy-start | bytes 2752516
  20.3 4.5 %copy-start.1 = (f32[16,112,128]{2,1,0:T(8,128)S(1)}, f32[16,112,128]{2,1,0:T(8,128)}, u32[]{:S(2)}) copy-start(f32[16,112,128]{2,1,0:T(8,128)} %get-tuple-element.21.centre) | copy-start | bytes 2752516
  20.3 4.5 %copy-start.2 = (f32[21,21]{1,0:T(8,128)S(1)}, f32[21,21]{1,0:T(8,128)}, u32[]{:S(2)}) copy-start(f32[21,21]{1,0:T(8,128)} %square_in.1) | copy-start | bytes 5296
  40.8 12.7 %all-to-all-start = ((f32[32,8,128]{2,1,0:T(8,128)}), f32[32,8,128]{2,1,0:T(8,128)S(1)}, u32[]{:S(2)}, u32[]{:S(2)}) async-start(f32[32,8,128]{2,1,0:T(8,128)} %get-tuple-element.38), calls=%async_computation | async-start | bytes 262144 | tf_op jit(solution)/shard_map/all_to_all | solution.py:845
